TPU v7x, 32 devices: a whole 2x2x4 slice. The times are simulated.
32 devices in a mesh: ens: 2 (over y), space: 4 (over z), tm: 4 (over x, core).
Axes of the slice: x: 2, y: 2, z: 4, core: 2. Of those that a mesh axis runs over, the one named last changes fastest.
Arguments:
- right_side: float32 [8, 4, 16, 8, 720], P(('ens', 'tm'), None, None, 'space'), parts along dimension 0, may hold values from -8 to 8
- error_precision: float32 [4, 4, 16, 8, 720], P('tm', None, None, 'space'), may hold values from 0.5 to 4
- obs_count: int32 [4, 4, 16, 8, 720], P('tm', None, None, 'space'), may hold values from 0 to 3
- background_wind: float32 [2, 16, 8, 720], P(None, None, 'space'), may hold values from -0.4 to 0.4
- wave_speed: float32 [16], replicated, may hold values from 0.3 to 1.2
- tracer_coupling: float32 [16], replicated, may hold values from 0.2 to 1
Outputs:
- solution_field: float32 [8, 4, 16, 8, 720], P(('ens', 'tm'), None, None, 'space'), parts along dimension 0
- residual: float32 [8, 4, 16, 8, 720], P(('ens', 'tm'), None, None, 'space'), parts along dimension 0
There are 2 independent parts, one for each index of `ens`. A program takes and returns all parts, laid end to end along the dimension named above; an argument that names none is the same for every part. Nothing has to cross between parts.
All inputs are finite; a program needn't handle non-finite values.
Results may differ from a plain program's by a relative error of at most 0.0001.
Values sent between devices are 32-bit elements; how exact they have to be, the bound alone decides.
No kernel may reach another device: no remote copies, remote signals or barrier semaphores. Data moves between devices by JAX's collectives and lax.ppermute only.
A program may use at most 64 MiB of HBM per device.

v0:
```python
import jax
import jax.numpy as jnp
from jax import lax
from jax.sharding import PartitionSpec as P

STEPS = 2
ITERS = 2


diffusion = 0.1


def extended_2(cells, sides, width):
    for axis, dim in sides:
        count = lax.axis_size(axis)
        ends = count - 1
        head = lax.slice_in_dim(cells, 0, width, axis=dim)
        tail = lax.slice_in_dim(cells, cells.shape[dim] - width, cells.shape[dim], axis=dim)
        cells = jnp.concatenate(
            [
                lax.ppermute(tail, axis, [(i, (i + 1) % count) for i in range(ends)]),
                cells,
                lax.ppermute(head, axis, [((i + 1) % count, i) for i in range(ends)]),
            ],
            axis=dim,
        )
    return cells


def shifted(value, axis, by):
    peers = lax.axis_size(axis)
    pairs = [(i, i + by) for i in range(peers) if 0 <= i + by < peers]
    return lax.ppermute(value, axis, pairs)


def along_x(field):
    return 0.5 * (jnp.roll(field, -1, axis=-1) - jnp.roll(field, 1, axis=-1))


def second_x(field):
    return jnp.roll(field, -1, axis=-1) + jnp.roll(field, 1, axis=-1) - 2.0 * field


def along_y(extended):
    return 0.5 * (extended[..., 2:, :] - extended[..., :-2, :])


def trimmed(field, count):
    if count == 0:
        return field
    return field[..., count : field.shape[-2] - count, :]


def row_valid(lat_rows):
    first_row = lax.axis_index("space") * lat_rows - 4
    row_total = lat_rows * lax.axis_size("space")
    global_rows = first_row + jnp.arange(lat_rows + 8, dtype=jnp.int32)
    inside = jnp.logical_and(global_rows >= 0, global_rows < row_total)
    return inside.astype(jnp.float32)[:, None]


def tangent_core(state, margin, coefs):
    speed_col, couple_col, winds, have, valid = coefs
    height, east, north, tracer = (state[:, 0], state[:, 1], state[:, 2], state[:, 3])
    east_mid = east - speed_col * along_x(height)
    north_mid = (trimmed(north, 1) - speed_col * along_y(height)) * trimmed(valid, 5 - margin)
    height_new = trimmed(height, 2) - speed_col * (
        along_x(trimmed(east_mid, 2)) + along_y(north_mid)
    )
    tracer_one = trimmed(tracer, 1)
    inner = trimmed(tracer, 2)
    tracer_lap = second_x(inner) + tracer_one[..., 2:, :] + tracer_one[..., :-2, :] - 2.0 * inner
    wind_east = trimmed(winds[0], have - margin + 2)
    wind_north = trimmed(winds[1], have - margin + 2)
    tracer_new = (
        inner
        - wind_east * along_x(inner)
        - wind_north * along_y(tracer_one)
        + diffusion * tracer_lap
        + couple_col * height_new
    )
    result = jnp.stack(
        [height_new, trimmed(east_mid, 2), trimmed(north_mid, 1), tracer_new], axis=1
    )
    return result * trimmed(valid, 6 - margin)


def adjoint_core(state, margin, coefs):
    speed_col, couple_col, winds, have, valid = coefs
    height, east, north, tracer = (state[:, 0], state[:, 1], state[:, 2], state[:, 3])
    height_mix = height + couple_col * tracer
    east_mid = east + speed_col * along_x(height_mix)
    north_mid = (trimmed(north, 1) + speed_col * along_y(height_mix)) * trimmed(valid, 5 - margin)
    height_new = trimmed(height_mix, 2) + speed_col * (
        along_x(trimmed(east_mid, 2)) + along_y(north_mid)
    )
    tracer_one = trimmed(tracer, 1)
    inner = trimmed(tracer, 2)
    tracer_lap = second_x(inner) + tracer_one[..., 2:, :] + tracer_one[..., :-2, :] - 2.0 * inner
    wind_east = trimmed(winds[0], have - margin + 2)
    wind_north = trimmed(winds[1], have - margin + 1)
    tracer_new = (
        inner
        + along_x(wind_east * inner)
        + along_y(wind_north * tracer_one)
        + diffusion * tracer_lap
    )
    result = jnp.stack(
        [height_new, trimmed(east_mid, 2), trimmed(north_mid, 1), tracer_new], axis=1
    )
    return result * trimmed(valid, 6 - margin)


def rebuild(state, sent):
    widths = [(0, 0)] * (state.ndim - 3) + [(2, 2), (0, 0)]
    east_wide = jnp.pad(state[:, 1], widths)
    return jnp.stack([sent[:, 0], east_wide, sent[:, 1], sent[:, 2]], axis=1)


def tangent_near(state):
    picked = jnp.stack([state[:, 0], state[:, 2], state[:, 3]], axis=1)
    sent = extended_2(picked, (("space", 3),), 2)
    return rebuild(state, sent)


def adjoint_near(state):
    picked = jnp.stack([state[:, 0], state[:, 2], state[:, 3]], axis=1)
    sent = extended_2(picked, (("space", 3),), 2)
    return rebuild(state, sent)


def propagate(fields, step_core, near_fn, coefs):
    current = fields
    for step in range(STEPS):
        current = step_core(near_fn(current), 2, coefs)
    return current


def operate(direction, error_precision, observed, coefs):
    moved = propagate(direction, tangent_core, tangent_near, coefs)
    incoming = shifted(moved, "tm", 1)
    previous = jnp.concatenate([incoming, moved[:-1]], axis=0)
    weighted = error_precision * (direction - previous)
    back = propagate(weighted, adjoint_core, adjoint_near, coefs)
    arriving = shifted(back, "tm", -1)
    following = jnp.concatenate([back[1:], arriving], axis=0)
    return weighted - following + observed * direction


def squares(residual):
    return lax.psum(jnp.sum(residual * residual), ("space", "tm"))


def on_device(right_side, error_precision, obs_count, background_wind, wave_speed, tracer_coupling):
    lat_rows = right_side.shape[3]
    valid = row_valid(lat_rows)
    winds = extended_2(background_wind, (("space", 2),), 1)
    have = 1
    coefs = (wave_speed[:, None, None], tracer_coupling[:, None, None], winds, have, valid)
    observed = obs_count.astype(jnp.float32)
    solution_field = jnp.zeros_like(right_side)
    residual = right_side
    direction = right_side
    norm_now = squares(residual)
    for step in range(ITERS):
        image = operate(direction, error_precision, observed, coefs)
        alpha = norm_now / lax.psum(jnp.sum(direction * image), ("space", "tm"))
        solution_field = solution_field + alpha * direction
        residual = residual - alpha * image
        norm_next = squares(residual)
        direction = residual + norm_next / norm_now * direction
        norm_now = norm_next
    return (solution_field, residual)


def solution(mesh):
    return jax.shard_map(
        on_device,
        mesh=mesh,
        in_specs=(
            P(("ens", "tm"), None, None, "space", None),
            P("tm", None, None, "space", None),
            P("tm", None, None, "space", None),
            P(None, None, "space", None),
            P(),
            P(),
        ),
        out_specs=(
            P(("ens", "tm"), None, None, "space", None),
            P(("ens", "tm"), None, None, "space", None),
        ),
        check_vma=False,
    )
```

profile of v0, /device:TPU:1, one launch (start us, length us, event | category | flops | bytes accessed | tf_op | source)
XLA Modules:
  0.0 280.2 jit_solution(4300498370695817430)
XLA Ops:
  2.8 1.3 collective-permute-start.1
  4.1 4.7 %collective-permute-start = (f32[1,3,16,2,720]{4,3,2,1,0:T(2,128)S(1)}, f32[1,3,16,2,720]{4,3,2,1,0:T(2,128)S(1)}, u32[]{:S(2)}, u32[]{:S(2)}) collective-permute-start(f32[1,3,16,2,720]{4,3,2,1,0:T(2,128)S(1)} %pad_maximum_fusion.9), channel_id=1, source_target_pairs={{0,4},{4,8},{8,12},{1,5},{5,9},{9,13},{2,6},{6,10},{10,14},{3,7},{... | collective-permute-start | bytes 829448 | tf_op jit(solution)/shard_map/ppermute | solution.py:21
  8.9 3.3 %collective-permute-start.2 = (f32[2,16,1,720]{3,2,1,0:T(1,128)S(1)}, f32[2,16,1,720]{3,2,1,0:T(1,128)S(1)}, u32[]{:S(2)}, u32[]{:S(2)}) collective-permute-start(f32[2,16,1,720]{3,2,1,0:T(1,128)S(1)} %get-tuple-element.168), channel_id=1, source_target_pairs={{0,4},{4,8},{8,12},{1,5},{5,9},{9,13},{2,6},{6,10},{10,14},{3,7},{... | collective-permute-start | bytes 276488 | tf_op jit(solution)/shard_map/ppermute | solution.py:21
  12.3 1.3 collective-permute-start.3
  13.8 2.7 collective-permute-done.2
  21.3 1.3 collective-permute-start.5
  22.6 4.2 %collective-permute-start.4 = (f32[1,3,16,2,720]{4,3,2,1,0:T(2,128)S(1)}, f32[1,3,16,2,720]{4,3,2,1,0:T(2,128)S(1)}, u32[]{:S(2)}, u32[]{:S(2)}) collective-permute-start(f32[1,3,16,2,720]{4,3,2,1,0:T(2,128)S(1)} %pad_maximum_fusion.10), channel_id=1, source_target_pairs={{0,4},{4,8},{8,12},{1,5},{5,9},{9,13},{2,6},{6,10},{10,14},{3,7},{... | collective-permute-start | bytes 829448 | tf_op jit(solution)/shard_map/ppermute | solution.py:21
  26.8 2.6 collective-permute-done.5
  33.7 6.7 %collective-permute-start.6 = (f32[1,4,16,2,720]{4,3,2,1,0:T(2,128)S(1)}, f32[1,4,16,2,720]{4,3,2,1,0:T(2,128)S(1)}, u32[]{:S(2)}, u32[]{:S(2)}) collective-permute-start(f32[1,4,16,2,720]{4,3,2,1,0:T(2,128)S(1)} %maximum_multiply_fusion.1), channel_id=1, source_target_pairs={{0,1},{1,2},{2,3},{4,5},{5,6},{6,7},{8,9},{9,10},{10,11},{12,13},{... | collective-permute-start | bytes 1105928 | tf_op jit(solution)/shard_map/ppermute | solution.py:33
  40.3 4.7 %collective-permute-done.6 = f32[1,4,16,2,720]{4,3,2,1,0:T(2,128)S(1)} collective-permute-done((f32[1,4,16,2,720]{4,3,2,1,0:T(2,128)S(1)}, f32[1,4,16,2,720]{4,3,2,1,0:T(2,128)S(1)}, u32[]{:S(2)}, u32[]{:S(2)}) %collective-permute-start.6) | collective-permute-done | bytes 368672 | tf_op jit(solution)/shard_map/ppermute | solution.py:33
  45.3 1.3 collective-permute-start.8
  46.6 4.8 %collective-permute-start.7 = (f32[1,3,16,2,720]{4,3,2,1,0:T(2,128)S(1)}, f32[1,3,16,2,720]{4,3,2,1,0:T(2,128)S(1)}, u32[]{:S(2)}, u32[]{:S(2)}) collective-permute-start(f32[1,3,16,2,720]{4,3,2,1,0:T(2,128)S(1)} %pad_maximum_fusion.11), channel_id=1, source_target_pairs={{0,4},{4,8},{8,12},{1,5},{5,9},{9,13},{2,6},{6,10},{10,14},{3,7},{... | collective-permute-start | bytes 829448 | tf_op jit(solution)/shard_map/ppermute | solution.py:21
  51.4 2.2 collective-permute-done.8
  53.5 1.5 collective-permute-done.7
  58.5 1.3 collective-permute-start.10
  59.8 4.6 %collective-permute-start.9 = (f32[1,3,16,2,720]{4,3,2,1,0:T(2,128)S(1)}, f32[1,3,16,2,720]{4,3,2,1,0:T(2,128)S(1)}, u32[]{:S(2)}, u32[]{:S(2)}) collective-permute-start(f32[1,3,16,2,720]{4,3,2,1,0:T(2,128)S(1)} %pad_maximum_fusion.12), channel_id=1, source_target_pairs={{0,4},{4,8},{8,12},{1,5},{5,9},{9,13},{2,6},{6,10},{10,14},{3,7},{... | collective-permute-start | bytes 829448 | tf_op jit(solution)/shard_map/ppermute | solution.py:21
  64.4 2.0 collective-permute-done.10
  66.4 1.5 collective-permute-done.9
  71.2 1.9 collective-permute-start.11
  73.1 9.9 %collective-permute-done.11 = f32[1,4,16,2,720]{4,3,2,1,0:T(2,128)S(1)} collective-permute-done((f32[1,4,16,2,720]{4,3,2,1,0:T(2,128)S(1)}, f32[1,4,16,2,720]{4,3,2,1,0:T(2,128)S(1)}, u32[]{:S(2)}, u32[]{:S(2)}) %collective-permute-start.11) | collective-permute-done | bytes 368672 | tf_op jit(solution)/shard_map/ppermute | solution.py:33
  83.0 1.4 multiply_reduce_fusion.2
  84.4 30.2 %all-reduce.8 = (f32[]{:T(128)}, f32[]{:T(128)}) all-reduce(f32[]{:T(128)} %get-tuple-element.3, f32[]{:T(128)} %get-tuple-element.2), channel_id=1, replica_groups=mesh['ens'=2,'space'=4,'tm'=4] {'space','tm'}, use_global_device_ids=true, to_apply=%region_1.0 | all-reduce | flops 2 | bytes 16 | tf_op jit(solution)/shard_map/psum | solution.py:151
  117.0 31.5 %psum.30 = f32[]{:T(128)} all-reduce(f32[]{:T(128)} %get-tuple-element.10), channel_id=1, replica_groups=mesh['ens'=2,'space'=4,'tm'=4] {'space','tm'}, use_global_device_ids=true, to_apply=%region_5.6 | all-reduce | flops 1 | bytes 8 | tf_op jit(solution)/shard_map/psum | solution.py:151
  150.1 1.3 collective-permute-start.13
  151.4 4.0 %collective-permute-start.12 = (f32[1,3,16,2,720]{4,3,2,1,0:T(2,128)S(1)}, f32[1,3,16,2,720]{4,3,2,1,0:T(2,128)S(1)}, u32[]{:S(2)}, u32[]{:S(2)}) collective-permute-start(f32[1,3,16,2,720]{4,3,2,1,0:T(2,128)S(1)} %pad_maximum_fusion.13), channel_id=1, source_target_pairs={{0,4},{4,8},{8,12},{1,5},{5,9},{9,13},{2,6},{6,10},{10,14},{3,7},{... | collective-permute-start | bytes 829448 | tf_op jit(solution)/shard_map/ppermute | solution.py:21
  155.4 4.5 %collective-permute-done.13 = f32[1,3,16,2,720]{4,3,2,1,0:T(2,128)S(1)} collective-permute-done((f32[1,3,16,2,720]{4,3,2,1,0:T(2,128)S(1)}, f32[1,3,16,2,720]{4,3,2,1,0:T(2,128)S(1)}, u32[]{:S(2)}, u32[]{:S(2)}) %collective-permute-start.13) | collective-permute-done | bytes 276512 | tf_op jit(solution)/shard_map/ppermute | solution.py:23
  166.4 1.4 copy.16
  167.8 1.4 copy.18
  169.2 1.4 copy.19
  170.6 1.3 copy.17
  172.9 2.1 add_bitcast_fusion.1
  176.8 4.8 %collective-permute-start.14 = (f32[1,3,16,2,720]{4,3,2,1,0:T(2,128)S(1)}, f32[1,3,16,2,720]{4,3,2,1,0:T(2,128)S(1)}, u32[]{:S(2)}, u32[]{:S(2)}) collective-permute-start(f32[1,3,16,2,720]{4,3,2,1,0:T(2,128)S(1)} %pad_maximum_fusion.14), channel_id=1, source_target_pairs={{0,4},{4,8},{8,12},{1,5},{5,9},{9,13},{2,6},{6,10},{10,14},{3,7},{... | collective-permute-start | bytes 829448 | tf_op jit(solution)/shard_map/ppermute | solution.py:21
  181.6 3.5 %collective-permute-done.15 = f32[1,3,16,2,720]{4,3,2,1,0:T(2,128)S(1)} collective-permute-done((f32[1,3,16,2,720]{4,3,2,1,0:T(2,128)S(1)}, f32[1,3,16,2,720]{4,3,2,1,0:T(2,128)S(1)}, u32[]{:S(2)}, u32[]{:S(2)}) %collective-permute-start.15) | collective-permute-done | bytes 276512 | tf_op jit(solution)/shard_map/ppermute | solution.py:23
  191.6 1.4 copy.20
  193.0 1.4 copy.22
  194.4 1.4 copy.23
  195.8 1.3 copy.21
  198.1 2.1 add_bitcast_fusion
  200.5 1.9 collective-permute-start.16
  202.4 4.7 %collective-permute-done.16 = f32[1,4,16,2,720]{4,3,2,1,0:T(2,128)S(1)} collective-permute-done((f32[1,4,16,2,720]{4,3,2,1,0:T(2,128)S(1)}, f32[1,4,16,2,720]{4,3,2,1,0:T(2,128)S(1)}, u32[]{:S(2)}, u32[]{:S(2)}) %collective-permute-start.16) | collective-permute-done | bytes 368672 | tf_op jit(solution)/shard_map/ppermute | solution.py:33
  208.7 5.0 %collective-permute-start.17 = (f32[1,3,16,2,720]{4,3,2,1,0:T(2,128)S(1)}, f32[1,3,16,2,720]{4,3,2,1,0:T(2,128)S(1)}, u32[]{:S(2)}, u32[]{:S(2)}) collective-permute-start(f32[1,3,16,2,720]{4,3,2,1,0:T(2,128)S(1)} %pad_maximum_fusion.15), channel_id=1, source_target_pairs={{0,4},{4,8},{8,12},{1,5},{5,9},{9,13},{2,6},{6,10},{10,14},{3,7},{... | collective-permute-start | bytes 829448 | tf_op jit(solution)/shard_map/ppermute | solution.py:21
  213.7 4.0 %collective-permute-done.18 = f32[1,3,16,2,720]{4,3,2,1,0:T(2,128)S(1)} collective-permute-done((f32[1,3,16,2,720]{4,3,2,1,0:T(2,128)S(1)}, f32[1,3,16,2,720]{4,3,2,1,0:T(2,128)S(1)}, u32[]{:S(2)}, u32[]{:S(2)}) %collective-permute-start.18) | collective-permute-done | bytes 276512 | tf_op jit(solution)/shard_map/ppermute | solution.py:23
  217.7 1.8 collective-permute-done.17
  224.3 4.5 %collective-permute-start.19 = (f32[1,3,16,2,720]{4,3,2,1,0:T(2,128)S(1)}, f32[1,3,16,2,720]{4,3,2,1,0:T(2,128)S(1)}, u32[]{:S(2)}, u32[]{:S(2)}) collective-permute-start(f32[1,3,16,2,720]{4,3,2,1,0:T(2,128)S(1)} %pad_maximum_fusion.16), channel_id=1, source_target_pairs={{0,4},{4,8},{8,12},{1,5},{5,9},{9,13},{2,6},{6,10},{10,14},{3,7},{... | collective-permute-start | bytes 829448 | tf_op jit(solution)/shard_map/ppermute | solution.py:21
  228.7 5.5 %collective-permute-done.20 = f32[1,3,16,2,720]{4,3,2,1,0:T(2,128)S(1)} collective-permute-done((f32[1,3,16,2,720]{4,3,2,1,0:T(2,128)S(1)}, f32[1,3,16,2,720]{4,3,2,1,0:T(2,128)S(1)}, u32[]{:S(2)}, u32[]{:S(2)}) %collective-permute-start.20) | collective-permute-done | bytes 276512 | tf_op jit(solution)/shard_map/ppermute | solution.py:23
  238.5 2.6 collective-permute-start.21
  241.1 6.5 %collective-permute-done.21 = f32[1,4,16,2,720]{4,3,2,1,0:T(2,128)S(1)} collective-permute-done((f32[1,4,16,2,720]{4,3,2,1,0:T(2,128)S(1)}, f32[1,4,16,2,720]{4,3,2,1,0:T(2,128)S(1)}, u32[]{:S(2)}, u32[]{:S(2)}) %collective-permute-start.21) | collective-permute-done | bytes 368672 | tf_op jit(solution)/shard_map/ppermute | solution.py:33
  248.6 29.2 %psum.31 = f32[]{:T(128)} all-reduce(f32[]{:T(128)} %multiply_reduce_fusion), channel_id=1, replica_groups=mesh['ens'=2,'space'=4,'tm'=4] {'space','tm'}, use_global_device_ids=true, to_apply=%region_7.8 | all-reduce | flops 1 | bytes 8 | tf_op jit(solution)/shard_map/psum | solution.py:167
  (198 shorter events, 48.9 us)
Async XLA Ops:
  0.6 8.1 %copy-start.3 = (f32[2,16,2,720]{3,2,1,0:T(2,128)S(1)}, f32[2,16,2,720]{3,2,1,0:T(2,128)}, u32[]{:S(2)}) copy-start(f32[2,16,2,720]{3,2,1,0:T(2,128)} %param.9) | copy-start | bytes 552964
  0.6 12.9 %copy-start.7 = (f32[16]{0:T(128)S(1)}, f32[16]{0:T(128)}, u32[]{:S(2)}) copy-start(f32[16]{0:T(128)} %param.10) | copy-start | bytes 196
  2.8 15.2 %collective-permute-start.1 = (f32[1,3,16,2,720]{4,3,2,1,0:T(2,128)S(1)}, f32[1,3,16,2,720]{4,3,2,1,0:T(2,128)S(1)}, u32[]{:S(2)}, u32[]{:S(2)}) collective-permute-start(f32[1,3,16,2,720]{4,3,2,1,0:T(2,128)S(1)} %pad_maximum_fusion.9), channel_id=1, source_target_pairs={{4,0},{8,4},{12,8},{5,1},{9,5},{13,9},{6,2},{10,6},{14,10},{7,3},{... | collective-permute-start | bytes 829448 | tf_op jit(solution)/shard_map/ppermute | solution.py:23
  4.1 13.9 %collective-permute-start = (f32[1,3,16,2,720]{4,3,2,1,0:T(2,128)S(1)}, f32[1,3,16,2,720]{4,3,2,1,0:T(2,128)S(1)}, u32[]{:S(2)}, u32[]{:S(2)}) collective-permute-start(f32[1,3,16,2,720]{4,3,2,1,0:T(2,128)S(1)} %pad_maximum_fusion.9), channel_id=1, source_target_pairs={{0,4},{4,8},{8,12},{1,5},{5,9},{9,13},{2,6},{6,10},{10,14},{3,7},{... | collective-permute-start | bytes 829448 | tf_op jit(solution)/shard_map/ppermute | solution.py:21
  8.9 7.6 %collective-permute-start.2 = (f32[2,16,1,720]{3,2,1,0:T(1,128)S(1)}, f32[2,16,1,720]{3,2,1,0:T(1,128)S(1)}, u32[]{:S(2)}, u32[]{:S(2)}) collective-permute-start(f32[2,16,1,720]{3,2,1,0:T(1,128)S(1)} %get-tuple-element.168), channel_id=1, source_target_pairs={{0,4},{4,8},{8,12},{1,5},{5,9},{9,13},{2,6},{6,10},{10,14},{3,7},{... | collective-permute-start | bytes 276488 | tf_op jit(solution)/shard_map/ppermute | solution.py:21
  12.3 5.4 %collective-permute-start.3 = (f32[2,16,1,720]{3,2,1,0:T(1,128)S(1)}, f32[2,16,1,720]{3,2,1,0:T(1,128)S(1)}, u32[]{:S(2)}, u32[]{:S(2)}) collective-permute-start(f32[2,16,1,720]{3,2,1,0:T(1,128)S(1)} %get-tuple-element.169), channel_id=1, source_target_pairs={{4,0},{8,4},{12,8},{5,1},{9,5},{13,9},{6,2},{10,6},{14,10},{7,3},{... | collective-permute-start | bytes 276488 | tf_op jit(solution)/shard_map/ppermute | solution.py:23
  18.9 1.2 copy-start.6
  21.3 8.0 %collective-permute-start.5 = (f32[1,3,16,2,720]{4,3,2,1,0:T(2,128)S(1)}, f32[1,3,16,2,720]{4,3,2,1,0:T(2,128)S(1)}, u32[]{:S(2)}, u32[]{:S(2)}) collective-permute-start(f32[1,3,16,2,720]{4,3,2,1,0:T(2,128)S(1)} %pad_maximum_fusion.10), channel_id=1, source_target_pairs={{4,0},{8,4},{12,8},{5,1},{9,5},{13,9},{6,2},{10,6},{14,10},{7,3},{... | collective-permute-start | bytes 829448 | tf_op jit(solution)/shard_map/ppermute | solution.py:23
  22.6 7.8 %collective-permute-start.4 = (f32[1,3,16,2,720]{4,3,2,1,0:T(2,128)S(1)}, f32[1,3,16,2,720]{4,3,2,1,0:T(2,128)S(1)}, u32[]{:S(2)}, u32[]{:S(2)}) collective-permute-start(f32[1,3,16,2,720]{4,3,2,1,0:T(2,128)S(1)} %pad_maximum_fusion.10), channel_id=1, source_target_pairs={{0,4},{4,8},{8,12},{1,5},{5,9},{9,13},{2,6},{6,10},{10,14},{3,7},{... | collective-permute-start | bytes 829448 | tf_op jit(solution)/shard_map/ppermute | solution.py:21
  32.6 12.4 %copy-start = (f32[1,4,16,2,720]{4,3,2,1,0:T(2,128)S(1)}, f32[1,4,16,2,720]{4,3,2,1,0:T(2,128)}, u32[]{:S(2)}) copy-start(f32[1,4,16,2,720]{4,3,2,1,0:T(2,128)} %param.6) | copy-start | bytes 1105924
  32.6 12.4 %copy-start.2 = (f32[1,4,16,2,720]{4,3,2,1,0:T(2,128)S(1)}, f32[1,4,16,2,720]{4,3,2,1,0:T(2,128)}, u32[]{:S(2)}) copy-start(f32[1,4,16,2,720]{4,3,2,1,0:T(2,128)} %param.7) | copy-start | bytes 1105924
  33.7 11.4 %collective-permute-start.6 = (f32[1,4,16,2,720]{4,3,2,1,0:T(2,128)S(1)}, f32[1,4,16,2,720]{4,3,2,1,0:T(2,128)S(1)}, u32[]{:S(2)}, u32[]{:S(2)}) collective-permute-start(f32[1,4,16,2,720]{4,3,2,1,0:T(2,128)S(1)} %maximum_multiply_fusion.1), channel_id=1, source_target_pairs={{0,1},{1,2},{2,3},{4,5},{5,6},{6,7},{8,9},{9,10},{10,11},{12,13},{... | collective-permute-start | bytes 1105928 | tf_op jit(solution)/shard_map/ppermute | solution.py:33
  45.3 8.2 %collective-permute-start.8 = (f32[1,3,16,2,720]{4,3,2,1,0:T(2,128)S(1)}, f32[1,3,16,2,720]{4,3,2,1,0:T(2,128)S(1)}, u32[]{:S(2)}, u32[]{:S(2)}) collective-permute-start(f32[1,3,16,2,720]{4,3,2,1,0:T(2,128)S(1)} %pad_maximum_fusion.11), channel_id=1, source_target_pairs={{4,0},{8,4},{12,8},{5,1},{9,5},{13,9},{6,2},{10,6},{14,10},{7,3},{... | collective-permute-start | bytes 829448 | tf_op jit(solution)/shard_map/ppermute | solution.py:23
  46.6 8.4 %collective-permute-start.7 = (f32[1,3,16,2,720]{4,3,2,1,0:T(2,128)S(1)}, f32[1,3,16,2,720]{4,3,2,1,0:T(2,128)S(1)}, u32[]{:S(2)}, u32[]{:S(2)}) collective-permute-start(f32[1,3,16,2,720]{4,3,2,1,0:T(2,128)S(1)} %pad_maximum_fusion.11), channel_id=1, source_target_pairs={{0,4},{4,8},{8,12},{1,5},{5,9},{9,13},{2,6},{6,10},{10,14},{3,7},{... | collective-permute-start | bytes 829448 | tf_op jit(solution)/shard_map/ppermute | solution.py:21
  58.5 7.9 %collective-permute-start.10 = (f32[1,3,16,2,720]{4,3,2,1,0:T(2,128)S(1)}, f32[1,3,16,2,720]{4,3,2,1,0:T(2,128)S(1)}, u32[]{:S(2)}, u32[]{:S(2)}) collective-permute-start(f32[1,3,16,2,720]{4,3,2,1,0:T(2,128)S(1)} %pad_maximum_fusion.12), channel_id=1, source_target_pairs={{4,0},{8,4},{12,8},{5,1},{9,5},{13,9},{6,2},{10,6},{14,10},{7,3},{... | collective-permute-start | bytes 829448 | tf_op jit(solution)/shard_map/ppermute | solution.py:23
  59.8 8.1 %collective-permute-start.9 = (f32[1,3,16,2,720]{4,3,2,1,0:T(2,128)S(1)}, f32[1,3,16,2,720]{4,3,2,1,0:T(2,128)S(1)}, u32[]{:S(2)}, u32[]{:S(2)}) collective-permute-start(f32[1,3,16,2,720]{4,3,2,1,0:T(2,128)S(1)} %pad_maximum_fusion.12), channel_id=1, source_target_pairs={{0,4},{4,8},{8,12},{1,5},{5,9},{9,13},{2,6},{6,10},{10,14},{3,7},{... | collective-permute-start | bytes 829448 | tf_op jit(solution)/shard_map/ppermute | solution.py:21
  70.1 12.9 %copy-start.1 = (s32[1,4,16,2,720]{4,3,2,1,0:T(2,128)S(1)}, s32[1,4,16,2,720]{4,3,2,1,0:T(2,128)}, u32[]{:S(2)}) copy-start(s32[1,4,16,2,720]{4,3,2,1,0:T(2,128)} %param.8) | copy-start | bytes 1105924
  71.2 11.8 %collective-permute-start.11 = (f32[1,4,16,2,720]{4,3,2,1,0:T(2,128)S(1)}, f32[1,4,16,2,720]{4,3,2,1,0:T(2,128)S(1)}, u32[]{:S(2)}, u32[]{:S(2)}) collective-permute-start(f32[1,4,16,2,720]{4,3,2,1,0:T(2,128)S(1)} %maximum_multiply_fusion.3), channel_id=1, source_target_pairs={{1,0},{2,1},{3,2},{5,4},{6,5},{7,6},{9,8},{10,9},{11,10},{13,12},{... | collective-permute-start | bytes 1105928 | tf_op jit(solution)/shard_map/ppermute | solution.py:33
  150.1 9.8 %collective-permute-start.13 = (f32[1,3,16,2,720]{4,3,2,1,0:T(2,128)S(1)}, f32[1,3,16,2,720]{4,3,2,1,0:T(2,128)S(1)}, u32[]{:S(2)}, u32[]{:S(2)}) collective-permute-start(f32[1,3,16,2,720]{4,3,2,1,0:T(2,128)S(1)} %pad_maximum_fusion.13), channel_id=1, source_target_pairs={{4,0},{8,4},{12,8},{5,1},{9,5},{13,9},{6,2},{10,6},{14,10},{7,3},{... | collective-permute-start | bytes 829448 | tf_op jit(solution)/shard_map/ppermute | solution.py:23
  151.4 9.4 %collective-permute-start.12 = (f32[1,3,16,2,720]{4,3,2,1,0:T(2,128)S(1)}, f32[1,3,16,2,720]{4,3,2,1,0:T(2,128)S(1)}, u32[]{:S(2)}, u32[]{:S(2)}) collective-permute-start(f32[1,3,16,2,720]{4,3,2,1,0:T(2,128)S(1)} %pad_maximum_fusion.13), channel_id=1, source_target_pairs={{0,4},{4,8},{8,12},{1,5},{5,9},{9,13},{2,6},{6,10},{10,14},{3,7},{... | collective-permute-start | bytes 829448 | tf_op jit(solution)/shard_map/ppermute | solution.py:21
  171.9 3.2 %copy-start.5 = (f32[1,1,16,2,720]{4,3,2,1,0:T(2,128)S(1)}, f32[1,1,16,2,720]{4,3,2,1,0:T(2,128)}, u32[]{:S(2)}) copy-start(f32[1,1,16,2,720]{4,3,2,1,0:T(2,128)} %slice_bitcast_fusion.36) | copy-start | bytes 276484
  175.5 9.6 %collective-permute-start.15 = (f32[1,3,16,2,720]{4,3,2,1,0:T(2,128)S(1)}, f32[1,3,16,2,720]{4,3,2,1,0:T(2,128)S(1)}, u32[]{:S(2)}, u32[]{:S(2)}) collective-permute-start(f32[1,3,16,2,720]{4,3,2,1,0:T(2,128)S(1)} %pad_maximum_fusion.14), channel_id=1, source_target_pairs={{4,0},{8,4},{12,8},{5,1},{9,5},{13,9},{6,2},{10,6},{14,10},{7,3},{... | collective-permute-start | bytes 829448 | tf_op jit(solution)/shard_map/ppermute | solution.py:23
  176.8 9.2 %collective-permute-start.14 = (f32[1,3,16,2,720]{4,3,2,1,0:T(2,128)S(1)}, f32[1,3,16,2,720]{4,3,2,1,0:T(2,128)S(1)}, u32[]{:S(2)}, u32[]{:S(2)}) collective-permute-start(f32[1,3,16,2,720]{4,3,2,1,0:T(2,128)S(1)} %pad_maximum_fusion.14), channel_id=1, source_target_pairs={{0,4},{4,8},{8,12},{1,5},{5,9},{9,13},{2,6},{6,10},{10,14},{3,7},{... | collective-permute-start | bytes 829448 | tf_op jit(solution)/shard_map/ppermute | solution.py:21
  197.1 3.2 %copy-start.4 = (f32[1,1,16,2,720]{4,3,2,1,0:T(2,128)S(1)}, f32[1,1,16,2,720]{4,3,2,1,0:T(2,128)}, u32[]{:S(2)}) copy-start(f32[1,1,16,2,720]{4,3,2,1,0:T(2,128)} %slice_bitcast_fusion.33) | copy-start | bytes 276484
  200.5 6.6 %collective-permute-start.16 = (f32[1,4,16,2,720]{4,3,2,1,0:T(2,128)S(1)}, f32[1,4,16,2,720]{4,3,2,1,0:T(2,128)S(1)}, u32[]{:S(2)}, u32[]{:S(2)}) collective-permute-start(f32[1,4,16,2,720]{4,3,2,1,0:T(2,128)S(1)} %maximum_multiply_fusion.5), channel_id=1, source_target_pairs={{0,1},{1,2},{2,3},{4,5},{5,6},{6,7},{8,9},{9,10},{10,11},{12,13},{... | collective-permute-start | bytes 1105928 | tf_op jit(solution)/shard_map/ppermute | solution.py:33
  207.4 10.3 %collective-permute-start.18 = (f32[1,3,16,2,720]{4,3,2,1,0:T(2,128)S(1)}, f32[1,3,16,2,720]{4,3,2,1,0:T(2,128)S(1)}, u32[]{:S(2)}, u32[]{:S(2)}) collective-permute-start(f32[1,3,16,2,720]{4,3,2,1,0:T(2,128)S(1)} %pad_maximum_fusion.15), channel_id=1, source_target_pairs={{4,0},{8,4},{12,8},{5,1},{9,5},{13,9},{6,2},{10,6},{14,10},{7,3},{... | collective-permute-start | bytes 829448 | tf_op jit(solution)/shard_map/ppermute | solution.py:23
  208.7 10.8 %collective-permute-start.17 = (f32[1,3,16,2,720]{4,3,2,1,0:T(2,128)S(1)}, f32[1,3,16,2,720]{4,3,2,1,0:T(2,128)S(1)}, u32[]{:S(2)}, u32[]{:S(2)}) collective-permute-start(f32[1,3,16,2,720]{4,3,2,1,0:T(2,128)S(1)} %pad_maximum_fusion.15), channel_id=1, source_target_pairs={{0,4},{4,8},{8,12},{1,5},{5,9},{9,13},{2,6},{6,10},{10,14},{3,7},{... | collective-permute-start | bytes 829448 | tf_op jit(solution)/shard_map/ppermute | solution.py:21
  223.0 11.2 %collective-permute-start.20 = (f32[1,3,16,2,720]{4,3,2,1,0:T(2,128)S(1)}, f32[1,3,16,2,720]{4,3,2,1,0:T(2,128)S(1)}, u32[]{:S(2)}, u32[]{:S(2)}) collective-permute-start(f32[1,3,16,2,720]{4,3,2,1,0:T(2,128)S(1)} %pad_maximum_fusion.16), channel_id=1, source_target_pairs={{4,0},{8,4},{12,8},{5,1},{9,5},{13,9},{6,2},{10,6},{14,10},{7,3},{... | collective-permute-start | bytes 829448 | tf_op jit(solution)/shard_map/ppermute | solution.py:23
  224.3 10.9 %collective-permute-start.19 = (f32[1,3,16,2,720]{4,3,2,1,0:T(2,128)S(1)}, f32[1,3,16,2,720]{4,3,2,1,0:T(2,128)S(1)}, u32[]{:S(2)}, u32[]{:S(2)}) collective-permute-start(f32[1,3,16,2,720]{4,3,2,1,0:T(2,128)S(1)} %pad_maximum_fusion.16), channel_id=1, source_target_pairs={{0,4},{4,8},{8,12},{1,5},{5,9},{9,13},{2,6},{6,10},{10,14},{3,7},{... | collective-permute-start | bytes 829448 | tf_op jit(solution)/shard_map/ppermute | solution.py:21
  238.5 9.1 %collective-permute-start.21 = (f32[1,4,16,2,720]{4,3,2,1,0:T(2,128)S(1)}, f32[1,4,16,2,720]{4,3,2,1,0:T(2,128)S(1)}, u32[]{:S(2)}, u32[]{:S(2)}) collective-permute-start(f32[1,4,16,2,720]{4,3,2,1,0:T(2,128)S(1)} %maximum_multiply_fusion.7), channel_id=1, source_target_pairs={{1,0},{2,1},{3,2},{5,4},{6,5},{7,6},{9,8},{10,9},{11,10},{13,12},{... | collective-permute-start | bytes 1105928 | tf_op jit(solution)/shard_map/ppermute | solution.py:33
where the time goes:
time: 283 us; the launch traced here: 280 us
  blocking collectives  90.9 us (32%)
  starting transfers between devices  64.5 us (23%)
  waiting for transfers between devices  62.4 us (22%)
  local copies, waits for them, and re-layouts  31.1 us (11%)
  other arithmetic  25.6 us (9%)
  between operations  5.65 us (2%)
    psum x2, blocking collectives, squares(): return lax.psum(jnp.sum(residual * residual), ('space', 'tm'))  61.7 us
    ppermute x9, starting transfers between devices, extended_2(): lax.ppermute(tail, axis, [(i, (i + 1) % count) for i in range(ends)])  39.8 us
    psum x1, blocking collectives, on_device(): alpha = norm_now / lax.psum(jnp.sum(direction * image), ('space', 'tm'))  29.2 us
    ppermute x4, waiting for transfers between devices, shifted(): return lax.ppermute(value, axis, pairs)  25.8 us
    ppermute x9, waiting for transfers between devices, extended_2(): lax.ppermute(head, axis, [((i + 1) % count, i) for i in range(ends)])  25.4 us
    slice x50, local copies, waits for them, and re-layouts, along_x(): return 0.5 * (jnp.roll(field, -1, axis=-1) - jnp.roll(field, 1, axis=-1))  14.8 us
    ppermute x4, starting transfers between devices, shifted(): return lax.ppermute(value, axis, pairs)  13.1 us
    ppermute x9, starting transfers between devices, extended_2(): lax.ppermute(head, axis, [((i + 1) % count, i) for i in range(ends)])  11.6 us
  transfers between devices with their start and end apart: 22, of which 20 were waited for; matrix products, arithmetic and copies ran while one was open for 0% of the time, Pallas kernels for 0%

commit v1 on v0

--- a/solution.py
+++ b/solution.py
@@ -1,6 +1,8 @@
 import jax
 import jax.numpy as jnp
 from jax import lax
+from jax.experimental import pallas as pl
+from jax.experimental.pallas import tpu as pltpu
 from jax.sharding import PartitionSpec as P
 
 STEPS = 2
@@ -8,6 +10,349 @@
 
 
 diffusion = 0.1
+
+
+LANES = 128
+ROWS = 8
+HALO = 24
+
+
+def tiles_of(lon):
+    return -(-lon // LANES)
+
+
+def pack_kernel(lon, b_ref, e_ref, o_ref, w_ref, out_ref):
+    fields, levels, share, _ = b_ref.shape
+    full = lon // LANES
+    rest = lon - full * LANES
+    over = LANES - rest
+    half = out_ref.shape[0] // levels // share
+    group = 3 * full + 2
+    spare = fields * group
+    mine = lax.axis_index("tm")
+    lower = lax.rem(mine, 2) == 0
+    for level in range(levels):
+        base = level * half * share
+
+        def put(row, value, lo, hi):
+            out_ref[pl.ds(base + row, share, stride=half), lo:hi] = value
+
+        for f in range(fields):
+            parts = [b_ref[f, level], e_ref[f, level], o_ref[f, level].astype(jnp.float32)]
+            for a, part in enumerate(parts):
+                for c in range(full):
+                    put(f * group + a * full + c, part[:, c * LANES : (c + 1) * LANES], 0, LANES)
+            tails = [part[:, full * LANES :] for part in parts]
+            put(f * group + 3 * full, jnp.concatenate([tails[0], tails[2][:, :over]], axis=1), 0, LANES)
+            put(f * group + 3 * full + 1, jnp.concatenate([tails[1], tails[2][:, over:]], axis=1), 0, 2 * rest - over)
+        wind = w_ref[mine // 2, level]
+        wind = jnp.where(lower, wind[0:1], wind[1:2])
+        for c in range(full + 1):
+            row = base + (c // 4) * half + spare + c % 4
+            if c < full:
+                out_ref[pl.ds(row, 1), :] = wind[:, c * LANES : (c + 1) * LANES]
+            else:
+                out_ref[pl.ds(row, 1), 0:rest] = wind[:, c * LANES :]
+
+
+def layer_kernel(lon, subwins, in_ref, speed_ref, couple_ref, out_ref, wind_ref):
+    fields = 4
+    full = lon // LANES
+    rest = lon - full * LANES
+    over = LANES - rest
+    tiles = full + 1
+    half = in_ref.shape[0] // (subwins * ROWS)
+    half_out = out_ref.shape[0] // (subwins * ROWS)
+    group = 3 * full + 2
+    spare = fields * group
+    layer = lax.axis_index("tm") * lax.axis_size("space") + lax.axis_index("space")
+    speed = 0.5 * speed_ref[layer]
+    couple = couple_ref[layer]
+    lane = lax.broadcasted_iota(jnp.int32, (ROWS, LANES), 1)
+    row = lax.broadcasted_iota(jnp.int32, (ROWS, LANES), 0)
+
+    def load(t, k):
+        return in_ref[pl.ds(t * ROWS * half + k, ROWS, stride=half), :]
+
+    def back(x, by):
+        return [
+            jnp.where(lane < by, before, here)
+            for before, here in _pairs([pltpu.roll(v, by, 1) for v in x], -1)
+        ]
+
+    def ahead(x, by):
+        return [
+            jnp.where(lane >= LANES - by, after, here)
+            for after, here in _pairs([pltpu.roll(v, LANES - by, 1) for v in x], 1)
+        ]
+
+    def up(x, by):
+        return [pltpu.roll(v, ROWS - by, 0) for v in x]
+
+    def down(x, by):
+        return [pltpu.roll(v, by, 0) for v in x]
+
+    def wrapped(x):
+        first, last = x[0], x[-1]
+        tail = jnp.where(lane < rest + HALO, pltpu.roll(first, rest, 1), pltpu.roll(last, LANES - rest, 1))
+        return x[:-1] + [jnp.where(lane < rest, last, tail)]
+
+    def staggered(f, x):
+        if f == 1:
+            return ahead(x, 1)
+        if f == 2:
+            return up(x, 1)
+        return x
+
+    def aligned(f, x):
+        if f == 1:
+            return back(x, 1)
+        if f == 2:
+            return down(x, 1)
+        return x
+
+    def fetch(t):
+        got = [[], [], []]
+        for f in range(fields):
+            at = f * group
+            one = load(t, at + 3 * full)
+            two = load(t, at + 3 * full + 1)
+            three = jnp.where(lane < over, pltpu.roll(one, over, 1), pltpu.roll(two, 2 * over, 1))
+            for a, tail in enumerate((one, two, three)):
+                x = [load(t, at + a * full + c) for c in range(full)] + [tail]
+                got[a].append(staggered(f, wrapped(x)))
+        return got
+
+    for comp in range(2):
+        for r in range(2):
+            for c in range(tiles):
+                at = (2 * comp + r) * ROWS * half + (c // 4) * half + spare + c % 4
+                wind_ref[comp, c, pl.ds(r, ROWS // 2, stride=2), :] = in_ref[
+                    pl.ds(at, ROWS // 2, stride=2 * half), :
+                ]
+    east = wrapped([wind_ref[0, c] for c in range(tiles)])
+    north = wrapped([wind_ref[1, c] for c in range(tiles)])
+    east_m = [diffusion - 0.5 * v for v in east]
+    east_p = [diffusion + 0.5 * v for v in east]
+    north_m = [jnp.where(row == ROWS - 1, 0.0, diffusion - 0.5 * v) for v in north]
+    north_p = [jnp.where(row == 0, 0.0, diffusion + 0.5 * v) for v in north]
+    stay = 1.0 - 4.0 * diffusion
+    grad_p = jnp.where(row == ROWS - 2, 0.0, speed)
+    grad_m = jnp.where(row == ROWS - 1, 0.0, speed)
+    div_p = jnp.where(row == ROWS - 1, 0.0, speed)
+    div_m = jnp.where(row == 0, 0.0, speed)
+
+    def tangent(state):
+        h, u, v, q = state
+        u = [a - speed * (n - m) for a, n, m in zip(u, ahead(h, 2), h)]
+        v = [a - (grad_p * n - grad_m * m) for a, n, m in zip(v, up(h, 2), h)]
+        h = [
+            a - (speed * (p - m) + (div_p * n - div_m * s))
+            for a, p, m, n, s in zip(h, u, back(u, 2), v, down(v, 2))
+        ]
+        q = [
+            stay * a + (em * e + ep * w) + (nm * n + np * s) + couple * p
+            for a, em, e, ep, w, nm, n, np, s, p in zip(
+                q, east_m, ahead(q, 1), east_p, back(q, 1), north_m, up(q, 1), north_p, down(q, 1), h
+            )
+        ]
+        return [h, u, v, q]
+
+    def adjoint(state):
+        h, u, v, q = state
+        h = [a + couple * b for a, b in zip(h, q)]
+        u = [a + speed * (n - m) for a, n, m in zip(u, ahead(h, 2), h)]
+        v = [a + (grad_p * n - grad_m * m) for a, n, m in zip(v, up(h, 2), h)]
+        h = [
+            a + (speed * (p - m) + (div_p * n - div_m * s))
+            for a, p, m, n, s in zip(h, u, back(u, 2), v, down(v, 2))
+        ]
+        e = ahead([a * b for a, b in zip(east_p, q)], 1)
+        w = back([a * b for a, b in zip(east_m, q)], 1)
+        n = up([a * b for a, b in zip(north_p, q)], 1)
+        s = down([a * b for a, b in zip(north_m, q)], 1)
+        q = [stay * a + (b + c) + (d + f) for a, b, c, d, f in zip(q, e, w, n, s)]
+        return [h, u, v, q]
+
+    def each(fn, *states):
+        return [[fn(*vals) for vals in zip(*xs)] for xs in zip(*states)]
+
+    def operate(p, precision, observed):
+        weighted = []
+        for t in range(subwins):
+            change = p[t]
+            if t > 0:
+                moved = p[t - 1]
+                for _ in range(STEPS):
+                    moved = tangent(moved)
+                change = each(lambda a, b: a - b, change, moved)
+            weighted.append(each(lambda a, b: a * b, precision[t], change))
+        image = []
+        for t in range(subwins):
+            out = each(lambda w, o, d: w + o * d, weighted[t], observed[t], p[t])
+            if t + 1 < subwins:
+                moved = weighted[t + 1]
+                for _ in range(STEPS):
+                    moved = adjoint(moved)
+                out = each(lambda a, b: a - b, out, moved)
+            image.append(out)
+        return image
+
+    got = [fetch(t) for t in range(subwins)]
+    b = [g[0] for g in got]
+    precision = [g[1] for g in got]
+    observed = [g[2] for g in got]
+    one = operate(b, precision, observed)
+    two = operate(one, precision, observed)
+
+    def flat(x):
+        return [(c, v) for state in x for field in state for c, v in enumerate(field)]
+
+    fb, f1, f2 = flat(b), flat(one), flat(two)
+
+    def total(terms):
+        inner, edge = None, None
+        for c, v in terms:
+            if c < full:
+                inner = v if inner is None else inner + v
+            else:
+                edge = v if edge is None else edge + v
+        both = inner + jnp.where(lane < rest, edge, 0.0)
+        return jnp.sum(both, axis=(0, 1), keepdims=True)
+
+    def dot(x, y):
+        return total([(c, v * w) for (c, v), (_, w) in zip(x, y)])
+
+    bb, b1, s11, s12 = dot(fb, fb), dot(fb, f1), dot(f1, f1), dot(f1, f2)
+    step = jnp.where(b1 > 0.0, bb / jnp.where(b1 > 0.0, b1, 1.0), 0.0)
+    grow = jnp.where(bb > 0.0, step * step * s11 / jnp.where(bb > 0.0, bb, 1.0) - 1.0, 0.0)
+    step_t = jnp.broadcast_to(step, (ROWS, LANES))
+    grow_t = jnp.broadcast_to(grow, (ROWS, LANES))
+    res = [(c, v - step_t * w) for (c, v), (_, w) in zip(fb, f1)]
+    mov = [(c, v + grow_t * w) for (c, v), (_, w) in zip(res, fb)]
+    img = [(c, (v - step_t * w) + grow_t * v) for (c, v), (_, w) in zip(f1, f2)]
+    sums = [step, grow, bb, b1, s11, s12, dot(res, res), dot(res, f1), dot(mov, img), dot(mov, f2), dot(mov, f1)]
+    for t in range(subwins):
+        for a, x in enumerate((one, two)):
+            for f in range(fields):
+                y = aligned(f, x[t][f])
+                for c in range(tiles):
+                    at = (a * fields + f) * tiles + c
+                    v = y[c]
+                    if c == full:
+                        i = a * fields + f
+                        even = sums[i]
+                        odd = sums[i + 8] if i + 8 < len(sums) else jnp.zeros_like(even)
+                        v = jnp.where(lane < rest, v, jnp.where(row % 2 == 0, even, odd))
+                    out_ref[pl.ds(t * ROWS * half_out + at, ROWS, stride=half_out), :] = v
+
+
+def _pairs(x, by):
+    n = len(x)
+    return [(x[(i + by) % n], x[i]) for i in range(n)]
+
+
+def finish_kernel(lon, b_ref, in_ref, x_ref, r_ref):
+    fields, levels, share, _ = b_ref.shape
+    full = lon // LANES
+    rest = lon - full * LANES
+    tiles = full + 1
+    half = in_ref.shape[0] // (levels * share)
+
+    def sums(i):
+        at = (i // 8) * half + (i % 8) * tiles + full
+        return in_ref[pl.ds(at, levels, stride=half * share), :]
+
+    step, grow, bb, b1, s11, s12, rr, r1, mi, m2, m1 = [sums(i) for i in range(11)]
+
+    def total(x):
+        return jnp.sum(x, axis=0, keepdims=True)
+
+    norm_0 = total(bb)
+    alpha_0 = norm_0 / total(b1)
+    d = step - alpha_0
+    norm_1 = total(rr + d * (2.0 * r1 + d * s11))
+    beta = norm_1 / norm_0
+    g = beta - grow
+    curve = total(mi + 2.0 * (d * m2 + g * m1) + d * (d * s12 + 2.0 * g * s11) + g * g * b1)
+    alpha_1 = norm_1 / curve
+    first = alpha_0 + alpha_1 * (1.0 + beta)
+    second = alpha_0 * alpha_1
+    first = jnp.broadcast_to(first[:, rest : rest + 1], (share, LANES))
+    second = jnp.broadcast_to(second[:, rest : rest + 1], (share, LANES))
+    for level in range(levels):
+        base = level * half * share
+        for f in range(fields):
+            b = b_ref[f, level]
+            for c in range(tiles):
+                width = LANES if c < full else rest
+                cols = pl.ds(c * LANES, width)
+                one = in_ref[pl.ds(base + f * tiles + c, share, stride=half), :][:, :width]
+                two = in_ref[pl.ds(base + (fields + f) * tiles + c, share, stride=half), :][:, :width]
+                part = b[:, c * LANES : c * LANES + width]
+                x_ref[f, level, :, cols] = first[:, :width] * part - second[:, :width] * one
+                r_ref[f, level, :, cols] = (part - first[:, :width] * one) + second[:, :width] * two
+
+
+def by_layer(right_side, error_precision, obs_count, background_wind, wave_speed, tracer_coupling):
+    _, fields, levels, share, lon = right_side.shape
+    subwins = lax.axis_size("tm")
+    full = lon // LANES
+    half = fields * (3 * full + 2) + 4
+    half_out = 2 * fields * (full + 1)
+    vmem = pl.BlockSpec(memory_space=pltpu.VMEM)
+    smem = pl.BlockSpec(memory_space=pltpu.SMEM)
+    params = pltpu.CompilerParams(vmem_limit_bytes=48 * 1024 * 1024)
+    state = (fields, levels, share, lon)
+
+    def exchange(x):
+        x = x.reshape(levels, -1, LANES)
+        return lax.all_to_all(x, ("tm", "space"), 0, 0, tiled=True).reshape(-1, LANES)
+
+    b = right_side.reshape(state)
+    with jax.named_scope("pack"):
+        packed = pl.pallas_call(
+            lambda *refs: pack_kernel(lon, *refs),
+            out_shape=jax.ShapeDtypeStruct((levels * share * half, LANES), jnp.float32),
+            in_specs=[vmem] * 4,
+            out_specs=vmem,
+            compiler_params=params,
+        )(b, error_precision.reshape(state), obs_count.reshape(state), background_wind)
+    packed = exchange(packed)
+    with jax.named_scope("layer"):
+        images = pl.pallas_call(
+            lambda *refs: layer_kernel(lon, subwins, *refs),
+            out_shape=jax.ShapeDtypeStruct((levels * share * half_out, LANES), jnp.float32),
+            in_specs=[vmem, smem, smem],
+            out_specs=vmem,
+            scratch_shapes=[pltpu.VMEM((2, full + 1, ROWS, LANES), jnp.float32)],
+            compiler_params=params,
+        )(packed, wave_speed, tracer_coupling)
+    images = exchange(images)
+    with jax.named_scope("finish"):
+        x, r = pl.pallas_call(
+            lambda *refs: finish_kernel(lon, *refs),
+            out_shape=[jax.ShapeDtypeStruct(state, jnp.float32)] * 2,
+            in_specs=[vmem] * 2,
+            out_specs=[vmem] * 2,
+            compiler_params=params,
+        )(b, images)
+    return x.reshape(right_side.shape), r.reshape(right_side.shape)
+
+
+def fits_by_layer(mesh, shape):
+    space, tm = mesh.shape["space"], mesh.shape["tm"]
+    subwins, fields, levels, lats, lon = shape
+    rest = lon % LANES
+    return (
+        subwins == mesh.shape["ens"] * tm
+        and (tm, space, fields, lats) == (4, 4, 4, ROWS)
+        and levels == space * tm
+        and lon >= 2 * LANES
+        and 2 * (LANES - rest) <= LANES
+        and LANES - rest >= 2 * HALO
+        and lon // LANES <= 7
+    )
 
 
 def extended_2(cells, sides, width):
@@ -174,20 +519,24 @@
 
 
 def solution(mesh):
-    return jax.shard_map(
-        on_device,
-        mesh=mesh,
-        in_specs=(
-            P(("ens", "tm"), None, None, "space", None),
-            P("tm", None, None, "space", None),
-            P("tm", None, None, "space", None),
-            P(None, None, "space", None),
-            P(),
-            P(),
-        ),
-        out_specs=(
-            P(("ens", "tm"), None, None, "space", None),
-            P(("ens", "tm"), None, None, "space", None),
-        ),
-        check_vma=False,
-    )
+    def run(right_side, *others):
+        body = by_layer if fits_by_layer(mesh, right_side.shape) else on_device
+        return jax.shard_map(
+            body,
+            mesh=mesh,
+            in_specs=(
+                P(("ens", "tm"), None, None, "space", None),
+                P("tm", None, None, "space", None),
+                P("tm", None, None, "space", None),
+                P(None, None, "space", None),
+                P(),
+                P(),
+            ),
+            out_specs=(
+                P(("ens", "tm"), None, None, "space", None),
+                P(("ens", "tm"), None, None, "space", None),
+            ),
+            check_vma=False,
+        )(right_side, *others)
+
+    return run

time: 283 us -> 71.3 us (0.25)
  starting transfers between devices: 64.5 us -> 0 us
  waiting for transfers between devices: 62.4 us -> 0 us
  blocking collectives: 90.9 us -> 60.8 us
  local copies, waits for them, and re-layouts: 31.1 us -> 3.93 us
  other arithmetic: 25.6 us -> 0 us
  between operations: 5.65 us -> 0.68 us
  Pallas kernels: 0 us -> 4.78 us
    psum x3 -> x0, blocking collectives: 90.9 us -> none  [the longest x2 61.7 us: squares(): return lax.psum(jnp.sum(residual * residual), ('space', 'tm'))]
    ppermute x22 -> x0, starting transfers between devices: 64.5 us -> none  [the longest x9 39.8 us: extended_2(): lax.ppermute(tail, axis, [(i, (i + 1) % count) for i in range(ends)])]
    ppermute x22 -> x0, waiting for transfers between devices: 62.4 us -> none  [the longest x4 25.8 us: shifted(): return lax.ppermute(value, axis, pairs)]
    all_to_all x0 -> x2, blocking collectives: none -> 60.8 us  [exchange(): lax.all_to_all(x, ('tm', 'space'), 0, 0, tiled=True).reshape(-1, LANES)]
    slice x69 -> x0, local copies, waits for them, and re-layouts: 17.3 us -> none  [the longest x50 14.8 us: along_x(): return 0.5 * (jnp.roll(field, -1, axis=-1) - jnp.roll(field, 1, axis=-1))]
    another operation x20 -> x0, other arithmetic: 9.99 us -> none  [the longest x4 5.81 us: tangent_core(): jnp.stack([height_new, trimmed(east_mid, 2), trimmed(north_mid, 1), trace...]
    concatenate x12 -> x0, local copies, waits for them, and re-layouts: 8.16 us -> none  [along_x(): return 0.5 * (jnp.roll(field, -1, axis=-1) - jnp.roll(field, 1, axis=-1))]
    mul x27 -> x0, other arithmetic: 5.46 us -> none  [the longest x4 2.12 us: tangent_core(): (trimmed(north, 1) - speed_col * along_y(height)) * trimmed(valid, 5 - ma...]
  transfers between devices with their start and end apart: 22 -> 0, of which waited for: 20 -> 0; matrix products, arithmetic and copies ran while one was open for 0% -> 0% of each run, Pallas kernels for 0% -> 0%
where the time goes in v1:
time: 71.3 us; the launch traced here: 70.2 us
  blocking collectives  60.8 us (85%)
  Pallas kernels  4.78 us (7%)
  local copies, waits for them, and re-layouts  3.93 us (6%)
    all_to_all x2, blocking collectives, exchange(): lax.all_to_all(x, ('tm', 'space'), 0, 0, tiled=True).reshape(-1, LANES)  60.8 us
    unnamed x14, local copies, waits for them, and re-layouts  3.93 us
    pallas_call x1, Pallas kernels, by_layer(): pl.pallas_call(lambda *refs: layer_kernel(lon, subwins, *refs), out_shape...  2.91 us

profile of v1, /device:TPU:1, one launch (start us, length us, event | category | flops | bytes accessed | tf_op | source)
XLA Modules:
  0.0 70.2 jit_solution(11557030606547136529)
XLA Ops:
  0.6 0.0 copy-start
  0.6 1.0 %copy-done = f32[1,4,16,2,720]{4,3,2,1,0:T(2,128)S(1)} copy-done((f32[1,4,16,2,720]{4,3,2,1,0:T(2,128)S(1)}, f32[1,4,16,2,720]{4,3,2,1,0:T(2,128)}, u32[]{:S(2)}) %copy-start) | copy-done | bytes 368664
  1.6 0.0 copy-start.2
  1.6 1.0 %copy-done.2 = f32[1,4,16,2,720]{4,3,2,1,0:T(2,128)S(1)} copy-done((f32[1,4,16,2,720]{4,3,2,1,0:T(2,128)S(1)}, f32[1,4,16,2,720]{4,3,2,1,0:T(2,128)}, u32[]{:S(2)}) %copy-start.2) | copy-done | bytes 368664
  2.6 0.0 copy-start.3
  2.6 1.0 %copy-done.3 = s32[1,4,16,2,720]{4,3,2,1,0:T(2,128)S(1)} copy-done((s32[1,4,16,2,720]{4,3,2,1,0:T(2,128)S(1)}, s32[1,4,16,2,720]{4,3,2,1,0:T(2,128)}, u32[]{:S(2)}) %copy-start.3) | copy-done | bytes 368664
  3.6 0.0 copy-start.4
  3.6 0.9 %copy-done.4 = f32[2,16,2,720]{3,2,1,0:T(2,128)S(1)} copy-done((f32[2,16,2,720]{3,2,1,0:T(2,128)S(1)}, f32[2,16,2,720]{3,2,1,0:T(2,128)}, u32[]{:S(2)}) %copy-start.4) | copy-done | bytes 184344
  4.5 0.4 pack.1
  5.0 0.0 copy-start.5
  5.0 0.0 copy-start.6
  5.0 36.5 %all_to_all.10 = f32[16,144,128]{2,1,0:T(8,128)S(1)} all-to-all(f32[16,144,128]{2,1,0:T(8,128)S(1)} %bitcast.9), channel_id=1, replica_groups=mesh['ens'=2,'space'=4,'tm'=4] {'tm','space'}, dimensions={0} | all-to-all | bytes 2359296 | tf_op jit(solution)/shard_map/all_to_all | solution.py:310
  41.5 0.0 copy-done.5
  41.5 0.0 copy-done.6
  41.5 2.9 %layer.1 = f32[1536,128]{1,0:T(8,128)S(1)} custom-call(f32[2304,128]{1,0:T(8,128)S(1)} %bitcast.10, f32[16]{0:T(128)S(1)} %copy-done.5, f32[16]{0:T(128)S(1)} %copy-done.6), custom_call_target="tpu_custom_call" | custom-call | tf_op jit(solution)/shard_map/layer/pallas_call | solution.py:323
  44.4 0.0 copy-start.1
  44.4 24.3 %all_to_all.11 = f32[16,96,128]{2,1,0:T(8,128)S(1)} all-to-all(f32[16,96,128]{2,1,0:T(8,128)S(1)} %bitcast.11), channel_id=1, replica_groups=mesh['ens'=2,'space'=4,'tm'=4] {'tm','space'}, dimensions={0} | all-to-all | bytes 1572864 | tf_op jit(solution)/shard_map/all_to_all | solution.py:310
  68.7 0.0 copy-done.1
  68.7 1.4 %finish.1 = (f32[4,16,2,720]{3,2,1,0:T(2,128)}, f32[4,16,2,720]{3,2,1,0:T(2,128)}) custom-call(f32[4,16,2,720]{3,2,1,0:T(2,128)S(1)} %bitcast.14, f32[1536,128]{1,0:T(8,128)S(1)} %bitcast.12), custom_call_target="tpu_custom_call" | custom-call | tf_op jit(solution)/shard_map/finish/pallas_call | solution.py:333
Async XLA Ops:
  0.6 1.0 %copy-start = (f32[1,4,16,2,720]{4,3,2,1,0:T(2,128)S(1)}, f32[1,4,16,2,720]{4,3,2,1,0:T(2,128)}, u32[]{:S(2)}) copy-start(f32[1,4,16,2,720]{4,3,2,1,0:T(2,128)} %param.6) | copy-start | bytes 1105924
  1.6 1.0 %copy-start.2 = (f32[1,4,16,2,720]{4,3,2,1,0:T(2,128)S(1)}, f32[1,4,16,2,720]{4,3,2,1,0:T(2,128)}, u32[]{:S(2)}) copy-start(f32[1,4,16,2,720]{4,3,2,1,0:T(2,128)} %param.7) | copy-start | bytes 1105924
  2.6 1.0 %copy-start.3 = (s32[1,4,16,2,720]{4,3,2,1,0:T(2,128)S(1)}, s32[1,4,16,2,720]{4,3,2,1,0:T(2,128)}, u32[]{:S(2)}) copy-start(s32[1,4,16,2,720]{4,3,2,1,0:T(2,128)} %param.8) | copy-start | bytes 1105924
  3.6 0.9 %copy-start.4 = (f32[2,16,2,720]{3,2,1,0:T(2,128)S(1)}, f32[2,16,2,720]{3,2,1,0:T(2,128)}, u32[]{:S(2)}) copy-start(f32[2,16,2,720]{3,2,1,0:T(2,128)} %refs_3_.1) | copy-start | bytes 552964
  5.0 36.5 %copy-start.5 = (f32[16]{0:T(128)S(1)}, f32[16]{0:T(128)}, u32[]{:S(2)}) copy-start(f32[16]{0:T(128)} %refs_1_.1) | copy-start | bytes 196
  5.0 36.5 %copy-start.6 = (f32[16]{0:T(128)S(1)}, f32[16]{0:T(128)}, u32[]{:S(2)}) copy-start(f32[16]{0:T(128)} %refs_2_.1) | copy-start | bytes 196
  44.4 24.3 %copy-start.1 = (f32[1,4,16,2,720]{4,3,2,1,0:T(2,128)S(1)}, f32[1,4,16,2,720]{4,3,2,1,0:T(2,128)}, u32[]{:S(2)}) copy-start(f32[1,4,16,2,720]{4,3,2,1,0:T(2,128)} %param.6) | copy-start | bytes 1105924

commit v2 on v1

v2 whole, which is shorter than its diff:
```python
import jax
import jax.numpy as jnp
from jax import lax
from jax.experimental import pallas as pl
from jax.experimental.pallas import tpu as pltpu
from jax.sharding import PartitionSpec as P

STEPS = 2
ITERS = 2


diffusion = 0.1


LANES = 128
ROWS = 8
TILES = 3
REACH = 4
FIELDS = 4
ROWS_IN = FIELDS * TILES * 2 + 2
ROWS_OUT = FIELDS * TILES * 2


def merge_lanes(lon):
    core = lon // 2
    return (core + 3 * REACH) % LANES, (core - 3 * REACH) % LANES


def pack_kernel(lon, merges, b_hbm, e_hbm, o_hbm, w_hbm, out_ref, b_ref, e_ref, o_ref, w_ref, sems):
    _, levels, share, _ = b_ref.shape
    copies = [
        pltpu.make_async_copy(src, dst, sems.at[i])
        for i, (src, dst) in enumerate(((w_hbm, w_ref), (b_hbm, b_ref), (e_hbm, e_ref), (o_hbm, o_ref)))
    ]
    for copy in copies:
        copy.start()
    full = lon // LANES
    rest = lon - full * LANES
    member = lax.axis_index("ens")
    first_member = member == 0
    turn = lax.axis_index("tm") * 2 + member
    lane = lax.broadcasted_iota(jnp.int32, (share, LANES), 1)

    def put(half, level, row, value):
        base = (half * levels + level) * share * ROWS_IN
        out_ref[pl.ds(base + row, share, stride=ROWS_IN), :] = value

    def windows(x):
        tiles = [x[:, c * LANES : (c + 1) * LANES] for c in range(full)]
        tail = jnp.concatenate([x[:, full * LANES :], x[:, : LANES - rest]], axis=1)
        ahead = x[:, lon - LANES :]
        ends = ((tiles[2], ahead), (tail, tiles[2]))
        halves = []
        for half, ((last, before), merge) in enumerate(zip(ends, merges)):
            merged = jnp.where(lane < merge, last, before)
            extra = jnp.where(lane < merge, before, last)
            halves.append((tiles[3 * half], tiles[3 * half + 1], merged, extra))
        return halves

    copies[0].wait()
    for level in range(levels):
        east, north = windows(w_ref[0, level]), windows(w_ref[1, level])
        for half in range(2):
            picks = list(east[half][:3]) + list(north[half][:3]) + [east[half][3], north[half][3]]
            value = picks[0]
            for i in range(1, len(picks)):
                value = jnp.where(turn == i, picks[i], value)
            put(half, level, ROWS_IN - 1, value)
    copies[1].wait()
    for level in range(levels):
        extras = [None, None]
        for f in range(FIELDS):
            for half, got in enumerate(windows(b_ref[f, level])):
                for c in range(TILES):
                    put(half, level, f * TILES + c, got[c])
                moved = got[3] if f == 0 else pltpu.roll(got[3], LANES - 2 * REACH * f, 1)
                edge = merges[half] + REACH - 2 * REACH * f
                extras[half] = moved if f == 0 else jnp.where(lane < edge, moved, extras[half])
        for half in range(2):
            put(half, level, ROWS_IN - 2, extras[half])
    copies[2].wait()
    copies[3].wait()
    for level in range(levels):
        for f in range(FIELDS):
            shared = jnp.where(first_member, e_ref[f, level], o_ref[f, level].astype(jnp.float32))
            for half, got in enumerate(windows(shared)):
                for c in range(TILES):
                    put(half, level, (FIELDS + f) * TILES + c, got[c])


def layer_kernel(lon, merges, subwins, in_ref, speed_ref, couple_ref, out_ref):
    layer = lax.axis_index("tm") * lax.axis_size("space") + lax.axis_index("space")
    half = lax.axis_index("ens")
    speed = 0.5 * speed_ref[layer]
    couple = couple_ref[layer]
    lane = lax.broadcasted_iota(jnp.int32, (ROWS, LANES), 1)
    row = lax.broadcasted_iota(jnp.int32, (ROWS, LANES), 0)
    below = lane < jnp.where(half == 0, merges[0], merges[1])
    free_lo = jnp.where(half == 0, merges[0] - 3 * REACH, merges[1] - 3 * REACH)
    free = jnp.logical_and(lane >= free_lo, lane < free_lo + 6 * REACH)

    def load(member, t, k):
        return in_ref[pl.ds((member * subwins + t) * ROWS * ROWS_IN + k, ROWS, stride=ROWS_IN), :]

    def back(x, by):
        moved = [pltpu.roll(v, by, 1) for v in x]
        return [jnp.where(lane < by, moved[i - 1], v) for i, v in enumerate(moved)]

    def ahead(x, by):
        moved = [pltpu.roll(v, LANES - by, 1) for v in x]
        return [jnp.where(lane >= LANES - by, moved[(i + 1) % len(x)], v) for i, v in enumerate(moved)]

    def up(x, by):
        return [pltpu.roll(v, ROWS - by, 0) for v in x]

    def down(x, by):
        return [pltpu.roll(v, by, 0) for v in x]

    def staggered(f, x):
        if f == 1:
            return ahead(x, 1)
        if f == 2:
            return up(x, 1)
        return x

    def aligned(f, x):
        if f == 1:
            return back(x, 1)
        if f == 2:
            return down(x, 1)
        return x

    def widened(x, extra):
        return x[:2] + [jnp.where(below, x[2], extra), jnp.where(below, extra, x[2])]

    def narrowed(x):
        return x[:2] + [jnp.where(below, x[2], x[3])]

    def fields_of(member, t, at):
        return [[load(member, t, (at + f) * TILES + c) for c in range(TILES)] for f in range(FIELDS)]

    def extras_of(member, t):
        packed = load(member, t, ROWS_IN - 2)
        return [packed] + [pltpu.roll(packed, 2 * REACH * f, 1) for f in range(1, FIELDS)]

    def stag(state):
        return [staggered(f, x) for f, x in enumerate(state)]

    def wind(turn):
        return load(turn % 2, turn // 2, ROWS_IN - 1)

    stay = 1.0 - 4.0 * diffusion
    grad_p = jnp.where(row == ROWS - 2, 0.0, speed)
    grad_m = jnp.where(row == ROWS - 1, 0.0, speed)
    div_p = jnp.where(row == ROWS - 1, 0.0, speed)
    div_m = jnp.where(row == 0, 0.0, speed)

    def coefficients(east, north):
        return (
            [diffusion - 0.5 * v for v in east],
            [diffusion + 0.5 * v for v in east],
            [jnp.where(row == ROWS - 1, 0.0, diffusion - 0.5 * v) for v in north],
            [jnp.where(row == 0, 0.0, diffusion + 0.5 * v) for v in north],
        )

    east, north = [wind(i) for i in range(3)], [wind(3 + i) for i in range(3)]
    narrow = coefficients(east, north)
    wide = coefficients(widened(east, wind(6)), widened(north, wind(7)))

    def tangent(state, coefs):
        h, u, v, q = state
        u = [a - speed * (n - m) for a, n, m in zip(u, ahead(h, 2), h)]
        v = [a - (grad_p * n - grad_m * m) for a, n, m in zip(v, up(h, 2), h)]
        h = [
            a - (speed * (p - m) + (div_p * n - div_m * s))
            for a, p, m, n, s in zip(h, u, back(u, 2), v, down(v, 2))
        ]
        q = [
            stay * a + (em * e + ep * w) + (nm * n + np * s) + couple * p
            for a, em, e, ep, w, nm, n, np, s, p in zip(
                q, coefs[0], ahead(q, 1), coefs[1], back(q, 1), coefs[2], up(q, 1), coefs[3], down(q, 1), h
            )
        ]
        return [h, u, v, q]

    def adjoint(state, coefs):
        h, u, v, q = state
        h = [a + couple * b for a, b in zip(h, q)]
        u = [a + speed * (n - m) for a, n, m in zip(u, ahead(h, 2), h)]
        v = [a + (grad_p * n - grad_m * m) for a, n, m in zip(v, up(h, 2), h)]
        h = [
            a + (speed * (p - m) + (div_p * n - div_m * s))
            for a, p, m, n, s in zip(h, u, back(u, 2), v, down(v, 2))
        ]
        e = ahead([a * b for a, b in zip(coefs[1], q)], 1)
        w = back([a * b for a, b in zip(coefs[0], q)], 1)
        n = up([a * b for a, b in zip(coefs[3], q)], 1)
        s = down([a * b for a, b in zip(coefs[2], q)], 1)
        q = [stay * a + (b + c) + (d + f) for a, b, c, d, f in zip(q, e, w, n, s)]
        return [h, u, v, q]

    def each(fn, *states):
        return [[fn(*vals) for vals in zip(*xs)] for xs in zip(*states)]

    def operate(p, p_wide, precision, observed):
        weighted = []
        for t in range(subwins):
            change = p[t]
            if t > 0:
                moved, coefs = (p[t - 1], narrow) if p_wide is None else (p_wide[t - 1], wide)
                for _ in range(STEPS):
                    moved = tangent(moved, coefs)
                if p_wide is not None:
                    moved = [narrowed(x) for x in moved]
                change = each(lambda a, b: a - b, change, moved)
            weighted.append(each(lambda a, b: a * b, precision[t], change))
        image = []
        for t in range(subwins):
            out = each(lambda w, o, d: w + o * d, weighted[t], observed[t], p[t])
            if t + 1 < subwins:
                moved = weighted[t + 1]
                for _ in range(STEPS):
                    moved = adjoint(moved, narrow)
                out = each(lambda a, b: a - b, out, moved)
            image.append(out)
        return image

    def flat(x):
        return [(c, v) for state in x for field in state for c, v in enumerate(field)]

    def total(terms):
        inner, edge = None, None
        for c, v in terms:
            if c < TILES - 1:
                inner = v if inner is None else inner + v
            else:
                edge = v if edge is None else edge + v
        both = inner + jnp.where(free, 0.0, edge)
        return jnp.sum(both, axis=(0, 1), keepdims=True)

    def dot(x, y):
        return total([(c, v * w) for (c, v), (_, w) in zip(x, y)])

    precision = [stag(fields_of(0, t, FIELDS)) for t in range(subwins)]
    observed = [stag(fields_of(1, t, FIELDS)) for t in range(subwins)]
    for member in range(2):
        plain = [fields_of(member, t, 0) for t in range(subwins)]
        b = [stag(x) for x in plain]
        b_wide = [
            stag([widened(x, e) for x, e in zip(plain[t], extras_of(member, t))]) for t in range(subwins - 1)
        ]
        one = operate(b, b_wide, precision, observed)
        two = operate(one, None, precision, observed)
        one, two = [[[aligned(f, x) for f, x in enumerate(state)] for state in y] for y in (one, two)]
        f0, f1, f2 = flat(plain), flat(one), flat(two)
        bb, b1, s11, s12 = dot(f0, f0), dot(f0, f1), dot(f1, f1), dot(f1, f2)
        step = jnp.where(b1 > 0.0, bb / jnp.where(b1 > 0.0, b1, 1.0), 0.0)
        grow = jnp.where(bb > 0.0, step * step * s11 / jnp.where(bb > 0.0, bb, 1.0) - 1.0, 0.0)
        step_t = jnp.broadcast_to(step, (ROWS, LANES))
        grow_t = jnp.broadcast_to(grow, (ROWS, LANES))
        res = [(c, v - step_t * w) for (c, v), (_, w) in zip(f0, f1)]
        mov = [(c, v + grow_t * w) for (c, v), (_, w) in zip(res, f0)]
        img = [(c, (v - step_t * w) + grow_t * v) for (c, v), (_, w) in zip(f1, f2)]
        sums = [step, grow, bb, b1, s11, s12, dot(res, res), dot(res, f1), dot(mov, img), dot(mov, f2), dot(mov, f1)]
        for t in range(subwins):
            for a, x in enumerate((one, two)):
                for f in range(FIELDS):
                    for c in range(TILES):
                        v = x[t][f][c]
                        at = (a * FIELDS + f) * TILES + c
                        if c == TILES - 1:
                            i = a * FIELDS + f
                            even = sums[i]
                            odd = sums[i + 8] if i + 8 < len(sums) else jnp.zeros_like(even)
                            v = jnp.where(free, jnp.where(row % 2 == 0, even, odd), v)
                        start = (member * subwins + t) * ROWS * ROWS_OUT + at
                        out_ref[pl.ds(start, ROWS, stride=ROWS_OUT), :] = v


def finish_kernel(lon, merges, b_ref, in_ref, x_ref, r_ref):
    _, levels, share, _ = b_ref.shape
    full = lon // LANES
    rest = lon - full * LANES
    size = share * ROWS_OUT
    apart = merges[0] - merges[1]
    at_lane = merges[0] - 3 * REACH

    def sums(i):
        at = (i // 8) * ROWS_OUT + (i % 8) * TILES + TILES - 1
        halves = [in_ref[pl.ds(half * levels * size + at, levels, stride=size), :] for half in range(2)]
        return jnp.concatenate([halves[0], pltpu.roll(halves[1], apart, 1)], axis=0)

    step, grow, bb, b1, s11, s12, rr, r1, mi, m2, m1 = [sums(i) for i in range(11)]

    def total(x):
        return jnp.sum(x, axis=0, keepdims=True)

    norm_0 = total(bb)
    alpha_0 = norm_0 / total(b1)
    d = step - alpha_0
    norm_1 = total(rr + d * (2.0 * r1 + d * s11))
    beta = norm_1 / norm_0
    g = beta - grow
    curve = total(mi + 2.0 * (d * m2 + g * m1) + d * (d * s12 + 2.0 * g * s11) + g * g * b1)
    alpha_1 = norm_1 / curve
    first = alpha_0 + alpha_1 * (1.0 + beta)
    second = alpha_0 * alpha_1
    first = jnp.broadcast_to(first[:, at_lane : at_lane + 1], (share, LANES))
    second = jnp.broadcast_to(second[:, at_lane : at_lane + 1], (share, LANES))
    lane = lax.broadcasted_iota(jnp.int32, (share, LANES), 1)

    def image(level, k):
        got = [
            [
                in_ref[pl.ds((half * levels + level) * size + k * TILES + c, share, stride=ROWS_OUT), :]
                for c in range(TILES)
            ]
            for half in range(2)
        ]
        middle = jnp.where(lane < at_lane, got[0][2], got[1][2])
        return got[0][:2] + [middle] + got[1]

    for level in range(levels):
        for f in range(FIELDS):
            b = b_ref[f, level]
            ones, twos = image(level, f), image(level, FIELDS + f)
            for c, (one, two) in enumerate(zip(ones, twos)):
                width = LANES if c < full else rest
                cols = pl.ds(c * LANES, width)
                one, two = one[:, :width], two[:, :width]
                part = b[:, c * LANES : c * LANES + width]
                x_ref[f, level, :, cols] = first[:, :width] * part - second[:, :width] * one
                r_ref[f, level, :, cols] = (part - first[:, :width] * one) + second[:, :width] * two


def by_layer(right_side, error_precision, obs_count, background_wind, wave_speed, tracer_coupling):
    _, fields, levels, share, lon = right_side.shape
    subwins = lax.axis_size("tm")
    merges = merge_lanes(lon)
    vmem = pl.BlockSpec(memory_space=pltpu.VMEM)
    smem = pl.BlockSpec(memory_space=pltpu.SMEM)
    hbm = pl.BlockSpec(memory_space=pltpu.HBM)
    params = pltpu.CompilerParams(vmem_limit_bytes=48 * 1024 * 1024)
    state = (fields, levels, share, lon)

    def exchange(x):
        x = x.reshape(2 * levels, -1, 1, LANES)
        return lax.all_to_all(x, ("ens", "tm", "space"), 0, 0, tiled=True).reshape(-1, LANES)

    b = right_side.reshape(state)
    with jax.named_scope("pack"):
        packed = pl.pallas_call(
            lambda *refs: pack_kernel(lon, merges, *refs),
            out_shape=jax.ShapeDtypeStruct((2 * levels * share * ROWS_IN, LANES), jnp.float32),
            in_specs=[hbm] * 4,
            out_specs=vmem,
            scratch_shapes=[
                pltpu.VMEM(state, jnp.float32),
                pltpu.VMEM(state, jnp.float32),
                pltpu.VMEM(state, jnp.int32),
                pltpu.VMEM(background_wind.shape, jnp.float32),
                pltpu.SemaphoreType.DMA((4,)),
            ],
            compiler_params=params,
        )(b, error_precision.reshape(state), obs_count.reshape(state), background_wind)
    packed = exchange(packed)
    with jax.named_scope("layer"):
        images = pl.pallas_call(
            lambda *refs: layer_kernel(lon, merges, subwins, *refs),
            out_shape=jax.ShapeDtypeStruct((2 * levels * share * ROWS_OUT, LANES), jnp.float32),
            in_specs=[vmem, smem, smem],
            out_specs=vmem,
            compiler_params=params,
        )(packed, wave_speed, tracer_coupling)
    images = exchange(images)
    with jax.named_scope("finish"):
        x, r = pl.pallas_call(
            lambda *refs: finish_kernel(lon, merges, *refs),
            out_shape=[jax.ShapeDtypeStruct(state, jnp.float32)] * 2,
            in_specs=[vmem] * 2,
            out_specs=[vmem] * 2,
            compiler_params=params,
        )(b, images)
    return x.reshape(right_side.shape), r.reshape(right_side.shape)


def fits_by_layer(mesh, shape):
    space, tm, ens = mesh.shape["space"], mesh.shape["tm"], mesh.shape["ens"]
    subwins, fields, levels, lats, lon = shape
    return (
        (ens, tm, space, fields, lats) == (2, 4, 4, FIELDS, ROWS)
        and subwins == ens * tm
        and levels == space * tm
        and lon == 720
    )


def extended_2(cells, sides, width):
    for axis, dim in sides:
        count = lax.axis_size(axis)
        ends = count - 1
        head = lax.slice_in_dim(cells, 0, width, axis=dim)
        tail = lax.slice_in_dim(cells, cells.shape[dim] - width, cells.shape[dim], axis=dim)
        cells = jnp.concatenate(
            [
                lax.ppermute(tail, axis, [(i, (i + 1) % count) for i in range(ends)]),
                cells,
                lax.ppermute(head, axis, [((i + 1) % count, i) for i in range(ends)]),
            ],
            axis=dim,
        )
    return cells


def shifted(value, axis, by):
    peers = lax.axis_size(axis)
    pairs = [(i, i + by) for i in range(peers) if 0 <= i + by < peers]
    return lax.ppermute(value, axis, pairs)


def along_x(field):
    return 0.5 * (jnp.roll(field, -1, axis=-1) - jnp.roll(field, 1, axis=-1))


def second_x(field):
    return jnp.roll(field, -1, axis=-1) + jnp.roll(field, 1, axis=-1) - 2.0 * field


def along_y(extended):
    return 0.5 * (extended[..., 2:, :] - extended[..., :-2, :])


def trimmed(field, count):
    if count == 0:
        return field
    return field[..., count : field.shape[-2] - count, :]


def row_valid(lat_rows):
    first_row = lax.axis_index("space") * lat_rows - 4
    row_total = lat_rows * lax.axis_size("space")
    global_rows = first_row + jnp.arange(lat_rows + 8, dtype=jnp.int32)
    inside = jnp.logical_and(global_rows >= 0, global_rows < row_total)
    return inside.astype(jnp.float32)[:, None]


def tangent_core(state, margin, coefs):
    speed_col, couple_col, winds, have, valid = coefs
    height, east, north, tracer = (state[:, 0], state[:, 1], state[:, 2], state[:, 3])
    east_mid = east - speed_col * along_x(height)
    north_mid = (trimmed(north, 1) - speed_col * along_y(height)) * trimmed(valid, 5 - margin)
    height_new = trimmed(height, 2) - speed_col * (
        along_x(trimmed(east_mid, 2)) + along_y(north_mid)
    )
    tracer_one = trimmed(tracer, 1)
    inner = trimmed(tracer, 2)
    tracer_lap = second_x(inner) + tracer_one[..., 2:, :] + tracer_one[..., :-2, :] - 2.0 * inner
    wind_east = trimmed(winds[0], have - margin + 2)
    wind_north = trimmed(winds[1], have - margin + 2)
    tracer_new = (
        inner
        - wind_east * along_x(inner)
        - wind_north * along_y(tracer_one)
        + diffusion * tracer_lap
        + couple_col * height_new
    )
    result = jnp.stack(
        [height_new, trimmed(east_mid, 2), trimmed(north_mid, 1), tracer_new], axis=1
    )
    return result * trimmed(valid, 6 - margin)


def adjoint_core(state, margin, coefs):
    speed_col, couple_col, winds, have, valid = coefs
    height, east, north, tracer = (state[:, 0], state[:, 1], state[:, 2], state[:, 3])
    height_mix = height + couple_col * tracer
    east_mid = east + speed_col * along_x(height_mix)
    north_mid = (trimmed(north, 1) + speed_col * along_y(height_mix)) * trimmed(valid, 5 - margin)
    height_new = trimmed(height_mix, 2) + speed_col * (
        along_x(trimmed(east_mid, 2)) + along_y(north_mid)
    )
    tracer_one = trimmed(tracer, 1)
    inner = trimmed(tracer, 2)
    tracer_lap = second_x(inner) + tracer_one[..., 2:, :] + tracer_one[..., :-2, :] - 2.0 * inner
    wind_east = trimmed(winds[0], have - margin + 2)
    wind_north = trimmed(winds[1], have - margin + 1)
    tracer_new = (
        inner
        + along_x(wind_east * inner)
        + along_y(wind_north * tracer_one)
        + diffusion * tracer_lap
    )
    result = jnp.stack(
        [height_new, trimmed(east_mid, 2), trimmed(north_mid, 1), tracer_new], axis=1
    )
    return result * trimmed(valid, 6 - margin)


def rebuild(state, sent):
    widths = [(0, 0)] * (state.ndim - 3) + [(2, 2), (0, 0)]
    east_wide = jnp.pad(state[:, 1], widths)
    return jnp.stack([sent[:, 0], east_wide, sent[:, 1], sent[:, 2]], axis=1)


def tangent_near(state):
    picked = jnp.stack([state[:, 0], state[:, 2], state[:, 3]], axis=1)
    sent = extended_2(picked, (("space", 3),), 2)
    return rebuild(state, sent)


def adjoint_near(state):
    picked = jnp.stack([state[:, 0], state[:, 2], state[:, 3]], axis=1)
    sent = extended_2(picked, (("space", 3),), 2)
    return rebuild(state, sent)


def propagate(fields, step_core, near_fn, coefs):
    current = fields
    for step in range(STEPS):
        current = step_core(near_fn(current), 2, coefs)
    return current


def operate(direction, error_precision, observed, coefs):
    moved = propagate(direction, tangent_core, tangent_near, coefs)
    incoming = shifted(moved, "tm", 1)
    previous = jnp.concatenate([incoming, moved[:-1]], axis=0)
    weighted = error_precision * (direction - previous)
    back = propagate(weighted, adjoint_core, adjoint_near, coefs)
    arriving = shifted(back, "tm", -1)
    following = jnp.concatenate([back[1:], arriving], axis=0)
    return weighted - following + observed * direction


def squares(residual):
    return lax.psum(jnp.sum(residual * residual), ("space", "tm"))


def on_device(right_side, error_precision, obs_count, background_wind, wave_speed, tracer_coupling):
    lat_rows = right_side.shape[3]
    valid = row_valid(lat_rows)
    winds = extended_2(background_wind, (("space", 2),), 1)
    have = 1
    coefs = (wave_speed[:, None, None], tracer_coupling[:, None, None], winds, have, valid)
    observed = obs_count.astype(jnp.float32)
    solution_field = jnp.zeros_like(right_side)
    residual = right_side
    direction = right_side
    norm_now = squares(residual)
    for step in range(ITERS):
        image = operate(direction, error_precision, observed, coefs)
        alpha = norm_now / lax.psum(jnp.sum(direction * image), ("space", "tm"))
        solution_field = solution_field + alpha * direction
        residual = residual - alpha * image
        norm_next = squares(residual)
        direction = residual + norm_next / norm_now * direction
        norm_now = norm_next
    return (solution_field, residual)


def solution(mesh):
    def run(right_side, *others):
        body = by_layer if fits_by_layer(mesh, right_side.shape) else on_device
        return jax.shard_map(
            body,
            mesh=mesh,
            in_specs=(
                P(("ens", "tm"), None, None, "space", None),
                P("tm", None, None, "space", None),
                P("tm", None, None, "space", None),
                P(None, None, "space", None),
                P(),
                P(),
            ),
            out_specs=(
                P(("ens", "tm"), None, None, "space", None),
                P(("ens", "tm"), None, None, "space", None),
            ),
            check_vma=False,
        )(right_side, *others)

    return run
```

time: 71.3 us -> 66 us (0.926); the launches traced: 70.2 us -> 65.7 us
  blocking collectives: 60.8 us -> 52.9 us
  Pallas kernels: 4.78 us -> 7.54 us
    all_to_all x2, blocking collectives: 60.8 us -> 52.9 us  [exchange(): lax.all_to_all(x, ('ens', 'tm', 'space'), 0, 0, tiled=True)]
    pallas_call x3, Pallas kernels: 4.78 us -> 7.54 us  [the longest x1 3.35 us: by_layer(): pl.pallas_call(lambda *refs: pack_kernel(lon, merges, *refs), out_shape=j...]
where the time goes in v2:
time: 66 us; the launch traced here: 65.7 us
  blocking collectives  52.9 us (80%)
  Pallas kernels  7.54 us (11%)
  local copies, waits for them, and re-layouts  4.58 us (7%)
  between operations  0.67 us (1%)
    all_to_all x2, blocking collectives, exchange(): lax.all_to_all(x, ('ens', 'tm', 'space'), 0, 0, tiled=True)  52.9 us
    unnamed x14, local copies, waits for them, and re-layouts  4.58 us
    pallas_call x1, Pallas kernels, by_layer(): pl.pallas_call(lambda *refs: pack_kernel(lon, merges, *refs), out_shape=j...  3.35 us
    pallas_call x1, Pallas kernels, by_layer(): pl.pallas_call(lambda *refs: layer_kernel(lon, merges, subwins, *refs), o...  2.7 us
    pallas_call x1, Pallas kernels, by_layer(): pl.pallas_call(lambda *refs: finish_kernel(lon, merges, *refs), out_shape...  1.49 us

profile of v2, /device:TPU:1, one launch (start us, length us, event | category | flops | bytes accessed | tf_op | source)
XLA Modules:
  0.0 65.7 jit_solution(10631029591986052940)
XLA Ops:
  0.6 0.0 copy-start
  0.6 1.0 %copy-done = f32[1,4,16,2,720]{4,3,2,1,0:T(2,128)S(1)} copy-done((f32[1,4,16,2,720]{4,3,2,1,0:T(2,128)S(1)}, f32[1,4,16,2,720]{4,3,2,1,0:T(2,128)}, u32[]{:S(2)}) %copy-start) | copy-done | bytes 368664
  1.6 0.0 copy-start.2
  1.6 1.0 %copy-done.2 = f32[1,4,16,2,720]{4,3,2,1,0:T(2,128)S(1)} copy-done((f32[1,4,16,2,720]{4,3,2,1,0:T(2,128)S(1)}, f32[1,4,16,2,720]{4,3,2,1,0:T(2,128)}, u32[]{:S(2)}) %copy-start.2) | copy-done | bytes 368664
  2.6 0.0 copy-start.3
  2.6 1.0 %copy-done.3 = s32[1,4,16,2,720]{4,3,2,1,0:T(2,128)S(1)} copy-done((s32[1,4,16,2,720]{4,3,2,1,0:T(2,128)S(1)}, s32[1,4,16,2,720]{4,3,2,1,0:T(2,128)}, u32[]{:S(2)}) %copy-start.3) | copy-done | bytes 368664
  3.6 0.0 copy-start.4
  3.6 0.9 %copy-done.4 = f32[2,16,2,720]{3,2,1,0:T(2,128)S(1)} copy-done((f32[2,16,2,720]{3,2,1,0:T(2,128)S(1)}, f32[2,16,2,720]{3,2,1,0:T(2,128)}, u32[]{:S(2)}) %copy-start.4) | copy-done | bytes 184344
  4.5 3.4 %pack.1 = f32[1664,128]{1,0:T(8,128)S(1)} custom-call(f32[4,16,2,720]{3,2,1,0:T(2,128)S(1)} %bitcast.15, f32[4,16,2,720]{3,2,1,0:T(2,128)S(1)} %bitcast.17, s32[4,16,2,720]{3,2,1,0:T(2,128)S(1)} %bitcast.18, f32[2,16,2,720]{3,2,1,0:T(2,128)S(1)} %copy-done.4), custom_call_target="tpu_custom_call" | custom-call | tf_op jit(solution)/shard_map/pack/pallas_call | solution.py:352
  7.9 29.1 %all_to_all.10 = f32[32,52,1,128]{3,2,1,0:T(1,128)S(1)} all-to-all(f32[32,52,1,128]{3,2,1,0:T(1,128)S(1)} %bitcast.11), channel_id=1, replica_groups=mesh['ens'=2,'space'=4,'tm'=4] {'ens','tm','space'}, dimensions={0} | all-to-all | bytes 1703936 | tf_op jit(solution)/shard_map/all_to_all | solution.py:348
  37.0 0.0 copy-start.5
  37.0 0.0 copy-start.6
  37.0 0.7 copy-done.5
  37.7 0.0 copy-done.6
  37.7 2.7 %layer.1 = f32[1536,128]{1,0:T(8,128)S(1)} custom-call(f32[1664,128]{1,0:T(8,128)S(1)} %bitcast.12, f32[16]{0:T(128)S(1)} %copy-done.5, f32[16]{0:T(128)S(1)} %copy-done.6), custom_call_target="tpu_custom_call" | custom-call | tf_op jit(solution)/shard_map/layer/pallas_call | solution.py:368
  40.4 0.0 copy-start.1
  40.4 23.8 %all_to_all.11 = f32[32,48,1,128]{3,1,2,0:T(8,128)S(1)} all-to-all(f32[32,48,1,128]{3,1,2,0:T(8,128)S(1)} %bitcast.14), channel_id=1, replica_groups=mesh['ens'=2,'space'=4,'tm'=4] {'ens','tm','space'}, dimensions={0} | all-to-all | bytes 1572864 | tf_op jit(solution)/shard_map/all_to_all | solution.py:348
  64.2 0.0 copy-done.1
  64.2 1.5 %finish.1 = (f32[4,16,2,720]{3,2,1,0:T(2,128)}, f32[4,16,2,720]{3,2,1,0:T(2,128)}) custom-call(f32[4,16,2,720]{3,2,1,0:T(2,128)S(1)} %bitcast.16, f32[1536,128]{1,0:T(8,128)S(1)} %bitcast.13), custom_call_target="tpu_custom_call" | custom-call | tf_op jit(solution)/shard_map/finish/pallas_call | solution.py:377
Async XLA Ops:
  0.6 1.0 %copy-start = (f32[1,4,16,2,720]{4,3,2,1,0:T(2,128)S(1)}, f32[1,4,16,2,720]{4,3,2,1,0:T(2,128)}, u32[]{:S(2)}) copy-start(f32[1,4,16,2,720]{4,3,2,1,0:T(2,128)} %param.6) | copy-start | bytes 1105924
  1.6 1.0 %copy-start.2 = (f32[1,4,16,2,720]{4,3,2,1,0:T(2,128)S(1)}, f32[1,4,16,2,720]{4,3,2,1,0:T(2,128)}, u32[]{:S(2)}) copy-start(f32[1,4,16,2,720]{4,3,2,1,0:T(2,128)} %param.7) | copy-start | bytes 1105924
  2.6 1.0 %copy-start.3 = (s32[1,4,16,2,720]{4,3,2,1,0:T(2,128)S(1)}, s32[1,4,16,2,720]{4,3,2,1,0:T(2,128)}, u32[]{:S(2)}) copy-start(s32[1,4,16,2,720]{4,3,2,1,0:T(2,128)} %param.8) | copy-start | bytes 1105924
  3.6 0.9 %copy-start.4 = (f32[2,16,2,720]{3,2,1,0:T(2,128)S(1)}, f32[2,16,2,720]{3,2,1,0:T(2,128)}, u32[]{:S(2)}) copy-start(f32[2,16,2,720]{3,2,1,0:T(2,128)} %refs_3_.1) | copy-start | bytes 552964
  37.0 0.7 copy-start.5
  37.0 0.7 %copy-start.6 = (f32[16]{0:T(128)S(1)}, f32[16]{0:T(128)}, u32[]{:S(2)}) copy-start(f32[16]{0:T(128)} %refs_2_.1) | copy-start | bytes 196
  40.4 23.8 %copy-start.1 = (f32[1,4,16,2,720]{4,3,2,1,0:T(2,128)S(1)}, f32[1,4,16,2,720]{4,3,2,1,0:T(2,128)}, u32[]{:S(2)}) copy-start(f32[1,4,16,2,720]{4,3,2,1,0:T(2,128)} %param.6) | copy-start | bytes 1105924

commit v3 on v2

--- a/solution.py
+++ b/solution.py
@@ -26,12 +26,16 @@
     return (core + 3 * REACH) % LANES, (core - 3 * REACH) % LANES
 
 
-def pack_kernel(lon, merges, b_hbm, e_hbm, o_hbm, w_hbm, out_ref, b_ref, e_ref, o_ref, w_ref, sems):
+def pack_kernel(
+    lon, merges, b_hbm, e_hbm, o_hbm, w_hbm, speed_hbm, couple_hbm, out_ref,
+    b_ref, e_ref, o_ref, w_ref, speed_ref, couple_ref, sems,
+):
     _, levels, share, _ = b_ref.shape
-    copies = [
-        pltpu.make_async_copy(src, dst, sems.at[i])
-        for i, (src, dst) in enumerate(((w_hbm, w_ref), (b_hbm, b_ref), (e_hbm, e_ref), (o_hbm, o_ref)))
-    ]
+    pairs = (
+        (b_hbm, b_ref), (w_hbm, w_ref), (speed_hbm, speed_ref), (couple_hbm, couple_ref),
+        (e_hbm, e_ref), (o_hbm, o_ref),
+    )
+    copies = [pltpu.make_async_copy(src, dst, sems.at[i]) for i, (src, dst) in enumerate(pairs)]
     for copy in copies:
         copy.start()
     full = lon // LANES
@@ -48,7 +52,7 @@
     def windows(x):
         tiles = [x[:, c * LANES : (c + 1) * LANES] for c in range(full)]
         tail = jnp.concatenate([x[:, full * LANES :], x[:, : LANES - rest]], axis=1)
-        ahead = x[:, lon - LANES :]
+        ahead = pltpu.roll(tail, LANES - rest, 1)
         ends = ((tiles[2], ahead), (tail, tiles[2]))
         halves = []
         for half, ((last, before), merge) in enumerate(zip(ends, merges)):
@@ -57,16 +61,8 @@
             halves.append((tiles[3 * half], tiles[3 * half + 1], merged, extra))
         return halves
 
-    copies[0].wait()
-    for level in range(levels):
-        east, north = windows(w_ref[0, level]), windows(w_ref[1, level])
-        for half in range(2):
-            picks = list(east[half][:3]) + list(north[half][:3]) + [east[half][3], north[half][3]]
-            value = picks[0]
-            for i in range(1, len(picks)):
-                value = jnp.where(turn == i, picks[i], value)
-            put(half, level, ROWS_IN - 1, value)
-    copies[1].wait()
+    for copy in copies[:4]:
+        copy.wait()
     for level in range(levels):
         extras = [None, None]
         for f in range(FIELDS):
@@ -76,10 +72,16 @@
                 moved = got[3] if f == 0 else pltpu.roll(got[3], LANES - 2 * REACH * f, 1)
                 edge = merges[half] + REACH - 2 * REACH * f
                 extras[half] = moved if f == 0 else jnp.where(lane < edge, moved, extras[half])
+        speeds = jnp.where(lane < LANES // 4, speed_ref[level], couple_ref[level])
         for half in range(2):
-            put(half, level, ROWS_IN - 2, extras[half])
-    copies[2].wait()
-    copies[3].wait()
+            put(half, level, ROWS_IN - 2, jnp.where(lane < LANES // 2, speeds, extras[half]))
+        for half, got in enumerate(windows(w_ref[jnp.where(turn < 2 * TILES, turn // TILES, turn - 2 * TILES), level])):
+            value = got[3]
+            for c in range(TILES):
+                value = jnp.where(jnp.logical_or(turn == c, turn == TILES + c), got[c], value)
+            put(half, level, ROWS_IN - 1, value)
+    copies[4].wait()
+    copies[5].wait()
     for level in range(levels):
         for f in range(FIELDS):
             shared = jnp.where(first_member, e_ref[f, level], o_ref[f, level].astype(jnp.float32))
@@ -88,11 +90,8 @@
                     put(half, level, (FIELDS + f) * TILES + c, got[c])
 
 
-def layer_kernel(lon, merges, subwins, in_ref, speed_ref, couple_ref, out_ref):
-    layer = lax.axis_index("tm") * lax.axis_size("space") + lax.axis_index("space")
+def layer_kernel(lon, merges, subwins, in_ref, out_ref):
     half = lax.axis_index("ens")
-    speed = 0.5 * speed_ref[layer]
-    couple = couple_ref[layer]
     lane = lax.broadcasted_iota(jnp.int32, (ROWS, LANES), 1)
     row = lax.broadcasted_iota(jnp.int32, (ROWS, LANES), 0)
     below = lane < jnp.where(half == 0, merges[0], merges[1])
@@ -101,6 +100,10 @@
 
     def load(member, t, k):
         return in_ref[pl.ds((member * subwins + t) * ROWS * ROWS_IN + k, ROWS, stride=ROWS_IN), :]
+
+    given = load(0, 0, ROWS_IN - 2)
+    speed = 0.5 * jnp.broadcast_to(given[:, :1], (ROWS, LANES))
+    couple = jnp.broadcast_to(given[:, LANES // 4 : LANES // 4 + 1], (ROWS, LANES))
 
     def back(x, by):
         moved = [pltpu.roll(v, by, 1) for v in x]
@@ -253,15 +256,15 @@
         two = operate(one, None, precision, observed)
         one, two = [[[aligned(f, x) for f, x in enumerate(state)] for state in y] for y in (one, two)]
         f0, f1, f2 = flat(plain), flat(one), flat(two)
-        bb, b1, s11, s12 = dot(f0, f0), dot(f0, f1), dot(f1, f1), dot(f1, f2)
-        step = jnp.where(b1 > 0.0, bb / jnp.where(b1 > 0.0, b1, 1.0), 0.0)
-        grow = jnp.where(bb > 0.0, step * step * s11 / jnp.where(bb > 0.0, bb, 1.0) - 1.0, 0.0)
+        s00, s01, s11, s02, s12 = dot(f0, f0), dot(f0, f1), dot(f1, f1), dot(f0, f2), dot(f1, f2)
+        step = jnp.where(s01 > 0.0, s00 / jnp.where(s01 > 0.0, s01, 1.0), 0.0)
+        more = jnp.where(s00 > 0.0, step * step * s11 / jnp.where(s00 > 0.0, s00, 1.0), 1.0)
         step_t = jnp.broadcast_to(step, (ROWS, LANES))
-        grow_t = jnp.broadcast_to(grow, (ROWS, LANES))
+        more_t = jnp.broadcast_to(more, (ROWS, LANES))
         res = [(c, v - step_t * w) for (c, v), (_, w) in zip(f0, f1)]
-        mov = [(c, v + grow_t * w) for (c, v), (_, w) in zip(res, f0)]
-        img = [(c, (v - step_t * w) + grow_t * v) for (c, v), (_, w) in zip(f1, f2)]
-        sums = [step, grow, bb, b1, s11, s12, dot(res, res), dot(res, f1), dot(mov, img), dot(mov, f2), dot(mov, f1)]
+        mov = [(c, more_t * v - step_t * w) for (c, v), (_, w) in zip(f0, f1)]
+        img = [(c, more_t * v - step_t * w) for (c, v), (_, w) in zip(f1, f2)]
+        sums = [step, more, s00, s01, s11, s02, s12, dot(res, res), dot(mov, img)]
         for t in range(subwins):
             for a, x in enumerate((one, two)):
                 for f in range(FIELDS):
@@ -277,7 +280,7 @@
                         out_ref[pl.ds(start, ROWS, stride=ROWS_OUT), :] = v
 
 
-def finish_kernel(lon, merges, b_ref, in_ref, x_ref, r_ref):
+def finish_kernel(lon, merges, b_ref, in_ref, x_hbm, r_hbm, x_ref, r_ref, sems):
     _, levels, share, _ = b_ref.shape
     full = lon // LANES
     rest = lon - full * LANES
@@ -290,18 +293,20 @@
         halves = [in_ref[pl.ds(half * levels * size + at, levels, stride=size), :] for half in range(2)]
         return jnp.concatenate([halves[0], pltpu.roll(halves[1], apart, 1)], axis=0)
 
-    step, grow, bb, b1, s11, s12, rr, r1, mi, m2, m1 = [sums(i) for i in range(11)]
+    step, more, s00, s01, s11, s02, s12, rr, mi = [sums(i) for i in range(9)]
 
     def total(x):
         return jnp.sum(x, axis=0, keepdims=True)
 
-    norm_0 = total(bb)
-    alpha_0 = norm_0 / total(b1)
+    norm_0 = total(s00)
+    alpha_0 = norm_0 / total(s01)
     d = step - alpha_0
-    norm_1 = total(rr + d * (2.0 * r1 + d * s11))
+    norm_1 = total(rr + d * (2.0 * (s01 - step * s11) + d * s11))
     beta = norm_1 / norm_0
-    g = beta - grow
-    curve = total(mi + 2.0 * (d * m2 + g * m1) + d * (d * s12 + 2.0 * g * s11) + g * g * b1)
+    g = (1.0 + beta) - more
+    cross_d = more * (s02 + s11) - 2.0 * step * s12
+    cross_g = 2.0 * more * s01 - step * (s11 + s02)
+    curve = total(mi + d * (cross_d + d * s12 + g * (s11 + s02)) + g * (cross_g + g * s01))
     alpha_1 = norm_1 / curve
     first = alpha_0 + alpha_1 * (1.0 + beta)
     second = alpha_0 * alpha_1
@@ -320,8 +325,9 @@
         middle = jnp.where(lane < at_lane, got[0][2], got[1][2])
         return got[0][:2] + [middle] + got[1]
 
-    for level in range(levels):
-        for f in range(FIELDS):
+    copies = []
+    for f in range(FIELDS):
+        for level in range(levels):
             b = b_ref[f, level]
             ones, twos = image(level, f), image(level, FIELDS + f)
             for c, (one, two) in enumerate(zip(ones, twos)):
@@ -331,6 +337,11 @@
                 part = b[:, c * LANES : c * LANES + width]
                 x_ref[f, level, :, cols] = first[:, :width] * part - second[:, :width] * one
                 r_ref[f, level, :, cols] = (part - first[:, :width] * one) + second[:, :width] * two
+        for i, (src, dst) in enumerate(((x_ref, x_hbm), (r_ref, r_hbm))):
+            copies.append(pltpu.make_async_copy(src.at[f], dst.at[f], sems.at[i, f]))
+            copies[-1].start()
+    for copy in copies:
+        copy.wait()
 
 
 def by_layer(right_side, error_precision, obs_count, background_wind, wave_speed, tracer_coupling):
@@ -338,7 +349,6 @@
     subwins = lax.axis_size("tm")
     merges = merge_lanes(lon)
     vmem = pl.BlockSpec(memory_space=pltpu.VMEM)
-    smem = pl.BlockSpec(memory_space=pltpu.SMEM)
     hbm = pl.BlockSpec(memory_space=pltpu.HBM)
     params = pltpu.CompilerParams(vmem_limit_bytes=48 * 1024 * 1024)
     state = (fields, levels, share, lon)
@@ -348,37 +358,41 @@
         return lax.all_to_all(x, ("ens", "tm", "space"), 0, 0, tiled=True).reshape(-1, LANES)
 
     b = right_side.reshape(state)
+    given = (b, error_precision.reshape(state), obs_count.reshape(state), background_wind, wave_speed, tracer_coupling)
     with jax.named_scope("pack"):
         packed = pl.pallas_call(
             lambda *refs: pack_kernel(lon, merges, *refs),
             out_shape=jax.ShapeDtypeStruct((2 * levels * share * ROWS_IN, LANES), jnp.float32),
-            in_specs=[hbm] * 4,
+            in_specs=[hbm] * len(given),
             out_specs=vmem,
             scratch_shapes=[
                 pltpu.VMEM(state, jnp.float32),
                 pltpu.VMEM(state, jnp.float32),
                 pltpu.VMEM(state, jnp.int32),
                 pltpu.VMEM(background_wind.shape, jnp.float32),
-                pltpu.SemaphoreType.DMA((4,)),
+                pltpu.SMEM(wave_speed.shape, jnp.float32),
+                pltpu.SMEM(tracer_coupling.shape, jnp.float32),
+                pltpu.SemaphoreType.DMA((len(given),)),
             ],
             compiler_params=params,
-        )(b, error_precision.reshape(state), obs_count.reshape(state), background_wind)
+        )(*[pltpu.with_memory_space_constraint(x, pltpu.HBM) for x in given])
     packed = exchange(packed)
     with jax.named_scope("layer"):
         images = pl.pallas_call(
             lambda *refs: layer_kernel(lon, merges, subwins, *refs),
             out_shape=jax.ShapeDtypeStruct((2 * levels * share * ROWS_OUT, LANES), jnp.float32),
-            in_specs=[vmem, smem, smem],
+            in_specs=[vmem],
             out_specs=vmem,
             compiler_params=params,
-        )(packed, wave_speed, tracer_coupling)
+        )(packed)
     images = exchange(images)
     with jax.named_scope("finish"):
         x, r = pl.pallas_call(
             lambda *refs: finish_kernel(lon, merges, *refs),
             out_shape=[jax.ShapeDtypeStruct(state, jnp.float32)] * 2,
             in_specs=[vmem] * 2,
-            out_specs=[vmem] * 2,
+            out_specs=[hbm] * 2,
+            scratch_shapes=[pltpu.VMEM(state, jnp.float32)] * 2 + [pltpu.SemaphoreType.DMA((2, FIELDS))],
             compiler_params=params,
         )(b, images)
     return x.reshape(right_side.shape), r.reshape(right_side.shape)

time: 66 us -> 60.1 us (0.911)
  local copies, waits for them, and re-layouts: 4.58 us -> 0.01 us
  Pallas kernels: 7.54 us -> 6.33 us
    unnamed x14 -> x2, local copies, waits for them, and re-layouts: 4.58 us -> 0.01 us
where the time goes in v3:
time: 60.1 us; the launch traced here: 59.9 us
  blocking collectives  52.9 us (88%)
  Pallas kernels  6.33 us (11%)
  between operations  0.66 us (1%)
    all_to_all x2, blocking collectives, exchange(): lax.all_to_all(x, ('ens', 'tm', 'space'), 0, 0, tiled=True)  52.9 us
    pallas_call x1, Pallas kernels, by_layer(): pl.pallas_call(lambda *refs: pack_kernel(lon, merges, *refs), out_shape=j...  2.81 us
    pallas_call x1, Pallas kernels, by_layer(): pl.pallas_call(lambda *refs: layer_kernel(lon, merges, subwins, *refs), o...  2.16 us
    pallas_call x1, Pallas kernels, by_layer(): pl.pallas_call(lambda *refs: finish_kernel(lon, merges, *refs), out_shape...  1.35 us

profile of v3, /device:TPU:1, one launch (start us, length us, event | category | flops | bytes accessed | tf_op | source)
XLA Modules:
  0.0 59.9 jit_solution(2420875294252001949)
XLA Ops:
  0.6 2.8 %pack.1 = f32[1664,128]{1,0:T(8,128)S(1)} custom-call(f32[4,16,2,720]{3,2,1,0:T(2,128)} %bitcast.15, f32[4,16,2,720]{3,2,1,0:T(2,128)} %bitcast.17, s32[4,16,2,720]{3,2,1,0:T(2,128)} %bitcast.18, f32[2,16,2,720]{3,2,1,0:T(2,128)} %refs_3_.1, f32[16]{0:T(128)} %refs_4_.1, f32[16]{0:T(128)} %refs_5_.1), custom_call_target="tpu_custom_call" | custom-call | tf_op jit(solution)/shard_map/pack/pallas_call | solution.py:363
  3.4 29.1 %all_to_all.10 = f32[32,52,1,128]{3,2,1,0:T(1,128)S(1)} all-to-all(f32[32,52,1,128]{3,2,1,0:T(1,128)S(1)} %bitcast.12), channel_id=1, replica_groups=mesh['ens'=2,'space'=4,'tm'=4] {'ens','tm','space'}, dimensions={0} | all-to-all | bytes 1703936 | tf_op jit(solution)/shard_map/all_to_all | solution.py:358
  32.6 2.2 %layer.1 = f32[1536,128]{1,0:T(8,128)S(1)} custom-call(f32[1664,128]{1,0:T(8,128)S(1)} %bitcast.11), custom_call_target="tpu_custom_call" | custom-call | tf_op jit(solution)/shard_map/layer/pallas_call | solution.py:381
  34.7 0.0 copy-start
  34.7 23.8 %all_to_all.11 = f32[32,48,1,128]{3,1,2,0:T(8,128)S(1)} all-to-all(f32[32,48,1,128]{3,1,2,0:T(8,128)S(1)} %bitcast.14), channel_id=1, replica_groups=mesh['ens'=2,'space'=4,'tm'=4] {'ens','tm','space'}, dimensions={0} | all-to-all | bytes 1572864 | tf_op jit(solution)/shard_map/all_to_all | solution.py:358
  58.5 0.0 copy-done
  58.5 1.4 %finish.1 = (f32[4,16,2,720]{3,2,1,0:T(2,128)}, f32[4,16,2,720]{3,2,1,0:T(2,128)}) custom-call(f32[4,16,2,720]{3,2,1,0:T(2,128)S(1)} %bitcast.16, f32[1536,128]{1,0:T(8,128)S(1)} %bitcast.13), custom_call_target="tpu_custom_call" | custom-call | tf_op jit(solution)/shard_map/finish/pallas_call | solution.py:390
Async XLA Ops:
  34.7 23.8 %copy-start = (f32[1,4,16,2,720]{4,3,2,1,0:T(2,128)S(1)}, f32[1,4,16,2,720]{4,3,2,1,0:T(2,128)}, u32[]{:S(2)}) copy-start(f32[1,4,16,2,720]{4,3,2,1,0:T(2,128)} %param.6) | copy-start | bytes 1105924

commit v4 on v3

--- a/solution.py
+++ b/solution.py
@@ -17,8 +17,13 @@
 TILES = 3
 REACH = 4
 FIELDS = 4
-ROWS_IN = FIELDS * TILES * 2 + 2
-ROWS_OUT = FIELDS * TILES * 2
+SLOT = 2 * REACH
+WINDS = LANES - FIELDS * SLOT
+FREE = 6 * REACH
+MIXED = 2 * FIELDS * TILES
+ROWS_IN = MIXED + 1
+THIRDS = 4 * FIELDS
+ROWS_OUT = THIRDS + 2 * FIELDS - 1
 
 
 def merge_lanes(lon):
@@ -28,66 +33,109 @@
 
 def pack_kernel(
     lon, merges, b_hbm, e_hbm, o_hbm, w_hbm, speed_hbm, couple_hbm, out_ref,
-    b_ref, e_ref, o_ref, w_ref, speed_ref, couple_ref, sems,
+    b_ref, e_ref, o_ref, w_ref, speed_ref, couple_ref, stage_ref, sems,
 ):
     _, levels, share, _ = b_ref.shape
-    pairs = (
-        (b_hbm, b_ref), (w_hbm, w_ref), (speed_hbm, speed_ref), (couple_hbm, couple_ref),
-        (e_hbm, e_ref), (o_hbm, o_ref),
-    )
-    copies = [pltpu.make_async_copy(src, dst, sems.at[i]) for i, (src, dst) in enumerate(pairs)]
-    for copy in copies:
-        copy.start()
     full = lon // LANES
     rest = lon - full * LANES
     member = lax.axis_index("ens")
-    first_member = member == 0
     turn = lax.axis_index("tm") * 2 + member
-    lane = lax.broadcasted_iota(jnp.int32, (share, LANES), 1)
-
-    def put(half, level, row, value):
-        base = (half * levels + level) * share * ROWS_IN
-        out_ref[pl.ds(base + row, share, stride=ROWS_IN), :] = value
-
-    def windows(x):
-        tiles = [x[:, c * LANES : (c + 1) * LANES] for c in range(full)]
-        tail = jnp.concatenate([x[:, full * LANES :], x[:, : LANES - rest]], axis=1)
-        ahead = pltpu.roll(tail, LANES - rest, 1)
-        ends = ((tiles[2], ahead), (tail, tiles[2]))
-        halves = []
-        for half, ((last, before), merge) in enumerate(zip(ends, merges)):
-            merged = jnp.where(lane < merge, last, before)
-            extra = jnp.where(lane < merge, before, last)
-            halves.append((tiles[3 * half], tiles[3 * half + 1], merged, extra))
-        return halves
-
-    for copy in copies[:4]:
+    comp = jnp.where(turn < 2 * TILES, turn // TILES, turn - 2 * TILES)
+    copy_b = pltpu.make_async_copy(b_hbm, b_ref, sems.at[0])
+    copy_e = pltpu.make_async_copy(e_hbm, e_ref, sems.at[1])
+    copy_o = pltpu.make_async_copy(o_hbm, o_ref, sems.at[2])
+    others = (
+        pltpu.make_async_copy(w_hbm.at[comp], w_ref, sems.at[3]),
+        pltpu.make_async_copy(speed_hbm, speed_ref, sems.at[4]),
+        pltpu.make_async_copy(couple_hbm, couple_ref, sems.at[5]),
+    )
+    copy_b.start()
+    pl.when(member == 0)(copy_e.start)
+    pl.when(member != 0)(copy_o.start)
+    for copy in others:
+        copy.start()
+    lane = lax.broadcasted_iota(jnp.int32, (ROWS, LANES), 1)
+    row = lax.broadcasted_iota(jnp.int32, (ROWS, LANES), 0)
+    group = ROWS // share
+
+    def raw(ref, first):
+        for level in range(levels):
+            for f in range(FIELDS):
+                for c in range(full + 1):
+                    half, tile = c // TILES, c % TILES
+                    width = LANES if c < full else rest
+                    value = ref[f, level, :, pl.ds(c * LANES, width)].astype(jnp.float32)
+                    start = (half * levels + level) * share * ROWS_IN + first + f * TILES + tile
+                    out_ref[pl.ds(start, share, stride=ROWS_IN), pl.ds(0, width)] = value
+
+    def place(half, g, k):
+        return pl.ds((half * levels + g * group) * share * ROWS_IN + k, ROWS, stride=ROWS_IN), slice(None)
+
+    def windows(first, third, last):
+        before = pltpu.roll(last, LANES - rest, 1)
+        after = jnp.where(lane < rest, last, pltpu.roll(first, rest, 1))
+        ends = ((third, before), (after, third))
+        merged = [jnp.where(lane < m, x, y) for m, (x, y) in zip(merges, ends)]
+        extra = [jnp.where(lane < m, y, x) for m, (x, y) in zip(merges, ends)]
+        return merged, extra
+
+    def merge(g, k):
+        merged, extra = windows(
+            out_ref[place(0, g, k)], out_ref[place(0, g, k + TILES - 1)], out_ref[place(1, g, k + TILES - 1)]
+        )
+        for half in range(2):
+            out_ref[place(half, g, k + TILES - 1)] = merged[half]
+        return extra
+
+    def by_level(ref, g):
+        value = jnp.full((ROWS, LANES), ref[g * group], jnp.float32)
+        for i in range(1, group):
+            value = jnp.where(row < i * share, value, ref[g * group + i])
+        return value
+
+    copy_b.wait()
+    raw(b_ref, 0)
+    for copy in others:
         copy.wait()
     for level in range(levels):
-        extras = [None, None]
+        for c in range(full + 1):
+            width = LANES if c < full else rest
+            stage_ref[c, pl.ds(level * share, share), pl.ds(0, width)] = w_ref[level, :, pl.ds(c * LANES, width)]
+    for g in range(levels // group):
+        mixed = [None, None]
         for f in range(FIELDS):
-            for half, got in enumerate(windows(b_ref[f, level])):
-                for c in range(TILES):
-                    put(half, level, f * TILES + c, got[c])
-                moved = got[3] if f == 0 else pltpu.roll(got[3], LANES - 2 * REACH * f, 1)
-                edge = merges[half] + REACH - 2 * REACH * f
-                extras[half] = moved if f == 0 else jnp.where(lane < edge, moved, extras[half])
-        speeds = jnp.where(lane < LANES // 4, speed_ref[level], couple_ref[level])
-        for half in range(2):
-            put(half, level, ROWS_IN - 2, jnp.where(lane < LANES // 2, speeds, extras[half]))
-        for half, got in enumerate(windows(w_ref[jnp.where(turn < 2 * TILES, turn // TILES, turn - 2 * TILES), level])):
-            value = got[3]
-            for c in range(TILES):
-                value = jnp.where(jnp.logical_or(turn == c, turn == TILES + c), got[c], value)
-            put(half, level, ROWS_IN - 1, value)
-    copies[4].wait()
-    copies[5].wait()
-    for level in range(levels):
+            extra = merge(g, f * TILES)
+            for half, m in enumerate(merges):
+                at = WINDS + f * SLOT
+                moved = pltpu.roll(extra[half], (at - (m - REACH)) % LANES, 1)
+                mixed[half] = moved if f == 0 else jnp.where(lane < at, mixed[half], moved)
+        tiles = [stage_ref[c, pl.ds(g * ROWS, ROWS), :] for c in range(full + 1)]
+        merged, extra = windows(tiles[0], tiles[2], tiles[5])
+        speed, couple = by_level(speed_ref, g), by_level(couple_ref, g)
+        for half, m in enumerate(merges):
+            parts = tiles[TILES * half : TILES * half + 2] + [merged[half]]
+            wind, left = parts[TILES - 1], pltpu.roll(parts[TILES - 1], LANES - SLOT * FIELDS, 1)
+            for c in reversed(range(TILES - 1)):
+                wind = jnp.where(jnp.logical_or(turn == c, turn == TILES + c), parts[c], wind)
+                by = (c + 1) * SLOT * FIELDS
+                left = jnp.where(lane < by, pltpu.roll(parts[c], by, 1), left)
+            wind = jnp.where(turn < 2 * TILES, wind, left)
+            value = jnp.where(lane < WINDS, wind, mixed[half])
+            value = jnp.where(lane == WINDS + SLOT, speed, value)
+            value = jnp.where(lane == WINDS + 2 * SLOT - 1, couple, value)
+            ends = pltpu.roll(extra[half], LANES - 1 - m, 1)
+            value = jnp.where(lane >= LANES - 2, ends, value)
+            out_ref[place(half, g, MIXED)] = value
+
+    def share_of(copy, ref):
+        copy.wait()
+        raw(ref, FIELDS * TILES)
+
+    pl.when(member == 0)(lambda: share_of(copy_e, e_ref))
+    pl.when(member != 0)(lambda: share_of(copy_o, o_ref))
+    for g in range(levels // group):
         for f in range(FIELDS):
-            shared = jnp.where(first_member, e_ref[f, level], o_ref[f, level].astype(jnp.float32))
-            for half, got in enumerate(windows(shared)):
-                for c in range(TILES):
-                    put(half, level, (FIELDS + f) * TILES + c, got[c])
+            merge(g, (FIELDS + f) * TILES)
 
 
 def layer_kernel(lon, merges, subwins, in_ref, out_ref):
@@ -96,14 +144,18 @@
     row = lax.broadcasted_iota(jnp.int32, (ROWS, LANES), 0)
     below = lane < jnp.where(half == 0, merges[0], merges[1])
     free_lo = jnp.where(half == 0, merges[0] - 3 * REACH, merges[1] - 3 * REACH)
-    free = jnp.logical_and(lane >= free_lo, lane < free_lo + 6 * REACH)
+    free = jnp.logical_and(lane >= free_lo, lane < free_lo + FREE)
 
     def load(member, t, k):
         return in_ref[pl.ds((member * subwins + t) * ROWS * ROWS_IN + k, ROWS, stride=ROWS_IN), :]
 
-    given = load(0, 0, ROWS_IN - 2)
-    speed = 0.5 * jnp.broadcast_to(given[:, :1], (ROWS, LANES))
-    couple = jnp.broadcast_to(given[:, LANES // 4 : LANES // 4 + 1], (ROWS, LANES))
+    def of_half(values):
+        return jnp.where(half == 0, values[0] % LANES, values[1] % LANES)
+
+    mixed = [[load(member, t, MIXED) for t in range(subwins)] for member in range(2)]
+    speed_at, couple_at = WINDS + SLOT, WINDS + 2 * SLOT - 1
+    speed = 0.5 * jnp.broadcast_to(mixed[0][0][:, speed_at : speed_at + 1], (ROWS, LANES))
+    couple = jnp.broadcast_to(mixed[0][0][:, couple_at : couple_at + 1], (ROWS, LANES))
 
     def back(x, by):
         moved = [pltpu.roll(v, by, 1) for v in x]
@@ -143,14 +195,20 @@
         return [[load(member, t, (at + f) * TILES + c) for c in range(TILES)] for f in range(FIELDS)]
 
     def extras_of(member, t):
-        packed = load(member, t, ROWS_IN - 2)
-        return [packed] + [pltpu.roll(packed, 2 * REACH * f, 1) for f in range(1, FIELDS)]
+        shifts = [of_half([m - REACH - WINDS - f * SLOT for m in merges]) for f in range(FIELDS)]
+        return [pltpu.roll(mixed[member][t], by, 1) for by in shifts]
 
     def stag(state):
         return [staggered(f, x) for f, x in enumerate(state)]
 
-    def wind(turn):
-        return load(turn % 2, turn // 2, ROWS_IN - 1)
+    def wind(comp):
+        sent = [mixed[turn % 2][turn // 2] for turn in range(2 * subwins)]
+        left = sent[2 * TILES + comp]
+        tiles = []
+        for c in range(TILES):
+            by = WINDS - c * SLOT * FIELDS
+            tiles.append(jnp.where(lane < WINDS, sent[comp * TILES + c], pltpu.roll(left, by, 1)))
+        return tiles, pltpu.roll(sent[comp * TILES], of_half([m + 1 - LANES for m in merges]), 1)
 
     stay = 1.0 - 4.0 * diffusion
     grad_p = jnp.where(row == ROWS - 2, 0.0, speed)
@@ -166,9 +224,9 @@
             [jnp.where(row == 0, 0.0, diffusion + 0.5 * v) for v in north],
         )
 
-    east, north = [wind(i) for i in range(3)], [wind(3 + i) for i in range(3)]
+    (east, east_extra), (north, north_extra) = wind(0), wind(1)
     narrow = coefficients(east, north)
-    wide = coefficients(widened(east, wind(6)), widened(north, wind(7)))
+    wide = coefficients(widened(east, east_extra), widened(north, north_extra))
 
     def tangent(state, coefs):
         h, u, v, q = state
@@ -265,22 +323,31 @@
         mov = [(c, more_t * v - step_t * w) for (c, v), (_, w) in zip(f0, f1)]
         img = [(c, more_t * v - step_t * w) for (c, v), (_, w) in zip(f1, f2)]
         sums = [step, more, s00, s01, s11, s02, s12, dot(res, res), dot(mov, img)]
+        sums += [sums[-1]] * (-len(sums) % 6)
         for t in range(subwins):
-            for a, x in enumerate((one, two)):
-                for f in range(FIELDS):
-                    for c in range(TILES):
-                        v = x[t][f][c]
-                        at = (a * FIELDS + f) * TILES + c
-                        if c == TILES - 1:
-                            i = a * FIELDS + f
-                            even = sums[i]
-                            odd = sums[i + 8] if i + 8 < len(sums) else jnp.zeros_like(even)
-                            v = jnp.where(free, jnp.where(row % 2 == 0, even, odd), v)
-                        start = (member * subwins + t) * ROWS * ROWS_OUT + at
-                        out_ref[pl.ds(start, ROWS, stride=ROWS_OUT), :] = v
-
-
-def finish_kernel(lon, merges, b_ref, in_ref, x_hbm, r_hbm, x_ref, r_ref, sems):
+
+            def put(k, value):
+                start = (member * subwins + t) * ROWS * ROWS_OUT + k
+                out_ref[pl.ds(start, ROWS, stride=ROWS_OUT), :] = value
+
+            images = one[t] + two[t]
+            last = images[-1][TILES - 1]
+            for k, x in enumerate(images):
+                put(2 * k, x[0])
+                put(2 * k + 1, x[1])
+                if k < 5:
+                    put(THIRDS + k, jnp.where(free, pltpu.roll(last, (-(k + 1) * FREE) % LANES, 1), x[2]))
+                elif k < 2 * FIELDS - 1:
+                    rows = []
+                    for i in (k - 5, k - 3):
+                        value = sums[3 * i + 2]
+                        for j in (1, 0):
+                            value = jnp.where(lane < free_lo + (j + 1) * SLOT, sums[3 * i + j], value)
+                        rows.append(value)
+                    put(THIRDS + k, jnp.where(free, jnp.where(row % 2 == 0, rows[0], rows[1]), x[2]))
+
+
+def finish_kernel(lon, merges, b_ref, in_ref, x_hbm, r_hbm, x_ref, r_ref, last_ref, sems):
     _, levels, share, _ = b_ref.shape
     full = lon // LANES
     rest = lon - full * LANES
@@ -288,10 +355,17 @@
     apart = merges[0] - merges[1]
     at_lane = merges[0] - 3 * REACH
 
+    group = ROWS // share
+
+    slots = []
+    for i in range(3):
+        at = THIRDS + 5 + i % 2 + (i // 2) * ROWS_OUT
+        halves = [in_ref[pl.ds(half * levels * size + at, levels, stride=size), :] for half in range(2)]
+        slots.append(jnp.concatenate([halves[0], pltpu.roll(halves[1], apart, 1)], axis=0))
+
     def sums(i):
-        at = (i // 8) * ROWS_OUT + (i % 8) * TILES + TILES - 1
-        halves = [in_ref[pl.ds(half * levels * size + at, levels, stride=size), :] for half in range(2)]
-        return jnp.concatenate([halves[0], pltpu.roll(halves[1], apart, 1)], axis=0)
+        value = slots[i // 3]
+        return pltpu.roll(value, LANES - (i % 3) * SLOT, 1) if i % 3 else value
 
     step, more, s00, s01, s11, s02, s12, rr, mi = [sums(i) for i in range(9)]
 
@@ -314,14 +388,28 @@
     second = jnp.broadcast_to(second[:, at_lane : at_lane + 1], (share, LANES))
     lane = lax.broadcasted_iota(jnp.int32, (share, LANES), 1)
 
+    lane_8 = lax.broadcasted_iota(jnp.int32, (ROWS, LANES), 1)
+    for half in range(2):
+        for g in range(levels // group):
+            value = None
+            for k in range(5):
+                start = (half * levels + g * group) * size + THIRDS + k
+                part = pltpu.roll(in_ref[pl.ds(start, ROWS, stride=ROWS_OUT), :], (k + 1) * FREE % LANES, 1)
+                begin = (merges[half] - 3 * REACH + (k + 1) * FREE) % LANES
+                here = jnp.logical_and(lane_8 >= begin, lane_8 < begin + FREE)
+                value = part if value is None else jnp.where(here, part, value)
+            last_ref[half, pl.ds(g * ROWS, ROWS), :] = value
+
     def image(level, k):
-        got = [
-            [
-                in_ref[pl.ds((half * levels + level) * size + k * TILES + c, share, stride=ROWS_OUT), :]
-                for c in range(TILES)
-            ]
-            for half in range(2)
-        ]
+        got = []
+        for half in range(2):
+            start = (half * levels + level) * size
+            tiles = [in_ref[pl.ds(start + 2 * k + c, share, stride=ROWS_OUT), :] for c in range(2)]
+            if k < 2 * FIELDS - 1:
+                tiles.append(in_ref[pl.ds(start + THIRDS + k, share, stride=ROWS_OUT), :])
+            else:
+                tiles.append(last_ref[half, pl.ds(level * share, share), :])
+            got.append(tiles)
         middle = jnp.where(lane < at_lane, got[0][2], got[1][2])
         return got[0][:2] + [middle] + got[1]
 
@@ -369,9 +457,10 @@
                 pltpu.VMEM(state, jnp.float32),
                 pltpu.VMEM(state, jnp.float32),
                 pltpu.VMEM(state, jnp.int32),
-                pltpu.VMEM(background_wind.shape, jnp.float32),
+                pltpu.VMEM(background_wind.shape[1:], jnp.float32),
                 pltpu.SMEM(wave_speed.shape, jnp.float32),
                 pltpu.SMEM(tracer_coupling.shape, jnp.float32),
+                pltpu.VMEM((lon // LANES + 1, levels * share, LANES), jnp.float32),
                 pltpu.SemaphoreType.DMA((len(given),)),
             ],
             compiler_params=params,
@@ -392,7 +481,12 @@
             out_shape=[jax.ShapeDtypeStruct(state, jnp.float32)] * 2,
             in_specs=[vmem] * 2,
             out_specs=[hbm] * 2,
-            scratch_shapes=[pltpu.VMEM(state, jnp.float32)] * 2 + [pltpu.SemaphoreType.DMA((2, FIELDS))],
+            scratch_shapes=[
+                pltpu.VMEM(state, jnp.float32),
+                pltpu.VMEM(state, jnp.float32),
+                pltpu.VMEM((2, levels * share, LANES), jnp.float32),
+                pltpu.SemaphoreType.DMA((2, FIELDS)),
+            ],
             compiler_params=params,
         )(b, images)
     return x.reshape(right_side.shape), r.reshape(right_side.shape)

time: 60.1 us -> 57.9 us (0.963)
  blocking collectives: 52.9 us -> 51.5 us
  Pallas kernels: 6.33 us -> 5.53 us
    all_to_all x2, blocking collectives: 52.9 us -> 51.5 us  [exchange(): lax.all_to_all(x, ('ens', 'tm', 'space'), 0, 0, tiled=True)]
    pallas_call x1, Pallas kernels: 2.81 us -> 1.76 us  [by_layer(): pl.pallas_call(lambda *refs: pack_kernel(lon, merges, *refs), out_shape=j...]
where the time goes in v4:
time: 57.9 us; the launch traced here: 57.7 us
  blocking collectives  51.5 us (89%)
  Pallas kernels  5.53 us (10%)
  between operations  0.66 us (1%)
    all_to_all x2, blocking collectives, exchange(): lax.all_to_all(x, ('ens', 'tm', 'space'), 0, 0, tiled=True)  51.5 us
    pallas_call x1, Pallas kernels, by_layer(): pl.pallas_call(lambda *refs: layer_kernel(lon, merges, subwins, *refs), o...  2.27 us
    pallas_call x1, Pallas kernels, by_layer(): pl.pallas_call(lambda *refs: pack_kernel(lon, merges, *refs), out_shape=j...  1.76 us
    pallas_call x1, Pallas kernels, by_layer(): pl.pallas_call(lambda *refs: finish_kernel(lon, merges, *refs), out_shape...  1.49 us

profile of v4, /device:TPU:1, one launch (start us, length us, event | category | flops | bytes accessed | tf_op | source)
XLA Modules:
  0.0 57.7 jit_solution(15115307258623551587)
XLA Ops:
  0.6 1.8 %pack.1 = f32[1600,128]{1,0:T(8,128)S(1)} custom-call(f32[4,16,2,720]{3,2,1,0:T(2,128)} %bitcast.13, f32[4,16,2,720]{3,2,1,0:T(2,128)} %bitcast.15, s32[4,16,2,720]{3,2,1,0:T(2,128)} %bitcast.16, f32[2,16,2,720]{3,2,1,0:T(2,128)} %refs_3_.1, f32[16]{0:T(128)} %refs_4_.1, f32[16]{0:T(128)} %refs_5_.1), custom_call_target="tpu_custom_call" | custom-call | tf_op jit(solution)/shard_map/pack/pallas_call | solution.py:451
  2.4 28.4 %all_to_all.10 = f32[32,50,1,128]{3,2,1,0:T(1,128)S(1)} all-to-all(f32[32,50,1,128]{3,2,1,0:T(1,128)S(1)} %bitcast.10), channel_id=1, replica_groups=mesh['ens'=2,'space'=4,'tm'=4] {'ens','tm','space'}, dimensions={0} | all-to-all | bytes 1638400 | tf_op jit(solution)/shard_map/all_to_all | solution.py:446
  30.8 2.3 %layer.1 = f32[1472,128]{1,0:T(8,128)S(1)} custom-call(f32[1600,128]{1,0:T(8,128)S(1)} %bitcast.9), custom_call_target="tpu_custom_call" | custom-call | tf_op jit(solution)/shard_map/layer/pallas_call | solution.py:470
  33.1 0.0 copy-start
  33.1 23.1 %all_to_all.11 = f32[32,46,1,128]{3,2,1,0:T(1,128)S(1)} all-to-all(f32[32,46,1,128]{3,2,1,0:T(1,128)S(1)} %bitcast.12), channel_id=1, replica_groups=mesh['ens'=2,'space'=4,'tm'=4] {'ens','tm','space'}, dimensions={0} | all-to-all | bytes 1507328 | tf_op jit(solution)/shard_map/all_to_all | solution.py:446
  56.2 0.0 copy-done
  56.2 1.5 %finish.1 = (f32[4,16,2,720]{3,2,1,0:T(2,128)}, f32[4,16,2,720]{3,2,1,0:T(2,128)}) custom-call(f32[4,16,2,720]{3,2,1,0:T(2,128)S(1)} %bitcast.14, f32[1472,128]{1,0:T(8,128)S(1)} %bitcast.11), custom_call_target="tpu_custom_call" | custom-call | tf_op jit(solution)/shard_map/finish/pallas_call | solution.py:479
Async XLA Ops:
  33.1 23.1 %copy-start = (f32[1,4,16,2,720]{4,3,2,1,0:T(2,128)S(1)}, f32[1,4,16,2,720]{4,3,2,1,0:T(2,128)}, u32[]{:S(2)}) copy-start(f32[1,4,16,2,720]{4,3,2,1,0:T(2,128)} %param.6) | copy-start | bytes 1105924

commit v5 on v4

--- a/solution.py
+++ b/solution.py
@@ -41,26 +41,32 @@
     member = lax.axis_index("ens")
     turn = lax.axis_index("tm") * 2 + member
     comp = jnp.where(turn < 2 * TILES, turn // TILES, turn - 2 * TILES)
-    copy_b = pltpu.make_async_copy(b_hbm, b_ref, sems.at[0])
-    copy_e = pltpu.make_async_copy(e_hbm, e_ref, sems.at[1])
-    copy_o = pltpu.make_async_copy(o_hbm, o_ref, sems.at[2])
+
+    def by_field(hbm, ref, first):
+        return [pltpu.make_async_copy(hbm, ref, sems.at[first])]
+
+    def start(copies):
+        for copy in copies:
+            copy.start()
+
+    copies_b, copies_e, copies_o = by_field(b_hbm, b_ref, 0), by_field(e_hbm, e_ref, FIELDS), by_field(o_hbm, o_ref, FIELDS)
     others = (
-        pltpu.make_async_copy(w_hbm.at[comp], w_ref, sems.at[3]),
-        pltpu.make_async_copy(speed_hbm, speed_ref, sems.at[4]),
-        pltpu.make_async_copy(couple_hbm, couple_ref, sems.at[5]),
-    )
-    copy_b.start()
-    pl.when(member == 0)(copy_e.start)
-    pl.when(member != 0)(copy_o.start)
-    for copy in others:
-        copy.start()
+        pltpu.make_async_copy(w_hbm.at[comp], w_ref, sems.at[2 * FIELDS]),
+        pltpu.make_async_copy(speed_hbm, speed_ref, sems.at[2 * FIELDS + 1]),
+        pltpu.make_async_copy(couple_hbm, couple_ref, sems.at[2 * FIELDS + 2]),
+    )
+    start(copies_b)
+    pl.when(member == 0)(lambda: start(copies_e))
+    pl.when(member != 0)(lambda: start(copies_o))
+    start(others)
     lane = lax.broadcasted_iota(jnp.int32, (ROWS, LANES), 1)
     row = lax.broadcasted_iota(jnp.int32, (ROWS, LANES), 0)
     group = ROWS // share
 
-    def raw(ref, first):
-        for level in range(levels):
-            for f in range(FIELDS):
+    def raw(copies, ref, first):
+        copies[0].wait()
+        for f in range(FIELDS):
+            for level in range(levels):
                 for c in range(full + 1):
                     half, tile = c // TILES, c % TILES
                     width = LANES if c < full else rest
@@ -93,8 +99,9 @@
             value = jnp.where(row < i * share, value, ref[g * group + i])
         return value
 
-    copy_b.wait()
-    raw(b_ref, 0)
+    raw(copies_b, b_ref, 0)
+    pl.when(member == 0)(lambda: raw(copies_e, e_ref, FIELDS * TILES))
+    pl.when(member != 0)(lambda: raw(copies_o, o_ref, FIELDS * TILES))
     for copy in others:
         copy.wait()
     for level in range(levels):
@@ -127,12 +134,6 @@
             value = jnp.where(lane >= LANES - 2, ends, value)
             out_ref[place(half, g, MIXED)] = value
 
-    def share_of(copy, ref):
-        copy.wait()
-        raw(ref, FIELDS * TILES)
-
-    pl.when(member == 0)(lambda: share_of(copy_e, e_ref))
-    pl.when(member != 0)(lambda: share_of(copy_o, o_ref))
     for g in range(levels // group):
         for f in range(FIELDS):
             merge(g, (FIELDS + f) * TILES)
@@ -306,17 +307,17 @@
     observed = [stag(fields_of(1, t, FIELDS)) for t in range(subwins)]
     for member in range(2):
         plain = [fields_of(member, t, 0) for t in range(subwins)]
-        b = [stag(x) for x in plain]
         b_wide = [
             stag([widened(x, e) for x, e in zip(plain[t], extras_of(member, t))]) for t in range(subwins - 1)
         ]
+        b = [[narrowed(x) for x in state] for state in b_wide] + [stag(plain[-1])]
         one = operate(b, b_wide, precision, observed)
         two = operate(one, None, precision, observed)
         one, two = [[[aligned(f, x) for f, x in enumerate(state)] for state in y] for y in (one, two)]
         f0, f1, f2 = flat(plain), flat(one), flat(two)
         s00, s01, s11, s02, s12 = dot(f0, f0), dot(f0, f1), dot(f1, f1), dot(f0, f2), dot(f1, f2)
-        step = jnp.where(s01 > 0.0, s00 / jnp.where(s01 > 0.0, s01, 1.0), 0.0)
-        more = jnp.where(s00 > 0.0, step * step * s11 / jnp.where(s00 > 0.0, s00, 1.0), 1.0)
+        step = jnp.where(s11 > 0.0, s01 / jnp.where(s11 > 0.0, s11, 1.0), 0.0)
+        more = 2.0 - jnp.where(s00 > 0.0, step * s01 / jnp.where(s00 > 0.0, s00, 1.0), 0.0)
         step_t = jnp.broadcast_to(step, (ROWS, LANES))
         more_t = jnp.broadcast_to(more, (ROWS, LANES))
         res = [(c, v - step_t * w) for (c, v), (_, w) in zip(f0, f1)]
@@ -388,17 +389,18 @@
     second = jnp.broadcast_to(second[:, at_lane : at_lane + 1], (share, LANES))
     lane = lax.broadcasted_iota(jnp.int32, (share, LANES), 1)
 
-    lane_8 = lax.broadcasted_iota(jnp.int32, (ROWS, LANES), 1)
-    for half in range(2):
-        for g in range(levels // group):
-            value = None
-            for k in range(5):
-                start = (half * levels + g * group) * size + THIRDS + k
-                part = pltpu.roll(in_ref[pl.ds(start, ROWS, stride=ROWS_OUT), :], (k + 1) * FREE % LANES, 1)
-                begin = (merges[half] - 3 * REACH + (k + 1) * FREE) % LANES
-                here = jnp.logical_and(lane_8 >= begin, lane_8 < begin + FREE)
-                value = part if value is None else jnp.where(here, part, value)
-            last_ref[half, pl.ds(g * ROWS, ROWS), :] = value
+    def gather_last():
+        lane_8 = lax.broadcasted_iota(jnp.int32, (ROWS, LANES), 1)
+        for half in range(2):
+            for g in range(levels // group):
+                value = None
+                for k in range(5):
+                    start = (half * levels + g * group) * size + THIRDS + k
+                    part = pltpu.roll(in_ref[pl.ds(start, ROWS, stride=ROWS_OUT), :], (k + 1) * FREE % LANES, 1)
+                    begin = (merges[half] - 3 * REACH + (k + 1) * FREE) % LANES
+                    here = jnp.logical_and(lane_8 >= begin, lane_8 < begin + FREE)
+                    value = part if value is None else jnp.where(here, part, value)
+                last_ref[half, pl.ds(g * ROWS, ROWS), :] = value
 
     def image(level, k):
         got = []
@@ -415,6 +417,8 @@
 
     copies = []
     for f in range(FIELDS):
+        if f == FIELDS - 1:
+            gather_last()
         for level in range(levels):
             b = b_ref[f, level]
             ones, twos = image(level, f), image(level, FIELDS + f)
@@ -461,7 +465,7 @@
                 pltpu.SMEM(wave_speed.shape, jnp.float32),
                 pltpu.SMEM(tracer_coupling.shape, jnp.float32),
                 pltpu.VMEM((lon // LANES + 1, levels * share, LANES), jnp.float32),
-                pltpu.SemaphoreType.DMA((len(given),)),
+                pltpu.SemaphoreType.DMA((2 * FIELDS + 3,)),
             ],
             compiler_params=params,
         )(*[pltpu.with_memory_space_constraint(x, pltpu.HBM) for x in given])

time: 57.9 us -> 57.9 us (level)
  no operation moved by 1% of the time
where the time goes in v5:
time: 57.9 us; the launch traced here: 57.7 us
  blocking collectives  51.5 us (89%)
  Pallas kernels  5.51 us (10%)
  between operations  0.66 us (1%)
    all_to_all x2, blocking collectives, exchange(): lax.all_to_all(x, ('ens', 'tm', 'space'), 0, 0, tiled=True)  51.5 us
    pallas_call x1, Pallas kernels, by_layer(): pl.pallas_call(lambda *refs: layer_kernel(lon, merges, subwins, *refs), o...  2.24 us
    pallas_call x1, Pallas kernels, by_layer(): pl.pallas_call(lambda *refs: pack_kernel(lon, merges, *refs), out_shape=j...  1.78 us
    pallas_call x1, Pallas kernels, by_layer(): pl.pallas_call(lambda *refs: finish_kernel(lon, merges, *refs), out_shape...  1.49 us

profile of v5, /device:TPU:1, one launch (start us, length us, event | category | flops | bytes accessed | tf_op | source)
XLA Modules:
  0.0 57.7 jit_solution(6358128852248397067)
XLA Ops:
  0.6 1.8 %pack.1 = f32[1600,128]{1,0:T(8,128)S(1)} custom-call(f32[4,16,2,720]{3,2,1,0:T(2,128)} %bitcast.13, f32[4,16,2,720]{3,2,1,0:T(2,128)} %bitcast.15, s32[4,16,2,720]{3,2,1,0:T(2,128)} %bitcast.16, f32[2,16,2,720]{3,2,1,0:T(2,128)} %refs_3_.1, f32[16]{0:T(128)} %refs_4_.1, f32[16]{0:T(128)} %refs_5_.1), custom_call_target="tpu_custom_call" | custom-call | tf_op jit(solution)/shard_map/pack/pallas_call | solution.py:455
  2.4 28.4 %all_to_all.10 = f32[32,50,1,128]{3,2,1,0:T(1,128)S(1)} all-to-all(f32[32,50,1,128]{3,2,1,0:T(1,128)S(1)} %bitcast.10), channel_id=1, replica_groups=mesh['ens'=2,'space'=4,'tm'=4] {'ens','tm','space'}, dimensions={0} | all-to-all | bytes 1638400 | tf_op jit(solution)/shard_map/all_to_all | solution.py:450
  30.8 2.2 %layer.1 = f32[1472,128]{1,0:T(8,128)S(1)} custom-call(f32[1600,128]{1,0:T(8,128)S(1)} %bitcast.9), custom_call_target="tpu_custom_call" | custom-call | tf_op jit(solution)/shard_map/layer/pallas_call | solution.py:474
  33.1 0.0 copy-start
  33.1 23.1 %all_to_all.11 = f32[32,46,1,128]{3,2,1,0:T(1,128)S(1)} all-to-all(f32[32,46,1,128]{3,2,1,0:T(1,128)S(1)} %bitcast.12), channel_id=1, replica_groups=mesh['ens'=2,'space'=4,'tm'=4] {'ens','tm','space'}, dimensions={0} | all-to-all | bytes 1507328 | tf_op jit(solution)/shard_map/all_to_all | solution.py:450
  56.2 0.0 copy-done
  56.2 1.5 %finish.1 = (f32[4,16,2,720]{3,2,1,0:T(2,128)}, f32[4,16,2,720]{3,2,1,0:T(2,128)}) custom-call(f32[4,16,2,720]{3,2,1,0:T(2,128)S(1)} %bitcast.14, f32[1472,128]{1,0:T(8,128)S(1)} %bitcast.11), custom_call_target="tpu_custom_call" | custom-call | tf_op jit(solution)/shard_map/finish/pallas_call | solution.py:483
Async XLA Ops:
  33.1 23.1 %copy-start = (f32[1,4,16,2,720]{4,3,2,1,0:T(2,128)S(1)}, f32[1,4,16,2,720]{4,3,2,1,0:T(2,128)}, u32[]{:S(2)}) copy-start(f32[1,4,16,2,720]{4,3,2,1,0:T(2,128)} %param.6) | copy-start | bytes 1105924

commit v6 on v5

--- a/solution.py
+++ b/solution.py
@@ -42,18 +42,21 @@
     turn = lax.axis_index("tm") * 2 + member
     comp = jnp.where(turn < 2 * TILES, turn // TILES, turn - 2 * TILES)
 
-    def by_field(hbm, ref, first):
-        return [pltpu.make_async_copy(hbm, ref, sems.at[first])]
+    def in_halves(hbm, ref, first):
+        n = FIELDS // 2
+        return [
+            pltpu.make_async_copy(hbm.at[pl.ds(i * n, n)], ref.at[pl.ds(i * n, n)], sems.at[first + i]) for i in range(2)
+        ]
 
     def start(copies):
         for copy in copies:
             copy.start()
 
-    copies_b, copies_e, copies_o = by_field(b_hbm, b_ref, 0), by_field(e_hbm, e_ref, FIELDS), by_field(o_hbm, o_ref, FIELDS)
+    copies_b, copies_e, copies_o = in_halves(b_hbm, b_ref, 0), in_halves(e_hbm, e_ref, 2), in_halves(o_hbm, o_ref, 7)
     others = (
-        pltpu.make_async_copy(w_hbm.at[comp], w_ref, sems.at[2 * FIELDS]),
-        pltpu.make_async_copy(speed_hbm, speed_ref, sems.at[2 * FIELDS + 1]),
-        pltpu.make_async_copy(couple_hbm, couple_ref, sems.at[2 * FIELDS + 2]),
+        pltpu.make_async_copy(w_hbm.at[comp], w_ref, sems.at[4]),
+        pltpu.make_async_copy(speed_hbm, speed_ref, sems.at[5]),
+        pltpu.make_async_copy(couple_hbm, couple_ref, sems.at[6]),
     )
     start(copies_b)
     pl.when(member == 0)(lambda: start(copies_e))
@@ -64,8 +67,9 @@
     group = ROWS // share
 
     def raw(copies, ref, first):
-        copies[0].wait()
         for f in range(FIELDS):
+            if f % 2 == 0:
+                copies[f // 2].wait()
             for level in range(levels):
                 for c in range(full + 1):
                     half, tile = c // TILES, c % TILES
@@ -231,11 +235,12 @@
 
     def tangent(state, coefs):
         h, u, v, q = state
+        u_back = [a - speed * (n - m) for a, n, m in zip(back(u, 2), h, back(h, 2))]
         u = [a - speed * (n - m) for a, n, m in zip(u, ahead(h, 2), h)]
         v = [a - (grad_p * n - grad_m * m) for a, n, m in zip(v, up(h, 2), h)]
         h = [
             a - (speed * (p - m) + (div_p * n - div_m * s))
-            for a, p, m, n, s in zip(h, u, back(u, 2), v, down(v, 2))
+            for a, p, m, n, s in zip(h, u, u_back, v, down(v, 2))
         ]
         q = [
             stay * a + (em * e + ep * w) + (nm * n + np * s) + couple * p
@@ -248,11 +253,12 @@
     def adjoint(state, coefs):
         h, u, v, q = state
         h = [a + couple * b for a, b in zip(h, q)]
+        u_back = [a + speed * (n - m) for a, n, m in zip(back(u, 2), h, back(h, 2))]
         u = [a + speed * (n - m) for a, n, m in zip(u, ahead(h, 2), h)]
         v = [a + (grad_p * n - grad_m * m) for a, n, m in zip(v, up(h, 2), h)]
         h = [
             a + (speed * (p - m) + (div_p * n - div_m * s))
-            for a, p, m, n, s in zip(h, u, back(u, 2), v, down(v, 2))
+            for a, p, m, n, s in zip(h, u, u_back, v, down(v, 2))
         ]
         e = ahead([a * b for a, b in zip(coefs[1], q)], 1)
         w = back([a * b for a, b in zip(coefs[0], q)], 1)
@@ -465,7 +471,7 @@
                 pltpu.SMEM(wave_speed.shape, jnp.float32),
                 pltpu.SMEM(tracer_coupling.shape, jnp.float32),
                 pltpu.VMEM((lon // LANES + 1, levels * share, LANES), jnp.float32),
-                pltpu.SemaphoreType.DMA((2 * FIELDS + 3,)),
+                pltpu.SemaphoreType.DMA((9,)),
             ],
             compiler_params=params,
         )(*[pltpu.with_memory_space_constraint(x, pltpu.HBM) for x in given])

time: 57.9 us -> 57.6 us (level)
  no operation moved by 1% of the time
where the time goes in v6:
time: 57.6 us; the launch traced here: 57.5 us
  blocking collectives  51.5 us (89%)
  Pallas kernels  5.28 us (9%)
  between operations  0.66 us (1%)
    all_to_all x2, blocking collectives, exchange(): lax.all_to_all(x, ('ens', 'tm', 'space'), 0, 0, tiled=True)  51.5 us
    pallas_call x1, Pallas kernels, by_layer(): pl.pallas_call(lambda *refs: layer_kernel(lon, merges, subwins, *refs), o...  2.07 us
    pallas_call x1, Pallas kernels, by_layer(): pl.pallas_call(lambda *refs: pack_kernel(lon, merges, *refs), out_shape=j...  1.72 us
    pallas_call x1, Pallas kernels, by_layer(): pl.pallas_call(lambda *refs: finish_kernel(lon, merges, *refs), out_shape...  1.49 us

profile of v6, /device:TPU:1, one launch (start us, length us, event | category | flops | bytes accessed | tf_op | source)
XLA Modules:
  0.0 57.5 jit_solution(568621450180812071)
XLA Ops:
  0.6 1.7 %pack.1 = f32[1600,128]{1,0:T(8,128)S(1)} custom-call(f32[4,16,2,720]{3,2,1,0:T(2,128)} %bitcast.13, f32[4,16,2,720]{3,2,1,0:T(2,128)} %bitcast.15, s32[4,16,2,720]{3,2,1,0:T(2,128)} %bitcast.16, f32[2,16,2,720]{3,2,1,0:T(2,128)} %refs_3_.1, f32[16]{0:T(128)} %refs_4_.1, f32[16]{0:T(128)} %refs_5_.1), custom_call_target="tpu_custom_call" | custom-call | tf_op jit(solution)/shard_map/pack/pallas_call | solution.py:461
  2.4 28.4 %all_to_all.10 = f32[32,50,1,128]{3,2,1,0:T(1,128)S(1)} all-to-all(f32[32,50,1,128]{3,2,1,0:T(1,128)S(1)} %bitcast.10), channel_id=1, replica_groups=mesh['ens'=2,'space'=4,'tm'=4] {'ens','tm','space'}, dimensions={0} | all-to-all | bytes 1638400 | tf_op jit(solution)/shard_map/all_to_all | solution.py:456
  30.8 2.1 %layer.1 = f32[1472,128]{1,0:T(8,128)S(1)} custom-call(f32[1600,128]{1,0:T(8,128)S(1)} %bitcast.9), custom_call_target="tpu_custom_call" | custom-call | tf_op jit(solution)/shard_map/layer/pallas_call | solution.py:480
  32.9 0.0 copy-start
  32.9 23.1 %all_to_all.11 = f32[32,46,1,128]{3,2,1,0:T(1,128)S(1)} all-to-all(f32[32,46,1,128]{3,2,1,0:T(1,128)S(1)} %bitcast.12), channel_id=1, replica_groups=mesh['ens'=2,'space'=4,'tm'=4] {'ens','tm','space'}, dimensions={0} | all-to-all | bytes 1507328 | tf_op jit(solution)/shard_map/all_to_all | solution.py:456
  56.0 0.0 copy-done
  56.0 1.5 %finish.1 = (f32[4,16,2,720]{3,2,1,0:T(2,128)}, f32[4,16,2,720]{3,2,1,0:T(2,128)}) custom-call(f32[4,16,2,720]{3,2,1,0:T(2,128)S(1)} %bitcast.14, f32[1472,128]{1,0:T(8,128)S(1)} %bitcast.11), custom_call_target="tpu_custom_call" | custom-call | tf_op jit(solution)/shard_map/finish/pallas_call | solution.py:489
Async XLA Ops:
  32.9 23.1 %copy-start = (f32[1,4,16,2,720]{4,3,2,1,0:T(2,128)S(1)}, f32[1,4,16,2,720]{4,3,2,1,0:T(2,128)}, u32[]{:S(2)}) copy-start(f32[1,4,16,2,720]{4,3,2,1,0:T(2,128)} %param.6) | copy-start | bytes 1105924

commit v7 on v6

--- a/solution.py
+++ b/solution.py
@@ -218,6 +218,8 @@
     stay = 1.0 - 4.0 * diffusion
     grad_p = jnp.where(row == ROWS - 2, 0.0, speed)
     grad_m = jnp.where(row == ROWS - 1, 0.0, speed)
+    before_p = jnp.where(row == 0, 0.0, speed)
+    before_m = jnp.where(row == 1, 0.0, speed)
     div_p = jnp.where(row == ROWS - 1, 0.0, speed)
     div_m = jnp.where(row == 0, 0.0, speed)
 
@@ -233,39 +235,63 @@
     narrow = coefficients(east, north)
     wide = coefficients(widened(east, east_extra), widened(north, north_extra))
 
+    here = 2.0 * speed * speed + (div_p * grad_m + div_m * before_p)
+    along, north_of, south_of = speed * speed, div_p * grad_p, div_m * before_m
+
+    def divergence(u, v):
+        return [
+            speed * (a - b) + (div_p * c - div_m * d) for a, b, c, d in zip(u, back(u, 2), v, down(v, 2))
+        ]
+
+    def spread(h):
+        ahead_h, up_h = ahead(h, 2), up(h, 2)
+        change = [
+            (along * (n + m) + (north_of * p + south_of * q)) - here * a
+            for a, n, m, p, q in zip(h, ahead_h, back(h, 2), up_h, down(h, 2))
+        ]
+        return change, ahead_h, up_h
+
+    def gradients(hs, aheads, ups):
+        here_h, ahead_h, up_h = ([sum(x[1:], x[0]) for x in zip(*y)] for y in (hs, aheads, ups))
+        east = [speed * (n - m) for n, m in zip(ahead_h, here_h)]
+        north = [grad_p * n - grad_m * m for n, m in zip(up_h, here_h)]
+        return east, north
+
     def tangent(state, coefs):
         h, u, v, q = state
-        u_back = [a - speed * (n - m) for a, n, m in zip(back(u, 2), h, back(h, 2))]
-        u = [a - speed * (n - m) for a, n, m in zip(u, ahead(h, 2), h)]
-        v = [a - (grad_p * n - grad_m * m) for a, n, m in zip(v, up(h, 2), h)]
-        h = [
-            a - (speed * (p - m) + (div_p * n - div_m * s))
-            for a, p, m, n, s in zip(h, u, u_back, v, down(v, 2))
-        ]
-        q = [
-            stay * a + (em * e + ep * w) + (nm * n + np * s) + couple * p
-            for a, em, e, ep, w, nm, n, np, s, p in zip(
-                q, coefs[0], ahead(q, 1), coefs[1], back(q, 1), coefs[2], up(q, 1), coefs[3], down(q, 1), h
-            )
-        ]
-        return [h, u, v, q]
+        flow = divergence(u, v)
+        passed = []
+        for _ in range(STEPS):
+            change, ahead_h, up_h = spread(h)
+            passed.append((h, ahead_h, up_h))
+            flow = [a - b for a, b in zip(flow, change)]
+            h = [a - b for a, b in zip(h, flow)]
+            q = [
+                stay * a + (em * e + ep * w) + (nm * n + np * s) + couple * p
+                for a, em, e, ep, w, nm, n, np, s, p in zip(
+                    q, coefs[0], ahead(q, 1), coefs[1], back(q, 1), coefs[2], up(q, 1), coefs[3], down(q, 1), h
+                )
+            ]
+        east, north = gradients(*zip(*passed))
+        return [h, [a - b for a, b in zip(u, east)], [a - b for a, b in zip(v, north)], q]
 
     def adjoint(state, coefs):
         h, u, v, q = state
-        h = [a + couple * b for a, b in zip(h, q)]
-        u_back = [a + speed * (n - m) for a, n, m in zip(back(u, 2), h, back(h, 2))]
-        u = [a + speed * (n - m) for a, n, m in zip(u, ahead(h, 2), h)]
-        v = [a + (grad_p * n - grad_m * m) for a, n, m in zip(v, up(h, 2), h)]
-        h = [
-            a + (speed * (p - m) + (div_p * n - div_m * s))
-            for a, p, m, n, s in zip(h, u, u_back, v, down(v, 2))
-        ]
-        e = ahead([a * b for a, b in zip(coefs[1], q)], 1)
-        w = back([a * b for a, b in zip(coefs[0], q)], 1)
-        n = up([a * b for a, b in zip(coefs[3], q)], 1)
-        s = down([a * b for a, b in zip(coefs[2], q)], 1)
-        q = [stay * a + (b + c) + (d + f) for a, b, c, d, f in zip(q, e, w, n, s)]
-        return [h, u, v, q]
+        flow = divergence(u, v)
+        passed = []
+        for _ in range(STEPS):
+            h = [a + couple * b for a, b in zip(h, q)]
+            change, ahead_h, up_h = spread(h)
+            passed.append((h, ahead_h, up_h))
+            flow = [a + b for a, b in zip(flow, change)]
+            h = [a + b for a, b in zip(h, flow)]
+            e = ahead([a * b for a, b in zip(coefs[1], q)], 1)
+            w = back([a * b for a, b in zip(coefs[0], q)], 1)
+            n = up([a * b for a, b in zip(coefs[3], q)], 1)
+            s = down([a * b for a, b in zip(coefs[2], q)], 1)
+            q = [stay * a + (b + c) + (d + f) for a, b, c, d, f in zip(q, e, w, n, s)]
+        east, north = gradients(*zip(*passed))
+        return [h, [a + b for a, b in zip(u, east)], [a + b for a, b in zip(v, north)], q]
 
     def each(fn, *states):
         return [[fn(*vals) for vals in zip(*xs)] for xs in zip(*states)]
@@ -275,9 +301,7 @@
         for t in range(subwins):
             change = p[t]
             if t > 0:
-                moved, coefs = (p[t - 1], narrow) if p_wide is None else (p_wide[t - 1], wide)
-                for _ in range(STEPS):
-                    moved = tangent(moved, coefs)
+                moved = tangent(p[t - 1], narrow) if p_wide is None else tangent(p_wide[t - 1], wide)
                 if p_wide is not None:
                     moved = [narrowed(x) for x in moved]
                 change = each(lambda a, b: a - b, change, moved)
@@ -286,9 +310,7 @@
         for t in range(subwins):
             out = each(lambda w, o, d: w + o * d, weighted[t], observed[t], p[t])
             if t + 1 < subwins:
-                moved = weighted[t + 1]
-                for _ in range(STEPS):
-                    moved = adjoint(moved, narrow)
+                moved = adjoint(weighted[t + 1], narrow)
                 out = each(lambda a, b: a - b, out, moved)
             image.append(out)
         return image

time: 57.6 us -> 57.4 us (level)
  no operation moved by 1% of the time
where the time goes in v7:
time: 57.4 us; the launch traced here: 57.2 us
  blocking collectives  51.5 us (90%)
  Pallas kernels  5.04 us (9%)
  between operations  0.66 us (1%)
    all_to_all x2, blocking collectives, exchange(): lax.all_to_all(x, ('ens', 'tm', 'space'), 0, 0, tiled=True)  51.5 us
    pallas_call x1, Pallas kernels, by_layer(): pl.pallas_call(lambda *refs: layer_kernel(lon, merges, subwins, *refs), o...  1.83 us
    pallas_call x1, Pallas kernels, by_layer(): pl.pallas_call(lambda *refs: pack_kernel(lon, merges, *refs), out_shape=j...  1.72 us
    pallas_call x1, Pallas kernels, by_layer(): pl.pallas_call(lambda *refs: finish_kernel(lon, merges, *refs), out_shape...  1.49 us

profile of v7, /device:TPU:1, one launch (start us, length us, event | category | flops | bytes accessed | tf_op | source)
XLA Modules:
  0.0 57.2 jit_solution(4620397142229467841)
XLA Ops:
  0.6 1.7 %pack.1 = f32[1600,128]{1,0:T(8,128)S(1)} custom-call(f32[4,16,2,720]{3,2,1,0:T(2,128)} %bitcast.13, f32[4,16,2,720]{3,2,1,0:T(2,128)} %bitcast.15, s32[4,16,2,720]{3,2,1,0:T(2,128)} %bitcast.16, f32[2,16,2,720]{3,2,1,0:T(2,128)} %refs_3_.1, f32[16]{0:T(128)} %refs_4_.1, f32[16]{0:T(128)} %refs_5_.1), custom_call_target="tpu_custom_call" | custom-call | tf_op jit(solution)/shard_map/pack/pallas_call | solution.py:483
  2.4 28.4 %all_to_all.10 = f32[32,50,1,128]{3,2,1,0:T(1,128)S(1)} all-to-all(f32[32,50,1,128]{3,2,1,0:T(1,128)S(1)} %bitcast.10), channel_id=1, replica_groups=mesh['ens'=2,'space'=4,'tm'=4] {'ens','tm','space'}, dimensions={0} | all-to-all | bytes 1638400 | tf_op jit(solution)/shard_map/all_to_all | solution.py:478
  30.8 1.8 %layer.1 = f32[1472,128]{1,0:T(8,128)S(1)} custom-call(f32[1600,128]{1,0:T(8,128)S(1)} %bitcast.9), custom_call_target="tpu_custom_call" | custom-call | tf_op jit(solution)/shard_map/layer/pallas_call | solution.py:502
  32.6 0.0 copy-start
  32.6 23.1 %all_to_all.11 = f32[32,46,1,128]{3,2,1,0:T(1,128)S(1)} all-to-all(f32[32,46,1,128]{3,2,1,0:T(1,128)S(1)} %bitcast.12), channel_id=1, replica_groups=mesh['ens'=2,'space'=4,'tm'=4] {'ens','tm','space'}, dimensions={0} | all-to-all | bytes 1507328 | tf_op jit(solution)/shard_map/all_to_all | solution.py:478
  55.7 0.0 copy-done
  55.7 1.5 %finish.1 = (f32[4,16,2,720]{3,2,1,0:T(2,128)}, f32[4,16,2,720]{3,2,1,0:T(2,128)}) custom-call(f32[4,16,2,720]{3,2,1,0:T(2,128)S(1)} %bitcast.14, f32[1472,128]{1,0:T(8,128)S(1)} %bitcast.11), custom_call_target="tpu_custom_call" | custom-call | tf_op jit(solution)/shard_map/finish/pallas_call | solution.py:511
Async XLA Ops:
  32.6 23.1 %copy-start = (f32[1,4,16,2,720]{4,3,2,1,0:T(2,128)S(1)}, f32[1,4,16,2,720]{4,3,2,1,0:T(2,128)}, u32[]{:S(2)}) copy-start(f32[1,4,16,2,720]{4,3,2,1,0:T(2,128)} %param.6) | copy-start | bytes 1105924

commit v8 on v7

--- a/solution.py
+++ b/solution.py
@@ -33,7 +33,7 @@
 
 def pack_kernel(
     lon, merges, b_hbm, e_hbm, o_hbm, w_hbm, speed_hbm, couple_hbm, out_ref,
-    b_ref, e_ref, o_ref, w_ref, speed_ref, couple_ref, stage_ref, sems,
+    b_ref, e_ref, o_ref, w_ref, speed_ref, couple_ref, b_row_ref, s_row_ref, w_row_ref, sems,
 ):
     _, levels, share, _ = b_ref.shape
     full = lon // LANES
@@ -43,9 +43,9 @@
     comp = jnp.where(turn < 2 * TILES, turn // TILES, turn - 2 * TILES)
 
     def in_halves(hbm, ref, first):
-        n = FIELDS // 2
+        n = FIELDS
         return [
-            pltpu.make_async_copy(hbm.at[pl.ds(i * n, n)], ref.at[pl.ds(i * n, n)], sems.at[first + i]) for i in range(2)
+            pltpu.make_async_copy(hbm.at[pl.ds(i * n, n)], ref.at[pl.ds(i * n, n)], sems.at[first + i]) for i in range(1)
         ]
 
     def start(copies):
@@ -66,17 +66,14 @@
     row = lax.broadcasted_iota(jnp.int32, (ROWS, LANES), 0)
     group = ROWS // share
 
-    def raw(copies, ref, first):
-        for f in range(FIELDS):
-            if f % 2 == 0:
-                copies[f // 2].wait()
-            for level in range(levels):
-                for c in range(full + 1):
-                    half, tile = c // TILES, c % TILES
-                    width = LANES if c < full else rest
-                    value = ref[f, level, :, pl.ds(c * LANES, width)].astype(jnp.float32)
-                    start = (half * levels + level) * share * ROWS_IN + first + f * TILES + tile
-                    out_ref[pl.ds(start, share, stride=ROWS_IN), pl.ds(0, width)] = value
+    def stage(copies, ref, row_ref):
+        n = FIELDS // len(copies)
+        for i, copy in enumerate(copies):
+            copy.wait()
+            for f in range(i * n, (i + 1) * n):
+                for level in range(levels):
+                    at = f, pl.ds(level * share, share), pl.ds(0, lon)
+                    row_ref[at] = ref[f, level].astype(jnp.float32)
 
     def place(half, g, k):
         return pl.ds((half * levels + g * group) * share * ROWS_IN + k, ROWS, stride=ROWS_IN), slice(None)
@@ -89,12 +86,12 @@
         extra = [jnp.where(lane < m, y, x) for m, (x, y) in zip(merges, ends)]
         return merged, extra
 
-    def merge(g, k):
-        merged, extra = windows(
-            out_ref[place(0, g, k)], out_ref[place(0, g, k + TILES - 1)], out_ref[place(1, g, k + TILES - 1)]
-        )
+    def put(g, k, row_ref, f):
+        tiles = [row_ref[f, pl.ds(g * ROWS, ROWS), pl.ds(c * LANES, LANES)] for c in range(full + 1)]
+        merged, extra = windows(tiles[0], tiles[2], tiles[5])
         for half in range(2):
-            out_ref[place(half, g, k + TILES - 1)] = merged[half]
+            for c, value in enumerate(tiles[TILES * half : TILES * half + 2] + [merged[half]]):
+                out_ref[place(half, g, k + c)] = value
         return extra
 
     def by_level(ref, g):
@@ -103,24 +100,22 @@
             value = jnp.where(row < i * share, value, ref[g * group + i])
         return value
 
-    raw(copies_b, b_ref, 0)
-    pl.when(member == 0)(lambda: raw(copies_e, e_ref, FIELDS * TILES))
-    pl.when(member != 0)(lambda: raw(copies_o, o_ref, FIELDS * TILES))
+    stage(copies_b, b_ref, b_row_ref)
+    pl.when(member == 0)(lambda: stage(copies_e, e_ref, s_row_ref))
+    pl.when(member != 0)(lambda: stage(copies_o, o_ref, s_row_ref))
     for copy in others:
         copy.wait()
     for level in range(levels):
-        for c in range(full + 1):
-            width = LANES if c < full else rest
-            stage_ref[c, pl.ds(level * share, share), pl.ds(0, width)] = w_ref[level, :, pl.ds(c * LANES, width)]
+        w_row_ref[pl.ds(level * share, share), pl.ds(0, lon)] = w_ref[level]
     for g in range(levels // group):
         mixed = [None, None]
         for f in range(FIELDS):
-            extra = merge(g, f * TILES)
+            extra = put(g, f * TILES, b_row_ref, f)
             for half, m in enumerate(merges):
                 at = WINDS + f * SLOT
                 moved = pltpu.roll(extra[half], (at - (m - REACH)) % LANES, 1)
                 mixed[half] = moved if f == 0 else jnp.where(lane < at, mixed[half], moved)
-        tiles = [stage_ref[c, pl.ds(g * ROWS, ROWS), :] for c in range(full + 1)]
+        tiles = [w_row_ref[pl.ds(g * ROWS, ROWS), pl.ds(c * LANES, LANES)] for c in range(full + 1)]
         merged, extra = windows(tiles[0], tiles[2], tiles[5])
         speed, couple = by_level(speed_ref, g), by_level(couple_ref, g)
         for half, m in enumerate(merges):
@@ -140,7 +135,7 @@
 
     for g in range(levels // group):
         for f in range(FIELDS):
-            merge(g, (FIELDS + f) * TILES)
+            put(g, (FIELDS + f) * TILES, s_row_ref, f)
 
 
 def layer_kernel(lon, merges, subwins, in_ref, out_ref):
@@ -376,7 +371,7 @@
                     put(THIRDS + k, jnp.where(free, jnp.where(row % 2 == 0, rows[0], rows[1]), x[2]))
 
 
-def finish_kernel(lon, merges, b_ref, in_ref, x_hbm, r_hbm, x_ref, r_ref, last_ref, sems):
+def finish_kernel(lon, merges, b_ref, in_ref, x_hbm, r_hbm, x_ref, r_ref, from_x_ref, from_r_ref, sems):
     _, levels, share, _ = b_ref.shape
     full = lon // LANES
     rest = lon - full * LANES
@@ -413,50 +408,43 @@
     alpha_1 = norm_1 / curve
     first = alpha_0 + alpha_1 * (1.0 + beta)
     second = alpha_0 * alpha_1
-    first = jnp.broadcast_to(first[:, at_lane : at_lane + 1], (share, LANES))
-    second = jnp.broadcast_to(second[:, at_lane : at_lane + 1], (share, LANES))
-    lane = lax.broadcasted_iota(jnp.int32, (share, LANES), 1)
-
-    def gather_last():
-        lane_8 = lax.broadcasted_iota(jnp.int32, (ROWS, LANES), 1)
+    first = jnp.broadcast_to(first[:, at_lane : at_lane + 1], (ROWS, LANES))
+    second = jnp.broadcast_to(second[:, at_lane : at_lane + 1], (ROWS, LANES))
+    lane = lax.broadcasted_iota(jnp.int32, (ROWS, LANES), 1)
+
+    def tiles_of(g, k):
+        halves = []
         for half in range(2):
-            for g in range(levels // group):
-                value = None
-                for k in range(5):
-                    start = (half * levels + g * group) * size + THIRDS + k
-                    part = pltpu.roll(in_ref[pl.ds(start, ROWS, stride=ROWS_OUT), :], (k + 1) * FREE % LANES, 1)
-                    begin = (merges[half] - 3 * REACH + (k + 1) * FREE) % LANES
-                    here = jnp.logical_and(lane_8 >= begin, lane_8 < begin + FREE)
-                    value = part if value is None else jnp.where(here, part, value)
-                last_ref[half, pl.ds(g * ROWS, ROWS), :] = value
-
-    def image(level, k):
-        got = []
-        for half in range(2):
-            start = (half * levels + level) * size
-            tiles = [in_ref[pl.ds(start + 2 * k + c, share, stride=ROWS_OUT), :] for c in range(2)]
+            start = (half * levels + g * group) * size
+
+            def rows(j):
+                return in_ref[pl.ds(start + j, ROWS, stride=ROWS_OUT), :]
+
             if k < 2 * FIELDS - 1:
-                tiles.append(in_ref[pl.ds(start + THIRDS + k, share, stride=ROWS_OUT), :])
+                third = rows(THIRDS + k)
             else:
-                tiles.append(last_ref[half, pl.ds(level * share, share), :])
-            got.append(tiles)
-        middle = jnp.where(lane < at_lane, got[0][2], got[1][2])
-        return got[0][:2] + [middle] + got[1]
+                third = None
+                for i in range(5):
+                    part = pltpu.roll(rows(THIRDS + i), (i + 1) * FREE % LANES, 1)
+                    begin = (merges[half] - 3 * REACH + (i + 1) * FREE) % LANES
+                    here = jnp.logical_and(lane >= begin, lane < begin + FREE)
+                    third = part if third is None else jnp.where(here, part, third)
+            halves.append([rows(2 * k), rows(2 * k + 1), third])
+        middle = jnp.where(lane < at_lane, halves[0][2], halves[1][2])
+        return halves[0][:2] + [middle] + halves[1]
 
     copies = []
     for f in range(FIELDS):
-        if f == FIELDS - 1:
-            gather_last()
-        for level in range(levels):
-            b = b_ref[f, level]
-            ones, twos = image(level, f), image(level, FIELDS + f)
-            for c, (one, two) in enumerate(zip(ones, twos)):
-                width = LANES if c < full else rest
-                cols = pl.ds(c * LANES, width)
-                one, two = one[:, :width], two[:, :width]
-                part = b[:, c * LANES : c * LANES + width]
-                x_ref[f, level, :, cols] = first[:, :width] * part - second[:, :width] * one
-                r_ref[f, level, :, cols] = (part - first[:, :width] * one) + second[:, :width] * two
+        for g in range(levels // group):
+            for c, (one, two) in enumerate(zip(tiles_of(g, f), tiles_of(g, FIELDS + f))):
+                at = pl.ds(g * ROWS, ROWS), pl.ds(c * LANES, LANES)
+                from_x_ref[(f, *at)] = second * one
+                from_r_ref[(f, *at)] = second * two - first * one
+            for level in range(g * group, (g + 1) * group):
+                at = pl.ds(level * share, share), pl.ds(0, lon)
+                b = b_ref[f, level]
+                x_ref[f, level] = first[:share, :1] * b - from_x_ref[(f, *at)]
+                r_ref[f, level] = b + from_r_ref[(f, *at)]
         for i, (src, dst) in enumerate(((x_ref, x_hbm), (r_ref, r_hbm))):
             copies.append(pltpu.make_async_copy(src.at[f], dst.at[f], sems.at[i, f]))
             copies[-1].start()
@@ -472,6 +460,7 @@
     hbm = pl.BlockSpec(memory_space=pltpu.HBM)
     params = pltpu.CompilerParams(vmem_limit_bytes=48 * 1024 * 1024)
     state = (fields, levels, share, lon)
+    wide = (lon // LANES + 1) * LANES
 
     def exchange(x):
         x = x.reshape(2 * levels, -1, 1, LANES)
@@ -492,7 +481,9 @@
                 pltpu.VMEM(background_wind.shape[1:], jnp.float32),
                 pltpu.SMEM(wave_speed.shape, jnp.float32),
                 pltpu.SMEM(tracer_coupling.shape, jnp.float32),
-                pltpu.VMEM((lon // LANES + 1, levels * share, LANES), jnp.float32),
+                pltpu.VMEM((fields, levels * share, wide), jnp.float32),
+                pltpu.VMEM((fields, levels * share, wide), jnp.float32),
+                pltpu.VMEM((levels * share, wide), jnp.float32),
                 pltpu.SemaphoreType.DMA((9,)),
             ],
             compiler_params=params,
@@ -516,7 +507,8 @@
             scratch_shapes=[
                 pltpu.VMEM(state, jnp.float32),
                 pltpu.VMEM(state, jnp.float32),
-                pltpu.VMEM((2, levels * share, LANES), jnp.float32),
+                pltpu.VMEM((fields, levels * share, wide), jnp.float32),
+                pltpu.VMEM((fields, levels * share, wide), jnp.float32),
                 pltpu.SemaphoreType.DMA((2, FIELDS)),
             ],
             compiler_params=params,

time: 57.4 us -> 57.1 us (level)
  no operation moved by 1% of the time
where the time goes in v8:
time: 57.1 us; the launch traced here: 56.9 us
  blocking collectives  51.5 us (90%)
  Pallas kernels  4.7 us (8%)
  between operations  0.66 us (1%)
    all_to_all x2, blocking collectives, exchange(): lax.all_to_all(x, ('ens', 'tm', 'space'), 0, 0, tiled=True)  51.5 us
    pallas_call x1, Pallas kernels, by_layer(): pl.pallas_call(lambda *refs: layer_kernel(lon, merges, subwins, *refs), o...  1.83 us
    pallas_call x1, Pallas kernels, by_layer(): pl.pallas_call(lambda *refs: pack_kernel(lon, merges, *refs), out_shape=j...  1.6 us
    pallas_call x1, Pallas kernels, by_layer(): pl.pallas_call(lambda *refs: finish_kernel(lon, merges, *refs), out_shape...  1.26 us

profile of v8, /device:TPU:1, one launch (start us, length us, event | category | flops | bytes accessed | tf_op | source)
XLA Modules:
  0.0 56.9 jit_solution(4807136812749719208)
XLA Ops:
  0.6 1.6 %pack.1 = f32[1600,128]{1,0:T(8,128)S(1)} custom-call(f32[4,16,2,720]{3,2,1,0:T(2,128)} %bitcast.13, f32[4,16,2,720]{3,2,1,0:T(2,128)} %bitcast.15, s32[4,16,2,720]{3,2,1,0:T(2,128)} %bitcast.16, f32[2,16,2,720]{3,2,1,0:T(2,128)} %refs_3_.1, f32[16]{0:T(128)} %refs_4_.1, f32[16]{0:T(128)} %refs_5_.1), custom_call_target="tpu_custom_call" | custom-call | tf_op jit(solution)/shard_map/pack/pallas_call | solution.py:472
  2.2 28.4 %all_to_all.10 = f32[32,50,1,128]{3,2,1,0:T(1,128)S(1)} all-to-all(f32[32,50,1,128]{3,2,1,0:T(1,128)S(1)} %bitcast.10), channel_id=1, replica_groups=mesh['ens'=2,'space'=4,'tm'=4] {'ens','tm','space'}, dimensions={0} | all-to-all | bytes 1638400 | tf_op jit(solution)/shard_map/all_to_all | solution.py:467
  30.7 1.8 %layer.1 = f32[1472,128]{1,0:T(8,128)S(1)} custom-call(f32[1600,128]{1,0:T(8,128)S(1)} %bitcast.9), custom_call_target="tpu_custom_call" | custom-call | tf_op jit(solution)/shard_map/layer/pallas_call | solution.py:493
  32.5 0.0 copy-start
  32.5 23.1 %all_to_all.11 = f32[32,46,1,128]{3,2,1,0:T(1,128)S(1)} all-to-all(f32[32,46,1,128]{3,2,1,0:T(1,128)S(1)} %bitcast.12), channel_id=1, replica_groups=mesh['ens'=2,'space'=4,'tm'=4] {'ens','tm','space'}, dimensions={0} | all-to-all | bytes 1507328 | tf_op jit(solution)/shard_map/all_to_all | solution.py:467
  55.6 0.0 copy-done
  55.6 1.3 %finish.1 = (f32[4,16,2,720]{3,2,1,0:T(2,128)}, f32[4,16,2,720]{3,2,1,0:T(2,128)}) custom-call(f32[4,16,2,720]{3,2,1,0:T(2,128)S(1)} %bitcast.14, f32[1472,128]{1,0:T(8,128)S(1)} %bitcast.11), custom_call_target="tpu_custom_call" | custom-call | tf_op jit(solution)/shard_map/finish/pallas_call | solution.py:502
Async XLA Ops:
  32.5 23.1 %copy-start = (f32[1,4,16,2,720]{4,3,2,1,0:T(2,128)S(1)}, f32[1,4,16,2,720]{4,3,2,1,0:T(2,128)}, u32[]{:S(2)}) copy-start(f32[1,4,16,2,720]{4,3,2,1,0:T(2,128)} %param.6) | copy-start | bytes 1105924

commit v9 on v8

--- a/solution.py
+++ b/solution.py
@@ -42,38 +42,28 @@
     turn = lax.axis_index("tm") * 2 + member
     comp = jnp.where(turn < 2 * TILES, turn // TILES, turn - 2 * TILES)
 
-    def in_halves(hbm, ref, first):
-        n = FIELDS
-        return [
-            pltpu.make_async_copy(hbm.at[pl.ds(i * n, n)], ref.at[pl.ds(i * n, n)], sems.at[first + i]) for i in range(1)
-        ]
-
-    def start(copies):
-        for copy in copies:
-            copy.start()
-
-    copies_b, copies_e, copies_o = in_halves(b_hbm, b_ref, 0), in_halves(e_hbm, e_ref, 2), in_halves(o_hbm, o_ref, 7)
+    copy_b = pltpu.make_async_copy(b_hbm, b_ref, sems.at[0])
+    copy_e = pltpu.make_async_copy(e_hbm, e_ref, sems.at[1])
+    copy_o = pltpu.make_async_copy(o_hbm, o_ref, sems.at[2])
     others = (
-        pltpu.make_async_copy(w_hbm.at[comp], w_ref, sems.at[4]),
-        pltpu.make_async_copy(speed_hbm, speed_ref, sems.at[5]),
-        pltpu.make_async_copy(couple_hbm, couple_ref, sems.at[6]),
+        pltpu.make_async_copy(w_hbm.at[comp], w_ref, sems.at[3]),
+        pltpu.make_async_copy(speed_hbm, speed_ref, sems.at[4]),
+        pltpu.make_async_copy(couple_hbm, couple_ref, sems.at[5]),
     )
-    start(copies_b)
-    pl.when(member == 0)(lambda: start(copies_e))
-    pl.when(member != 0)(lambda: start(copies_o))
-    start(others)
+    copy_b.start()
+    pl.when(member == 0)(copy_e.start)
+    pl.when(member != 0)(copy_o.start)
+    for copy in others:
+        copy.start()
     lane = lax.broadcasted_iota(jnp.int32, (ROWS, LANES), 1)
     row = lax.broadcasted_iota(jnp.int32, (ROWS, LANES), 0)
     group = ROWS // share
 
-    def stage(copies, ref, row_ref):
-        n = FIELDS // len(copies)
-        for i, copy in enumerate(copies):
-            copy.wait()
-            for f in range(i * n, (i + 1) * n):
-                for level in range(levels):
-                    at = f, pl.ds(level * share, share), pl.ds(0, lon)
-                    row_ref[at] = ref[f, level].astype(jnp.float32)
+    def stage(copy, ref, row_ref):
+        copy.wait()
+        for f in range(FIELDS):
+            for level in range(levels):
+                row_ref[f, pl.ds(level * share, share), pl.ds(0, lon)] = ref[f, level].astype(jnp.float32)
 
     def place(half, g, k):
         return pl.ds((half * levels + g * group) * share * ROWS_IN + k, ROWS, stride=ROWS_IN), slice(None)
@@ -100,9 +90,9 @@
             value = jnp.where(row < i * share, value, ref[g * group + i])
         return value
 
-    stage(copies_b, b_ref, b_row_ref)
-    pl.when(member == 0)(lambda: stage(copies_e, e_ref, s_row_ref))
-    pl.when(member != 0)(lambda: stage(copies_o, o_ref, s_row_ref))
+    stage(copy_b, b_ref, b_row_ref)
+    pl.when(member == 0)(lambda: stage(copy_e, e_ref, s_row_ref))
+    pl.when(member != 0)(lambda: stage(copy_o, o_ref, s_row_ref))
     for copy in others:
         copy.wait()
     for level in range(levels):
@@ -378,7 +368,6 @@
     size = share * ROWS_OUT
     apart = merges[0] - merges[1]
     at_lane = merges[0] - 3 * REACH
-
     group = ROWS // share
 
     slots = []
@@ -484,7 +473,7 @@
                 pltpu.VMEM((fields, levels * share, wide), jnp.float32),
                 pltpu.VMEM((fields, levels * share, wide), jnp.float32),
                 pltpu.VMEM((levels * share, wide), jnp.float32),
-                pltpu.SemaphoreType.DMA((9,)),
+                pltpu.SemaphoreType.DMA((len(given),)),
             ],
             compiler_params=params,
         )(*[pltpu.with_memory_space_constraint(x, pltpu.HBM) for x in given])

time: 57.1 us -> 57 us (level)
  no operation moved by 1% of the time
where the time goes in v9:
time: 57 us; the launch traced here: 56.8 us
  blocking collectives  51.5 us (90%)
  Pallas kernels  4.67 us (8%)
  between operations  0.66 us (1%)
    all_to_all x2, blocking collectives, exchange(): lax.all_to_all(x, ('ens', 'tm', 'space'), 0, 0, tiled=True)  51.5 us
    pallas_call x1, Pallas kernels, by_layer(): pl.pallas_call(lambda *refs: layer_kernel(lon, merges, subwins, *refs), o...  1.83 us
    pallas_call x1, Pallas kernels, by_layer(): pl.pallas_call(lambda *refs: pack_kernel(lon, merges, *refs), out_shape=j...  1.58 us
    pallas_call x1, Pallas kernels, by_layer(): pl.pallas_call(lambda *refs: finish_kernel(lon, merges, *refs), out_shape...  1.26 us

profile of v9, /device:TPU:1, one launch (start us, length us, event | category | flops | bytes accessed | tf_op | source)
XLA Modules:
  0.0 56.8 jit_solution(7339244459959379203)
XLA Ops:
  0.6 1.6 %pack.1 = f32[1600,128]{1,0:T(8,128)S(1)} custom-call(f32[4,16,2,720]{3,2,1,0:T(2,128)} %bitcast.13, f32[4,16,2,720]{3,2,1,0:T(2,128)} %bitcast.15, s32[4,16,2,720]{3,2,1,0:T(2,128)} %bitcast.16, f32[2,16,2,720]{3,2,1,0:T(2,128)} %refs_3_.1, f32[16]{0:T(128)} %refs_4_.1, f32[16]{0:T(128)} %refs_5_.1), custom_call_target="tpu_custom_call" | custom-call | tf_op jit(solution)/shard_map/pack/pallas_call | solution.py:461
  2.2 28.4 %all_to_all.10 = f32[32,50,1,128]{3,2,1,0:T(1,128)S(1)} all-to-all(f32[32,50,1,128]{3,2,1,0:T(1,128)S(1)} %bitcast.10), channel_id=1, replica_groups=mesh['ens'=2,'space'=4,'tm'=4] {'ens','tm','space'}, dimensions={0} | all-to-all | bytes 1638400 | tf_op jit(solution)/shard_map/all_to_all | solution.py:456
  30.6 1.8 %layer.1 = f32[1472,128]{1,0:T(8,128)S(1)} custom-call(f32[1600,128]{1,0:T(8,128)S(1)} %bitcast.9), custom_call_target="tpu_custom_call" | custom-call | tf_op jit(solution)/shard_map/layer/pallas_call | solution.py:482
  32.5 0.0 copy-start
  32.5 23.1 %all_to_all.11 = f32[32,46,1,128]{3,2,1,0:T(1,128)S(1)} all-to-all(f32[32,46,1,128]{3,2,1,0:T(1,128)S(1)} %bitcast.12), channel_id=1, replica_groups=mesh['ens'=2,'space'=4,'tm'=4] {'ens','tm','space'}, dimensions={0} | all-to-all | bytes 1507328 | tf_op jit(solution)/shard_map/all_to_all | solution.py:456
  55.6 0.0 copy-done
  55.6 1.3 %finish.1 = (f32[4,16,2,720]{3,2,1,0:T(2,128)}, f32[4,16,2,720]{3,2,1,0:T(2,128)}) custom-call(f32[4,16,2,720]{3,2,1,0:T(2,128)S(1)} %bitcast.14, f32[1472,128]{1,0:T(8,128)S(1)} %bitcast.11), custom_call_target="tpu_custom_call" | custom-call | tf_op jit(solution)/shard_map/finish/pallas_call | solution.py:491
Async XLA Ops:
  32.5 23.1 %copy-start = (f32[1,4,16,2,720]{4,3,2,1,0:T(2,128)S(1)}, f32[1,4,16,2,720]{4,3,2,1,0:T(2,128)}, u32[]{:S(2)}) copy-start(f32[1,4,16,2,720]{4,3,2,1,0:T(2,128)} %param.6) | copy-start | bytes 1105924

commit v10 on v9

--- a/solution.py
+++ b/solution.py
@@ -32,8 +32,8 @@
 
 
 def pack_kernel(
-    lon, merges, b_hbm, e_hbm, o_hbm, w_hbm, speed_hbm, couple_hbm, out_ref,
-    b_ref, e_ref, o_ref, w_ref, speed_ref, couple_ref, b_row_ref, s_row_ref, w_row_ref, sems,
+    lon, merges, b_hbm, e_hbm, o_hbm, w_hbm, speed_hbm, couple_hbm, out_ref, b_row_ref,
+    b_ref, e_ref, o_ref, w_ref, speed_ref, couple_ref, s_row_ref, w_row_ref, sems,
 ):
     _, levels, share, _ = b_ref.shape
     full = lon // LANES
@@ -236,19 +236,18 @@
         ]
         return change, ahead_h, up_h
 
-    def gradients(hs, aheads, ups):
-        here_h, ahead_h, up_h = ([sum(x[1:], x[0]) for x in zip(*y)] for y in (hs, aheads, ups))
-        east = [speed * (n - m) for n, m in zip(ahead_h, here_h)]
-        north = [grad_p * n - grad_m * m for n, m in zip(up_h, here_h)]
+    def gradients(h, ahead_h, up_h):
+        east = [speed * (n - m) for n, m in zip(ahead_h, h)]
+        north = [grad_p * n - grad_m * m for n, m in zip(up_h, h)]
         return east, north
 
     def tangent(state, coefs):
         h, u, v, q = state
         flow = divergence(u, v)
-        passed = []
         for _ in range(STEPS):
             change, ahead_h, up_h = spread(h)
-            passed.append((h, ahead_h, up_h))
+            east, north = gradients(h, ahead_h, up_h)
+            u, v = [a - b for a, b in zip(u, east)], [a - b for a, b in zip(v, north)]
             flow = [a - b for a, b in zip(flow, change)]
             h = [a - b for a, b in zip(h, flow)]
             q = [
@@ -257,17 +256,16 @@
                     q, coefs[0], ahead(q, 1), coefs[1], back(q, 1), coefs[2], up(q, 1), coefs[3], down(q, 1), h
                 )
             ]
-        east, north = gradients(*zip(*passed))
-        return [h, [a - b for a, b in zip(u, east)], [a - b for a, b in zip(v, north)], q]
+        return [h, u, v, q]
 
     def adjoint(state, coefs):
         h, u, v, q = state
         flow = divergence(u, v)
-        passed = []
         for _ in range(STEPS):
             h = [a + couple * b for a, b in zip(h, q)]
             change, ahead_h, up_h = spread(h)
-            passed.append((h, ahead_h, up_h))
+            east, north = gradients(h, ahead_h, up_h)
+            u, v = [a + b for a, b in zip(u, east)], [a + b for a, b in zip(v, north)]
             flow = [a + b for a, b in zip(flow, change)]
             h = [a + b for a, b in zip(h, flow)]
             e = ahead([a * b for a, b in zip(coefs[1], q)], 1)
@@ -275,8 +273,7 @@
             n = up([a * b for a, b in zip(coefs[3], q)], 1)
             s = down([a * b for a, b in zip(coefs[2], q)], 1)
             q = [stay * a + (b + c) + (d + f) for a, b, c, d, f in zip(q, e, w, n, s)]
-        east, north = gradients(*zip(*passed))
-        return [h, [a + b for a, b in zip(u, east)], [a + b for a, b in zip(v, north)], q]
+        return [h, u, v, q]
 
     def each(fn, *states):
         return [[fn(*vals) for vals in zip(*xs)] for xs in zip(*states)]
@@ -361,8 +358,8 @@
                     put(THIRDS + k, jnp.where(free, jnp.where(row % 2 == 0, rows[0], rows[1]), x[2]))
 
 
-def finish_kernel(lon, merges, b_ref, in_ref, x_hbm, r_hbm, x_ref, r_ref, from_x_ref, from_r_ref, sems):
-    _, levels, share, _ = b_ref.shape
+def finish_kernel(lon, merges, b_row_ref, in_ref, x_hbm, r_hbm, x_ref, r_ref, x_row_ref, r_row_ref, sems):
+    _, levels, share, _ = x_ref.shape
     full = lon // LANES
     rest = lon - full * LANES
     size = share * ROWS_OUT
@@ -426,14 +423,14 @@
     for f in range(FIELDS):
         for g in range(levels // group):
             for c, (one, two) in enumerate(zip(tiles_of(g, f), tiles_of(g, FIELDS + f))):
-                at = pl.ds(g * ROWS, ROWS), pl.ds(c * LANES, LANES)
-                from_x_ref[(f, *at)] = second * one
-                from_r_ref[(f, *at)] = second * two - first * one
+                at = f, pl.ds(g * ROWS, ROWS), pl.ds(c * LANES, LANES)
+                b = b_row_ref[at]
+                x_row_ref[at] = first * b - second * one
+                r_row_ref[at] = b + (second * two - first * one)
             for level in range(g * group, (g + 1) * group):
-                at = pl.ds(level * share, share), pl.ds(0, lon)
-                b = b_ref[f, level]
-                x_ref[f, level] = first[:share, :1] * b - from_x_ref[(f, *at)]
-                r_ref[f, level] = b + from_r_ref[(f, *at)]
+                at = f, pl.ds(level * share, share), pl.ds(0, lon)
+                x_ref[f, level] = x_row_ref[at]
+                r_ref[f, level] = r_row_ref[at]
         for i, (src, dst) in enumerate(((x_ref, x_hbm), (r_ref, r_hbm))):
             copies.append(pltpu.make_async_copy(src.at[f], dst.at[f], sems.at[i, f]))
             copies[-1].start()
@@ -458,11 +455,14 @@
     b = right_side.reshape(state)
     given = (b, error_precision.reshape(state), obs_count.reshape(state), background_wind, wave_speed, tracer_coupling)
     with jax.named_scope("pack"):
-        packed = pl.pallas_call(
+        packed, b_rows = pl.pallas_call(
             lambda *refs: pack_kernel(lon, merges, *refs),
-            out_shape=jax.ShapeDtypeStruct((2 * levels * share * ROWS_IN, LANES), jnp.float32),
+            out_shape=[
+                jax.ShapeDtypeStruct((2 * levels * share * ROWS_IN, LANES), jnp.float32),
+                jax.ShapeDtypeStruct((fields, levels * share, wide), jnp.float32),
+            ],
             in_specs=[hbm] * len(given),
-            out_specs=vmem,
+            out_specs=[vmem] * 2,
             scratch_shapes=[
                 pltpu.VMEM(state, jnp.float32),
                 pltpu.VMEM(state, jnp.float32),
@@ -470,7 +470,6 @@
                 pltpu.VMEM(background_wind.shape[1:], jnp.float32),
                 pltpu.SMEM(wave_speed.shape, jnp.float32),
                 pltpu.SMEM(tracer_coupling.shape, jnp.float32),
-                pltpu.VMEM((fields, levels * share, wide), jnp.float32),
                 pltpu.VMEM((fields, levels * share, wide), jnp.float32),
                 pltpu.VMEM((levels * share, wide), jnp.float32),
                 pltpu.SemaphoreType.DMA((len(given),)),
@@ -501,7 +500,7 @@
                 pltpu.SemaphoreType.DMA((2, FIELDS)),
             ],
             compiler_params=params,
-        )(b, images)
+        )(b_rows, images)
     return x.reshape(right_side.shape), r.reshape(right_side.shape)
 
 

time: 57 us -> 57 us (level)
  no operation moved by 1% of the time
where the time goes in v10:
time: 57 us; the launch traced here: 56.8 us
  blocking collectives  51.5 us (90%)
  Pallas kernels  4.67 us (8%)
  between operations  0.65 us (1%)
    all_to_all x2, blocking collectives, exchange(): lax.all_to_all(x, ('ens', 'tm', 'space'), 0, 0, tiled=True)  51.5 us
    pallas_call x1, Pallas kernels, by_layer(): pl.pallas_call(lambda *refs: layer_kernel(lon, merges, subwins, *refs), o...  1.83 us
    pallas_call x1, Pallas kernels, by_layer(): pl.pallas_call(lambda *refs: pack_kernel(lon, merges, *refs), out_shape=[...  1.57 us
    pallas_call x1, Pallas kernels, by_layer(): pl.pallas_call(lambda *refs: finish_kernel(lon, merges, *refs), out_shape...  1.27 us

profile of v10, /device:TPU:1, one launch (start us, length us, event | category | flops | bytes accessed | tf_op | source)
XLA Modules:
  0.0 56.8 jit_solution(6321066925606944151)
XLA Ops:
  0.6 1.6 %pack.1 = (f32[1600,128]{1,0:T(8,128)S(1)}, f32[4,32,768]{2,1,0:T(8,128)S(1)}) custom-call(f32[4,16,2,720]{3,2,1,0:T(2,128)} %bitcast.13, f32[4,16,2,720]{3,2,1,0:T(2,128)} %bitcast.14, s32[4,16,2,720]{3,2,1,0:T(2,128)} %bitcast.15, f32[2,16,2,720]{3,2,1,0:T(2,128)} %refs_3_.1, f32[16]{0:T(128)} %refs_4_.1, f32[16]{0:T(128)} %refs_5_.1), custom_call_target="tpu_custom_call" | custom-call | tf_op jit(solution)/shard_map/pack/pallas_call | solution.py:458
  2.2 28.4 %all_to_all.10 = f32[32,50,1,128]{3,2,1,0:T(1,128)S(1)} all-to-all(f32[32,50,1,128]{3,2,1,0:T(1,128)S(1)} %bitcast.12), channel_id=1, replica_groups=mesh['ens'=2,'space'=4,'tm'=4] {'ens','tm','space'}, dimensions={0} | all-to-all | bytes 1638400 | tf_op jit(solution)/shard_map/all_to_all | solution.py:453
  30.6 1.8 %layer.1 = f32[1472,128]{1,0:T(8,128)S(1)} custom-call(f32[1600,128]{1,0:T(8,128)S(1)} %bitcast.9), custom_call_target="tpu_custom_call" | custom-call | tf_op jit(solution)/shard_map/layer/pallas_call | solution.py:481
  32.5 23.1 %all_to_all.11 = f32[32,46,1,128]{3,2,1,0:T(1,128)S(1)} all-to-all(f32[32,46,1,128]{3,2,1,0:T(1,128)S(1)} %bitcast.11), channel_id=1, replica_groups=mesh['ens'=2,'space'=4,'tm'=4] {'ens','tm','space'}, dimensions={0} | all-to-all | bytes 1507328 | tf_op jit(solution)/shard_map/all_to_all | solution.py:453
  55.6 1.3 %finish.1 = (f32[4,16,2,720]{3,2,1,0:T(2,128)}, f32[4,16,2,720]{3,2,1,0:T(2,128)}) custom-call(f32[4,32,768]{2,1,0:T(8,128)S(1)} %get-tuple-element.6.refs_0_, f32[1472,128]{1,0:T(8,128)S(1)} %bitcast.10), custom_call_target="tpu_custom_call" | custom-call | tf_op jit(solution)/shard_map/finish/pallas_call | solution.py:490

commit v11 on v10

--- a/solution.py
+++ b/solution.py
@@ -420,20 +420,22 @@
         return halves[0][:2] + [middle] + halves[1]
 
     copies = []
-    for f in range(FIELDS):
+
+    def send(i, f, row_ref, ref, hbm):
+        for level in range(levels):
+            ref[f, level] = row_ref[f, pl.ds(level * share, share), pl.ds(0, lon)]
+        copies.append(pltpu.make_async_copy(ref.at[f], hbm.at[f], sems.at[i, f]))
+        copies[-1].start()
+
+    for f in reversed(range(FIELDS)):
         for g in range(levels // group):
             for c, (one, two) in enumerate(zip(tiles_of(g, f), tiles_of(g, FIELDS + f))):
                 at = f, pl.ds(g * ROWS, ROWS), pl.ds(c * LANES, LANES)
                 b = b_row_ref[at]
                 x_row_ref[at] = first * b - second * one
                 r_row_ref[at] = b + (second * two - first * one)
-            for level in range(g * group, (g + 1) * group):
-                at = f, pl.ds(level * share, share), pl.ds(0, lon)
-                x_ref[f, level] = x_row_ref[at]
-                r_ref[f, level] = r_row_ref[at]
-        for i, (src, dst) in enumerate(((x_ref, x_hbm), (r_ref, r_hbm))):
-            copies.append(pltpu.make_async_copy(src.at[f], dst.at[f], sems.at[i, f]))
-            copies[-1].start()
+        send(0, f, x_row_ref, x_ref, x_hbm)
+        send(1, f, r_row_ref, r_ref, r_hbm)
     for copy in copies:
         copy.wait()
 

time: 57 us -> 57 us (level)
  no operation moved by 1% of the time
where the time goes in v11:
time: 57 us; the launch traced here: 56.8 us
  blocking collectives  51.5 us (90%)
  Pallas kernels  4.65 us (8%)
  between operations  0.65 us (1%)
    all_to_all x2, blocking collectives, exchange(): lax.all_to_all(x, ('ens', 'tm', 'space'), 0, 0, tiled=True)  51.5 us
    pallas_call x1, Pallas kernels, by_layer(): pl.pallas_call(lambda *refs: layer_kernel(lon, merges, subwins, *refs), o...  1.83 us
    pallas_call x1, Pallas kernels, by_layer(): pl.pallas_call(lambda *refs: pack_kernel(lon, merges, *refs), out_shape=[...  1.57 us
    pallas_call x1, Pallas kernels, by_layer(): pl.pallas_call(lambda *refs: finish_kernel(lon, merges, *refs), out_shape...  1.25 us

profile of v11, /device:TPU:1, one launch (start us, length us, event | category | flops | bytes accessed | tf_op | source)
XLA Modules:
  0.0 56.8 jit_solution(2494002389285150245)
XLA Ops:
  0.6 1.6 %pack.1 = (f32[1600,128]{1,0:T(8,128)S(1)}, f32[4,32,768]{2,1,0:T(8,128)S(1)}) custom-call(f32[4,16,2,720]{3,2,1,0:T(2,128)} %bitcast.13, f32[4,16,2,720]{3,2,1,0:T(2,128)} %bitcast.14, s32[4,16,2,720]{3,2,1,0:T(2,128)} %bitcast.15, f32[2,16,2,720]{3,2,1,0:T(2,128)} %refs_3_.1, f32[16]{0:T(128)} %refs_4_.1, f32[16]{0:T(128)} %refs_5_.1), custom_call_target="tpu_custom_call" | custom-call | tf_op jit(solution)/shard_map/pack/pallas_call | solution.py:460
  2.2 28.4 %all_to_all.10 = f32[32,50,1,128]{3,2,1,0:T(1,128)S(1)} all-to-all(f32[32,50,1,128]{3,2,1,0:T(1,128)S(1)} %bitcast.12), channel_id=1, replica_groups=mesh['ens'=2,'space'=4,'tm'=4] {'ens','tm','space'}, dimensions={0} | all-to-all | bytes 1638400 | tf_op jit(solution)/shard_map/all_to_all | solution.py:455
  30.6 1.8 %layer.1 = f32[1472,128]{1,0:T(8,128)S(1)} custom-call(f32[1600,128]{1,0:T(8,128)S(1)} %bitcast.9), custom_call_target="tpu_custom_call" | custom-call | tf_op jit(solution)/shard_map/layer/pallas_call | solution.py:483
  32.5 23.1 %all_to_all.11 = f32[32,46,1,128]{3,2,1,0:T(1,128)S(1)} all-to-all(f32[32,46,1,128]{3,2,1,0:T(1,128)S(1)} %bitcast.11), channel_id=1, replica_groups=mesh['ens'=2,'space'=4,'tm'=4] {'ens','tm','space'}, dimensions={0} | all-to-all | bytes 1507328 | tf_op jit(solution)/shard_map/all_to_all | solution.py:455
  55.6 1.2 %finish.1 = (f32[4,16,2,720]{3,2,1,0:T(2,128)}, f32[4,16,2,720]{3,2,1,0:T(2,128)}) custom-call(f32[4,32,768]{2,1,0:T(8,128)S(1)} %get-tuple-element.6.refs_0_, f32[1472,128]{1,0:T(8,128)S(1)} %bitcast.10), custom_call_target="tpu_custom_call" | custom-call | tf_op jit(solution)/shard_map/finish/pallas_call | solution.py:492

commit v12 on v10

--- a/solution.py
+++ b/solution.py
@@ -279,7 +279,7 @@
         return [[fn(*vals) for vals in zip(*xs)] for xs in zip(*states)]
 
     def operate(p, p_wide, precision, observed):
-        weighted = []
+        image = []
         for t in range(subwins):
             change = p[t]
             if t > 0:
@@ -287,15 +287,11 @@
                 if p_wide is not None:
                     moved = [narrowed(x) for x in moved]
                 change = each(lambda a, b: a - b, change, moved)
-            weighted.append(each(lambda a, b: a * b, precision[t], change))
-        image = []
-        for t in range(subwins):
-            out = each(lambda w, o, d: w + o * d, weighted[t], observed[t], p[t])
-            if t + 1 < subwins:
-                moved = adjoint(weighted[t + 1], narrow)
-                out = each(lambda a, b: a - b, out, moved)
-            image.append(out)
-        return image
+            weighted = each(lambda a, b: a * b, precision[t], change)
+            if t > 0:
+                image[-1] = each(lambda a, b: a - b, image[-1], adjoint(weighted, narrow))
+            image.append(weighted)
+        return [each(lambda w, o, d: w + o * d, *x) for x in zip(image, observed, p)]
 
     def flat(x):
         return [(c, v) for state in x for field in state for c, v in enumerate(field)]

time: 57 us -> 57 us (level)
  no operation moved by 1% of the time
where the time goes in v12:
time: 57 us; the launch traced here: 56.8 us
  blocking collectives  51.5 us (90%)
  Pallas kernels  4.67 us (8%)
  between operations  0.65 us (1%)
    all_to_all x2, blocking collectives, exchange(): lax.all_to_all(x, ('ens', 'tm', 'space'), 0, 0, tiled=True)  51.5 us
    pallas_call x1, Pallas kernels, by_layer(): pl.pallas_call(lambda *refs: layer_kernel(lon, merges, subwins, *refs), o...  1.82 us
    pallas_call x1, Pallas kernels, by_layer(): pl.pallas_call(lambda *refs: pack_kernel(lon, merges, *refs), out_shape=[...  1.57 us
    pallas_call x1, Pallas kernels, by_layer(): pl.pallas_call(lambda *refs: finish_kernel(lon, merges, *refs), out_shape...  1.27 us

profile of v12, /device:TPU:1, one launch (start us, length us, event | category | flops | bytes accessed | tf_op | source)
XLA Modules:
  0.0 56.8 jit_solution(4446932600536805488)
XLA Ops:
  0.6 1.6 %pack.1 = (f32[1600,128]{1,0:T(8,128)S(1)}, f32[4,32,768]{2,1,0:T(8,128)S(1)}) custom-call(f32[4,16,2,720]{3,2,1,0:T(2,128)} %bitcast.13, f32[4,16,2,720]{3,2,1,0:T(2,128)} %bitcast.14, s32[4,16,2,720]{3,2,1,0:T(2,128)} %bitcast.15, f32[2,16,2,720]{3,2,1,0:T(2,128)} %refs_3_.1, f32[16]{0:T(128)} %refs_4_.1, f32[16]{0:T(128)} %refs_5_.1), custom_call_target="tpu_custom_call" | custom-call | tf_op jit(solution)/shard_map/pack/pallas_call | solution.py:454
  2.2 28.4 %all_to_all.10 = f32[32,50,1,128]{3,2,1,0:T(1,128)S(1)} all-to-all(f32[32,50,1,128]{3,2,1,0:T(1,128)S(1)} %bitcast.12), channel_id=1, replica_groups=mesh['ens'=2,'space'=4,'tm'=4] {'ens','tm','space'}, dimensions={0} | all-to-all | bytes 1638400 | tf_op jit(solution)/shard_map/all_to_all | solution.py:449
  30.6 1.8 %layer.1 = f32[1472,128]{1,0:T(8,128)S(1)} custom-call(f32[1600,128]{1,0:T(8,128)S(1)} %bitcast.9), custom_call_target="tpu_custom_call" | custom-call | tf_op jit(solution)/shard_map/layer/pallas_call | solution.py:477
  32.5 23.1 %all_to_all.11 = f32[32,46,1,128]{3,2,1,0:T(1,128)S(1)} all-to-all(f32[32,46,1,128]{3,2,1,0:T(1,128)S(1)} %bitcast.11), channel_id=1, replica_groups=mesh['ens'=2,'space'=4,'tm'=4] {'ens','tm','space'}, dimensions={0} | all-to-all | bytes 1507328 | tf_op jit(solution)/shard_map/all_to_all | solution.py:449
  55.6 1.3 %finish.1 = (f32[4,16,2,720]{3,2,1,0:T(2,128)}, f32[4,16,2,720]{3,2,1,0:T(2,128)}) custom-call(f32[4,32,768]{2,1,0:T(8,128)S(1)} %get-tuple-element.6.refs_0_, f32[1472,128]{1,0:T(8,128)S(1)} %bitcast.10), custom_call_target="tpu_custom_call" | custom-call | tf_op jit(solution)/shard_map/finish/pallas_call | solution.py:486
